TPU v7x, 256 devices: a whole 4x4x8 slice. The times are simulated.
256 devices in a mesh: src: 64 (over z, y_lo, x), rcv: 4 (over y_hi, core).
Axes of the slice: x: 4, y: 4 (y_hi: 2, y_lo: 2; y = y_hi * 2 + y_lo), z: 8, core: 2. Of those that a mesh axis runs over, the one named last changes fastest.
Arguments:
- probes: bfloat16 [256, 1024, 256], P('rcv', 'src'), may hold values from -6 to 6
- kappa: float32 [1024, 256], P('src'), may hold values from 0.02 to 0.24
- footprint: bfloat16 [64, 4, 192, 128, 128], P('src', 'rcv'), may hold values from -0.0390625 to 0.0390625
- block_source: int32 [64, 4, 192], P('src', 'rcv'), may hold values from 0 to 31
- block_receptor: int32 [64, 4, 192], P('src', 'rcv'), may hold values from 0 to 15
- block_count: int32 [64, 4], P('src', 'rcv'), may hold values from 1 to 192, as said below
- obs_weight: float32 [8192], P('rcv'), may hold values from 1 to 8
Outputs:
- hessian_probe: float32 [256, 1024, 256], P('rcv', 'src')
Inputs may be any that keep to these rules, and one draw needn't show every extreme that they name: Slots 0 to block_count - 1 of a tile and group hold its footprint blocks, later slots are unused; some tile and group uses all 192 slots.
All inputs are finite; a program needn't handle non-finite values.
Results may differ from a plain program's by a relative error of at most 0.006.
Values may be sent and summed in bfloat16 or wider, within the bound.
A program may use at most 64 MiB of HBM per device.

v0:
```python
import jax
import jax.numpy as jnp
from jax import lax
from jax.sharding import PartitionSpec as P

BLK = 128
RB_LOC = 16
GROUP = 32
SMOOTH = 4


def extended(shard, sides, width):
    for axis, dim in sides:
        size, length = (lax.axis_size(axis), shard.shape[dim])
        up = [(i, (i + 1) % size) for i in range(size - 1)]
        down = [(j, i) for i, j in up]
        last = lax.slice_in_dim(shard, length - width, length, axis=dim)
        leading = lax.slice_in_dim(shard, 0, width, axis=dim)
        before = lax.ppermute(last, axis, up)
        after = lax.ppermute(leading, axis, down)
        shard = jnp.concatenate([before, shard, after], axis=dim)
    return shard


def laplacian_operator(emission_source_field):
    padded = extended(emission_source_field.astype(jnp.bfloat16), (("src", 1),), 1).astype(
        emission_source_field.dtype
    )
    padded = jnp.pad(padded, ((0, 0), (0, 0), (1, 1)))
    return (
        padded[:, 2:, 1:-1]
        + padded[:, :-2, 1:-1]
        + padded[:, 1:-1, 2:]
        + padded[:, 1:-1, :-2]
        - 4.0 * emission_source_field
    )


def run_groups(step_group, initial, slot_total):
    rounds = slot_total // GROUP
    return lax.fori_loop(
        0, rounds, lambda group_index, running: step_group(group_index * GROUP, running), initial
    )


def per_device(probes, kappa, footprint, block_source, block_receptor, block_count, obs_weight):
    probe_local, lat_rows, lon_cells = probes.shape
    smoothed = probes.astype(jnp.float32)
    for repeat in range(SMOOTH):
        smoothed = smoothed + kappa * laplacian_operator(smoothed)
    local_field = smoothed.astype(jnp.bfloat16)
    gathered = lax.all_gather(local_field, "rcv", axis=0, tiled=True)
    probe_total = gathered.shape[0]
    tile_field = gathered.reshape(probe_total, -1, BLK).transpose(1, 2, 0)
    source_blocks = tile_field.shape[0]
    blocks = footprint.reshape(footprint.shape[2:])
    sources = block_source.reshape(-1)
    receptors = block_receptor.reshape(-1)
    used_slots = block_count.reshape(())
    slot_total = blocks.shape[0]

    def slot_contents(offset):
        block_portion = lax.dynamic_slice_in_dim(blocks, offset, GROUP, 0)
        source_ids = lax.dynamic_slice_in_dim(sources, offset, GROUP, 0)
        receptor_ids = lax.dynamic_slice_in_dim(receptors, offset, GROUP, 0)
        in_use = (offset + jnp.arange(GROUP, dtype=jnp.int32) < used_slots).astype(jnp.float32)
        return (block_portion, source_ids, receptor_ids, in_use)

    def forward_group(offset, running):
        block_portion, source_ids, receptor_ids, in_use = slot_contents(offset)
        selected_entries = jnp.take(tile_field, source_ids, axis=0)
        hessian_result = jnp.einsum(
            "wlq,wqd->wld", block_portion, selected_entries, preferred_element_type=jnp.float32
        )
        return running.at[receptor_ids].add(hessian_result * in_use[:, None, None])

    evolved = run_groups(
        forward_group, jnp.zeros((RB_LOC, BLK, probe_total), jnp.float32), slot_total
    )
    sim_rows = evolved.reshape(-1, probe_total)
    receptor_all = lax.psum(sim_rows, "src")
    weighted = (obs_weight[:, None] * receptor_all).astype(jnp.bfloat16)
    weighted = weighted.reshape(RB_LOC, BLK, probe_total)

    def adjoint_group(offset, running):
        block_portion, source_ids, receptor_ids, in_use = slot_contents(offset)
        selected_entries = jnp.take(weighted, receptor_ids, axis=0)
        hessian_result = jnp.einsum(
            "grc,grp->pgc", block_portion, selected_entries, preferred_element_type=jnp.float32
        )
        return running.at[:, source_ids].add(hessian_result * in_use[None, :, None])

    adjoint_terms = run_groups(
        adjoint_group, jnp.zeros((probe_total, source_blocks, BLK), jnp.float32), slot_total
    )
    adjoint_rows = adjoint_terms.reshape(probe_total, lat_rows, lon_cells).astype(jnp.bfloat16)
    back = lax.psum_scatter(adjoint_rows, "rcv", scatter_dimension=0, tiled=True).astype(
        jnp.float32
    )
    for repeat in range(SMOOTH):
        back = back + laplacian_operator(kappa * back)
    return probes.astype(jnp.float32) + back


def solution(mesh):
    placed = (
        P("rcv", "src", None),
        P("src", None),
        P("src", "rcv", None, None, None),
        P("src", "rcv", None),
        P("src", "rcv", None),
        P("src", "rcv"),
        P("rcv"),
    )
    return jax.shard_map(
        per_device, mesh=mesh, in_specs=placed, out_specs=P("rcv", "src", None), check_vma=False
    )
```

profile of v0, /device:TPU:1, one launch (start us, length us, event | category | flops | bytes accessed | tf_op | source)
XLA Modules:
  0.0 1003.0 jit_solution(7618383937822140229)
XLA Ops:
  7.7 3.9 collective-permute-start
  13.0 3.7 collective-permute-done.1
  23.5 3.7 collective-permute-done.3
  28.4 4.7 collective-permute-start.4
  34.4 3.7 collective-permute-done.5
  39.3 4.0 collective-permute-start.6
  44.7 4.0 collective-permute-done.7
  50.6 46.8 %all-gather.2.cloned.1.call-done = bf16[256,16,256]{2,1,0:T(8,128)(2,1)} async-done(((bf16[64,16,256]{2,1,0:T(8,128)(2,1)}), bf16[256,16,256]{2,1,0:T(8,128)(2,1)}) %all-gather.2.cloned.1.call-update) | async-done | bytes 2097168 | tf_op jit(solution)/shard_map/all_gather | solution.py:52
  97.5 4.3 copy.15
  102.5 94.1 %while.26 = (s32[]{:T(128)}, f32[16,128,256]{2,1,0:T(8,128)S(1)}, s32[192]{0:T(256)S(1)}, bf16[192,128,128]{2,1,0:T(8,128)(2,1)}, s32[192]{0:T(256)S(1)}, /*inde...) while((s32[]{:T(128)}, f32[16,128,256]{2,1,0:T(8,128)S(1)}, ...), condition=%wide.region_2.3_spmd, body=%wide.region_0.2_spmd.sunk | while | flops 271582592 | bytes 24122736 | solution.py:41
  103.3 3.7 gather_fusion
  107.0 4.7 convolution_multiply_fusion.4
  111.7 6.5 scatter_fusion
  119.0 3.7 gather_fusion
  122.6 4.7 convolution_multiply_fusion.4
  127.3 6.5 scatter_fusion
  134.7 3.7 gather_fusion
  138.3 4.7 convolution_multiply_fusion.4
  143.0 6.5 scatter_fusion
  150.3 3.7 gather_fusion
  154.0 4.7 convolution_multiply_fusion.4
  158.7 6.5 scatter_fusion
  169.7 4.7 convolution_multiply_fusion.4
  174.4 6.5 scatter_fusion
  181.7 3.7 gather_fusion
  185.4 4.7 convolution_multiply_fusion.4
  190.1 6.5 scatter_fusion
  198.2 565.5 %all-reduce.10.cloned.1.call-done = f32[2048,256]{1,0:T(8,128)} async-done(((f32[2048,256]{1,0:T(8,128)}), f32[2048,256]{1,0:T(8,128)}) %all-reduce.10.cloned.1.call-update) | async-done | bytes 2097168 | tf_op jit(solution)/shard_map/psum | solution.py:81
  768.1 94.0 %while.27 = (s32[]{:T(128)}, f32[256,32,128]{2,0,1:T(8,128)}, s32[192]{0:T(256)S(1)}, s32[192]{0:T(256)S(1)}, bf16[16,128,256]{2,1,0:T(8,128)(2,1)S(1)}, /*index...) while((s32[]{:T(128)}, f32[256,32,128]{2,0,1:T(8,128)}, ...), condition=%wide.region_6.7_spmd, body=%wide.region_4.6_spmd.sunk | while | flops 271582592 | bytes 24122736 | solution.py:41
  769.6 4.2 convolution_multiply_fusion.5
  773.8 10.0 scatter_fusion.1
  785.3 4.2 convolution_multiply_fusion.5
  789.5 9.8 scatter_fusion.1
  800.8 4.2 convolution_multiply_fusion.5
  805.1 10.0 scatter_fusion.1
  816.6 4.2 convolution_multiply_fusion.5
  820.8 9.9 scatter_fusion.1
  832.2 4.2 convolution_multiply_fusion.5
  836.4 10.0 scatter_fusion.1
  847.9 4.2 convolution_multiply_fusion.5
  852.1 9.9 scatter_fusion.1
  868.2 86.7 %reduce-scatter.2.cloned.1.call-done = bf16[64,16,256]{2,1,0:T(8,128)(2,1)} async-done(((bf16[256,16,256]{2,1,0:T(8,128)(2,1)}), bf16[64,16,256]{2,1,0:T(8,128)(2,1)}) %reduce-scatter.2.cloned.1.call-update) | async-done | bytes 524304 | tf_op jit(solution)/shard_map/reduce_scatter | solution.py:97
  960.6 3.7 collective-permute-done.9
  970.0 3.7 collective-permute-done.11
  974.9 3.8 collective-permute-start.12
  980.0 3.7 collective-permute-done.13
  984.9 4.2 collective-permute-start.14
  990.4 4.0 collective-permute-done.15
  (115 shorter events, 64.8 us)
Async XLA Ops:
  6.5 11.6 %copy-start.1 = (bf16[64,16,256]{2,1,0:T(8,128)(2,1)S(1)}, bf16[64,16,256]{2,1,0:T(8,128)(2,1)}, u32[]{:S(2)}) copy-start(bf16[64,16,256]{2,1,0:T(8,128)(2,1)} %param.11) | copy-start | bytes 1572868
  6.5 11.6 %copy-start.4 = (f32[16,256]{1,0:T(8,128)S(1)}, f32[16,256]{1,0:T(8,128)}, u32[]{:S(2)}) copy-start(f32[16,256]{1,0:T(8,128)} %param.12) | copy-start | bytes 49156
  6.5 90.9 %all-gather.2.cloned.1.call-start = ((), (), s32[]{:S(2)}) async-start(), calls=%async_computation.1 | async-start | bytes 2621440 | tf_op jit(solution)/shard_map/all_gather | solution.py:52
  7.7 5.3 collective-permute-start
  11.7 5.0 collective-permute-start.1
  19.0 4.4 collective-permute-start.2
  22.2 5.0 collective-permute-start.3
  28.4 6.0 collective-permute-start.4
  33.1 5.0 collective-permute-start.5
  39.3 5.3 collective-permute-start.6
  43.4 5.3 collective-permute-start.7
  50.6 713.0 %all-reduce.10.cloned.1.call-start = ((), (), s32[]{:S(2)}) async-start(), calls=%async_computation.2 | async-start | bytes 4194304 | tf_op jit(solution)/shard_map/psum | solution.py:81
  101.8 0.7 copy-start.6
  101.8 0.7 copy-start.7
  196.6 1.3 copy-start
  196.6 567.0 %copy-start.5 = (f32[2048]{0:T(1024)S(1)}, f32[2048]{0:T(1024)}, u32[]{:S(2)}) copy-start(f32[2048]{0:T(1024)} %param.17) | copy-start | bytes 24580
  197.9 757.0 %reduce-scatter.2.cloned.1.call-start = ((), (), s32[]{:S(2)}) async-start(), calls=%async_computation.3 | async-start | bytes 2621440 | tf_op jit(solution)/shard_map/reduce_scatter | solution.py:97
  954.9 9.8 copy-start.3
  956.2 4.4 collective-permute-start.8
  959.3 5.0 collective-permute-start.9
  965.6 4.4 collective-permute-start.10
  968.6 5.0 collective-permute-start.11
  974.9 5.1 collective-permute-start.12
  978.7 5.0 collective-permute-start.13
  984.8 10.0 copy-start.2
  984.9 5.5 collective-permute-start.14
  989.1 5.3 collective-permute-start.15
Sparse Core Ops, SparseCore 0:
  50.7 46.7 all-gather.1
  198.0 565.5 all-reduce.9
  868.3 86.5 reduce-scatter.1
where the time goes:
time: 1020 us; the launch traced here: 1000 us
  waiting for transfers between devices  729 us (71%)
  other arithmetic  126 us (12%)
  matrix products  53.5 us (5%)
  local copies, waits for them, and re-layouts  40.5 us (4%)
  starting transfers between devices  40.5 us (4%)
  between operations  13.5 us (1%)
    psum x1, waiting for transfers between devices, per_device(): receptor_all = lax.psum(sim_rows, 'src')  565 us
    reduce_scatter x1, waiting for transfers between devices, per_device(): lax.psum_scatter(adjoint_rows, 'rcv', scatter_dimension=0, tiled=True)  86.7 us
    scatter-add x6, other arithmetic, adjoint_group(): return running.at[:, source_ids].add(hessian_result * in_use[None, :, None])  59.6 us
    all_gather x1, waiting for transfers between devices, per_device(): gathered = lax.all_gather(local_field, 'rcv', axis=0, tiled=True)  46.8 us
    scatter-add x6, other arithmetic, forward_group(): return running.at[receptor_ids].add(hessian_result * in_use[:, None, None])  38.9 us
    ppermute x8, waiting for transfers between devices, extended(): after = lax.ppermute(leading, axis, down)  30.1 us
    ppermute x8, starting transfers between devices, extended(): before = lax.ppermute(last, axis, up)  29.9 us
    dot_general x6, matrix products, forward_group(): jnp.einsum('wlq,wqd->wld', block_portion, selected_entries, preferred_ele...  28.1 us
  transfers between devices with their start and end apart: 19, of which 11 were waited for; matrix products, arithmetic and copies ran while one was open for 0% of the time, Pallas kernels for 0%

commit v1 on v0

v1 whole, which is shorter than its diff:
```python
import functools

import jax
import jax.numpy as jnp
from jax import lax
from jax.experimental import pallas as pl
from jax.experimental.pallas import tpu as pltpu
from jax.sharding import PartitionSpec as P

BLK = 128
RB_LOC = 16
SMOOTH = 4
PLANE = 8
SLAB = 16
FETCH = 16
MESH = pl.DeviceIdType.MESH
VMEM = pltpu.VMEM
F32 = jnp.float32
BF16 = jnp.bfloat16
VMEM_LIMIT = 56 * 1024 * 1024


def barrier_with(devices):
    barrier = pltpu.get_barrier_semaphore()
    for device in devices:
        pl.semaphore_signal(barrier, inc=1, device_id=device, device_id_type=MESH)
    pl.semaphore_wait(barrier, len(devices))


def remote(src, dst, send_sem, recv_sem, device):
    return pltpu.make_async_remote_copy(
        src_ref=src,
        dst_ref=dst,
        send_sem=send_sem,
        recv_sem=recv_sem,
        device_id=device,
        device_id_type=MESH,
    )


def neighbours(n_src):
    me = lax.axis_index("src")
    group = lax.axis_index("rcv")
    high, core = group // 2, group % 2
    before = (lax.rem(me + n_src - 1, n_src), group)
    after = (lax.rem(me + 1, n_src), group)
    twin = high * 2 + (1 - core)
    opposite = (1 - high) * 2 + core
    return me, group, before, after, twin, opposite


def beside(centre):
    lanes = centre.shape[-1]
    lane = lax.broadcasted_iota(jnp.int32, centre.shape, centre.ndim - 1)
    west = jnp.where(lane == 0, 0.0, pltpu.roll(centre, 1, centre.ndim - 1))
    east = jnp.where(lane == lanes - 1, 0.0, pltpu.roll(centre, lanes - 1, centre.ndim - 1))
    return west + east


def spread_kappa(n_src, me, kext_ref, kwide):
    rows = kwide.shape[0]
    for row in range(rows):
        value = kext_ref[8 - SMOOTH + row : 8 - SMOOTH + row + 1, :]
        if row < SMOOTH:
            value = jnp.where(me == 0, 0.0, value)
        if row >= rows - SMOOTH:
            value = jnp.where(me == n_src - 1, 0.0, value)
        kwide[row] = jnp.broadcast_to(value, kwide.shape[1:])


def smooth_kernel(
    n_src, probes_ref, kappa_ref, field_ref, kext_ref, halo, wide, kwide, edge_send, edge_recv, send, recv
):
    me, group, before, after, twin, opposite = neighbours(n_src)
    lat, loc, lon = probes_ref.shape
    slabs = loc // SLAB
    src = me
    barrier_with([before, after, (src, twin), (src, opposite)])

    edges = [
        remote(probes_ref.at[pl.ds(lat - SMOOTH, SMOOTH)], halo.at[0], edge_send.at[0], edge_recv.at[0], after),
        remote(probes_ref.at[pl.ds(0, SMOOTH)], halo.at[1], edge_send.at[1], edge_recv.at[1], before),
        remote(kappa_ref.at[pl.ds(lat - 8, 8)], kext_ref.at[pl.ds(0, 8)], edge_send.at[2], edge_recv.at[2], after),
        remote(kappa_ref.at[pl.ds(0, 8)], kext_ref.at[pl.ds(lat + 8, 8)], edge_send.at[3], edge_recv.at[3], before),
    ]
    for copy in edges:
        copy.start()
    kext_ref[8 : lat + 8, :] = kappa_ref[...]
    wide[SMOOTH : lat + SMOOTH] = probes_ref[...].astype(F32)
    for copy in edges:
        copy.wait()
    wide[0:SMOOTH] = jnp.where(me == 0, 0.0, halo[0].astype(F32))
    wide[lat + SMOOTH :] = jnp.where(me == n_src - 1, 0.0, halo[1].astype(F32))
    spread_kappa(n_src, me, kext_ref, kwide)

    def place(owner, slab):
        return field_ref.at[:, pl.ds(pl.multiple_of(owner * loc + slab * SLAB, SLAB), SLAB), :]

    def to_twin(slab):
        return remote(place(group, slab), place(group, slab), send.at[0, slab], recv.at[0, slab], (src, twin))

    def to_opposite(slab):
        return remote(place(group, slab), place(group, slab), send.at[1, slab], recv.at[1, slab], (src, opposite))

    def relay(slab):
        return remote(place(opposite, slab), place(opposite, slab), send.at[2, slab], recv.at[2, slab], (src, twin))

    def one_slab(slab, carry):
        for half in range(SLAB // 8):
            some = pl.ds(pl.multiple_of(slab * SLAB + half * 8, 8), 8)
            value = wide[:, some, :]
            for step in range(SMOOTH):
                centre = value[1:-1]
                lap = value[:-2] + value[2:] + beside(centre) - 4.0 * centre
                value = centre + kwide[step + 1 : lat + 2 * SMOOTH - 1 - step] * lap
            wide[SMOOTH : lat + SMOOTH, some, :] = value
        some = pl.ds(pl.multiple_of(slab * SLAB, SLAB), SLAB)
        mine = pl.ds(pl.multiple_of(group * loc + slab * SLAB, SLAB), SLAB)
        field_ref[:, mine, :] = wide[SMOOTH : lat + SMOOTH, some, :].astype(BF16)
        to_opposite(slab).start()
        to_twin(slab).start()
        return carry

    lax.fori_loop(0, slabs, one_slab, 0)

    def pass_on(slab, carry):
        to_opposite(slab).wait_recv()
        relay(slab).start()
        return carry

    lax.fori_loop(0, slabs, pass_on, 0)

    def finish(slab, carry):
        to_opposite(slab).wait_send()
        to_twin(slab).wait()
        relay(slab).wait()
        return carry

    lax.fori_loop(0, slabs, finish, 0)


def smooth_and_gather(n_src, n_rcv, probes, kappa):
    lat, loc, lon = probes.shape
    slabs = loc // SLAB
    return pl.pallas_call(
        functools.partial(smooth_kernel, n_src),
        out_shape=(
            jax.ShapeDtypeStruct((lat, loc * n_rcv, lon), BF16),
            jax.ShapeDtypeStruct((lat + 16, lon), F32),
        ),
        in_specs=[pl.BlockSpec(memory_space=VMEM)] * 2,
        out_specs=(pl.BlockSpec(memory_space=VMEM),) * 2,
        scratch_shapes=[
            VMEM((2, SMOOTH, loc, lon), BF16),
            VMEM((lat + 2 * SMOOTH, loc, lon), F32),
            VMEM((lat + 2 * SMOOTH, 8, lon), F32),
            pltpu.SemaphoreType.DMA((4,)),
            pltpu.SemaphoreType.DMA((4,)),
            pltpu.SemaphoreType.DMA((3, slabs)),
            pltpu.SemaphoreType.DMA((3, slabs)),
        ],
        compiler_params=pltpu.CompilerParams(
            collective_id=0, has_side_effects=True, vmem_limit_bytes=VMEM_LIMIT
        ),
        name="smooth_and_gather",
    )(probes, kappa)


def each_used_block(count, blocks_ref, held, sems, work):
    fetches = (count + FETCH - 1) // FETCH

    def fetch(index):
        part = pl.ds(pl.multiple_of(index * FETCH, FETCH), FETCH)
        return pltpu.make_async_copy(blocks_ref.at[part], held.at[part], sems.at[index])

    def begin(index, carry):
        fetch(index).start()
        return carry

    def consume(index, carry):
        fetch(index).wait()
        first = index * FETCH
        here = jnp.minimum(count - first, FETCH)

        def several(turn, inner):
            work([first + turn * 4 + step for step in range(4)])
            return inner

        def single(turn, inner):
            work([first + turn])
            return inner

        lax.fori_loop(0, here // 4, several, 0)
        lax.fori_loop(here // 4 * 4, here, single, 0)
        return carry

    return (
        lambda: lax.fori_loop(0, fetches, begin, 0),
        lambda: lax.fori_loop(0, fetches, consume, 0),
    )


def forward_kernel(source_ref, receptor_ref, count_ref, field_ref, blocks_ref, out_ref, total, held, sems):
    def work(slots):
        products = []
        for slot in slots:
            source = source_ref[slot]
            half = pl.ds(pl.multiple_of(source % 2 * BLK, BLK), BLK)
            products.append(
                lax.dot_general(
                    field_ref[source // 2, :, half],
                    held[slot],
                    (((1,), (1,)), ((), ())),
                    preferred_element_type=F32,
                )
            )
        for slot, product in zip(slots, products):
            total[receptor_ref[slot]] += product

    begin, consume = each_used_block(count_ref[0], blocks_ref, held, sems, work)
    begin()
    total[...] = jnp.zeros_like(total)
    consume()
    out_ref[...] = total[...].astype(BF16)


def adjoint_kernel(source_ref, receptor_ref, count_ref, weighted_ref, blocks_ref, out_ref, total, held, sems):
    def work(slots):
        products = [
            jnp.dot(weighted_ref[receptor_ref[slot]], held[slot], preferred_element_type=F32) for slot in slots
        ]
        for slot, product in zip(slots, products):
            total[source_ref[slot]] += product

    begin, consume = each_used_block(count_ref[0], blocks_ref, held, sems, work)
    begin()
    total[...] = jnp.zeros_like(total)
    consume()
    for row in range(out_ref.shape[0]):
        for half in range(2):
            out_ref[row, :, half * BLK : (half + 1) * BLK] = total[2 * row + half].astype(BF16)


def block_products(kernel, name, out_shape, total_shape, sources, receptors, count, dense, blocks):
    slots = blocks.shape[0]
    fetches = (slots + FETCH - 1) // FETCH
    smem = pl.BlockSpec(memory_space=pltpu.SMEM)
    return pl.pallas_call(
        kernel,
        out_shape=jax.ShapeDtypeStruct(out_shape, BF16),
        in_specs=[smem, smem, smem, pl.BlockSpec(memory_space=VMEM), pl.BlockSpec(memory_space=pl.ANY)],
        out_specs=pl.BlockSpec(memory_space=VMEM),
        scratch_shapes=[
            VMEM(total_shape, F32),
            VMEM(blocks.shape, BF16),
            pltpu.SemaphoreType.DMA((fetches,)),
        ],
        compiler_params=pltpu.CompilerParams(vmem_limit_bytes=VMEM_LIMIT),
        name=name,
    )(sources, receptors, count, dense, blocks)


def reduce_kernel(planes, probes, weight_ref, mine_ref, out_ref, first, part, second, *sems):
    me = lax.axis_index("src")
    group = lax.axis_index("rcv")
    plane, spot = me // PLANE, me % PLANE
    send1, recv1, send2, recv2, send3, recv3, send4, recv4 = sems
    rows = mine_ref.shape[2]

    def spot_of(distance):
        return lax.rem(spot + distance, PLANE)

    def plane_of(distance):
        return lax.rem(plane + distance, planes)

    def in_plane(distance):
        return (plane * PLANE + spot_of(distance), group)

    def in_line(distance):
        return (plane_of(distance) * PLANE + spot, group)

    def scatter_plane(d):
        return remote(mine_ref.at[spot_of(d)], first.at[d - 1], send1.at[d - 1], recv1.at[d - 1], in_plane(d))

    def scatter_line(d):
        return remote(part.at[plane_of(d)], second.at[d - 1], send2.at[d - 1], recv2.at[d - 1], in_line(d))

    def gather_line(d):
        return remote(out_ref.at[spot, plane], out_ref.at[spot, plane], send3.at[d - 1], recv3.at[d - 1], in_line(d))

    def gather_plane(d):
        return remote(out_ref.at[spot], out_ref.at[spot], send4.at[d - 1], recv4.at[d - 1], in_plane(d))

    barrier_with(
        [in_plane(d) for d in range(1, PLANE)] + [in_line(d) for d in range(1, planes)]
    )
    for d in range(1, PLANE):
        scatter_plane(d).start()
    for d in range(1, PLANE):
        scatter_plane(d).wait_recv()
    for d in list(range(1, planes)) + [0]:
        piece = plane_of(d)
        total = mine_ref[spot, piece].astype(F32)
        for other in range(PLANE - 1):
            total = total + first[other, piece].astype(F32)
        part[piece] = total.astype(BF16)
        if d:
            scatter_line(d).start()
    for d in range(1, planes):
        scatter_line(d).wait_recv()
    total = part[plane].astype(F32)
    for other in range(planes - 1):
        total = total + second[other].astype(F32)
    block = spot * (RB_LOC // PLANE) + plane * rows // probes
    out_ref[spot, plane] = (total * weight_ref[pl.ds(block, 1), :]).astype(BF16)
    for d in range(1, planes):
        gather_line(d).start()
    for d in range(1, planes):
        gather_line(d).wait_recv()
    for d in range(1, PLANE):
        gather_plane(d).start()
    for d in range(1, PLANE):
        scatter_plane(d).wait_send()
        gather_plane(d).wait()
    for d in range(1, planes):
        scatter_line(d).wait_send()
        gather_line(d).wait_send()


def reduce_and_weigh(n_src, evolved, weight):
    blocks, probes, receptors = evolved.shape
    planes = n_src // PLANE
    rows = blocks * probes // (PLANE * planes)
    dma = pltpu.SemaphoreType.DMA
    out = pl.pallas_call(
        functools.partial(reduce_kernel, planes, probes),
        out_shape=jax.ShapeDtypeStruct((PLANE, planes, rows, receptors), BF16),
        in_specs=[pl.BlockSpec(memory_space=VMEM)] * 2,
        out_specs=pl.BlockSpec(memory_space=VMEM),
        scratch_shapes=[
            VMEM((PLANE - 1, planes, rows, receptors), BF16),
            VMEM((planes, rows, receptors), BF16),
            VMEM((planes - 1, rows, receptors), BF16),
            dma((PLANE - 1,)),
            dma((PLANE - 1,)),
            dma((planes - 1,)),
            dma((planes - 1,)),
            dma((planes - 1,)),
            dma((planes - 1,)),
            dma((PLANE - 1,)),
            dma((PLANE - 1,)),
        ],
        compiler_params=pltpu.CompilerParams(
            collective_id=1, has_side_effects=True, vmem_limit_bytes=VMEM_LIMIT
        ),
        name="reduce_and_weigh",
    )(weight, evolved.reshape(PLANE, planes, rows, receptors))
    return out.reshape(blocks, probes, receptors)


def back_kernel(
    n_src, terms_ref, probes_ref, kext_ref, out_ref, pair, relayed, joined, far, edge, halo, wide, kwide,
    edge_send, edge_recv, send, recv,
):
    me, group, before, after, twin, opposite = neighbours(n_src)
    lat, loc, lon = probes_ref.shape
    diagonal = 3 - group
    order = (0, lat // SMOOTH - 1) + tuple(range(1, lat // SMOOTH - 1))
    barrier_with([before, after, (me, twin), (me, opposite)])

    def term(owner, piece):
        return terms_ref.at[
            pl.ds(piece * SMOOTH, SMOOTH), pl.ds(pl.multiple_of(owner * loc, loc), loc), :
        ]

    def for_relay(k):
        return remote(term(diagonal, k), relayed.at[k], send.at[0, k], recv.at[0, k], (me, twin))

    def for_twin(k):
        return remote(term(twin, k), pair.at[k], send.at[1, k], recv.at[1, k], (me, twin))

    def across(k):
        return remote(joined.at[k], far.at[k], send.at[2, k], recv.at[2, k], (me, opposite))

    edges = [
        remote(edge.at[0], halo.at[1], edge_send.at[0], edge_recv.at[0], before),
        remote(edge.at[1], halo.at[0], edge_send.at[1], edge_recv.at[1], after),
    ]
    for k in order:
        for_relay(k).start()
    for k in order:
        for_twin(k).start()
    for k in order:
        for_relay(k).wait_recv()
        joined[k] = (term(opposite, k)[...].astype(F32) + relayed[k].astype(F32)).astype(BF16)
        across(k).start()
    spread_kappa(n_src, me, kext_ref, kwide)
    for k in order:
        for_twin(k).wait_recv()
        across(k).wait_recv()
        total = term(group, k)[...].astype(F32) + pair[k].astype(F32) + far[k].astype(F32)
        wide[SMOOTH + k * SMOOTH : 2 * SMOOTH + k * SMOOTH] = total
        if k == 0:
            edge[0] = total.astype(BF16)
            edges[0].start()
        if k == lat // SMOOTH - 1:
            edge[1] = total.astype(BF16)
            edges[1].start()
    for copy in edges:
        copy.wait()
    wide[0:SMOOTH] = halo[0].astype(F32)
    wide[lat + SMOOTH :] = halo[1].astype(F32)

    def one_slab(slab, carry):
        for half in range(SLAB // 8):
            some = pl.ds(pl.multiple_of(slab * SLAB + half * 8, 8), 8)
            value = wide[:, some, :]
            for step in range(SMOOTH):
                scaled = kwide[step : lat + 2 * SMOOTH - step] * value
                centre = scaled[1:-1]
                lap = scaled[:-2] + scaled[2:] + beside(centre) - 4.0 * centre
                value = value[1:-1] + lap
            out_ref[:, some, :] = value
        some = pl.ds(pl.multiple_of(slab * SLAB, SLAB), SLAB)
        out_ref[:, some, :] += probes_ref[:, some, :].astype(F32)
        return carry

    lax.fori_loop(0, loc // SLAB, one_slab, 0)
    for k in order:
        for_relay(k).wait_send()
        for_twin(k).wait_send()
        across(k).wait_send()


def scatter_and_smooth(n_src, terms, probes, kext):
    lat, loc, lon = probes.shape
    pieces = lat // SMOOTH
    landing = VMEM((pieces, SMOOTH, loc, lon), BF16)
    dma = pltpu.SemaphoreType.DMA
    return pl.pallas_call(
        functools.partial(back_kernel, n_src),
        out_shape=jax.ShapeDtypeStruct((lat, loc, lon), F32),
        in_specs=[pl.BlockSpec(memory_space=VMEM)] * 3,
        out_specs=pl.BlockSpec(memory_space=VMEM),
        scratch_shapes=[
            landing,
            landing,
            landing,
            landing,
            VMEM((2, SMOOTH, loc, lon), BF16),
            VMEM((2, SMOOTH, loc, lon), BF16),
            VMEM((lat + 2 * SMOOTH, loc, lon), F32),
            VMEM((lat + 2 * SMOOTH, 8, lon), F32),
            dma((2,)),
            dma((2,)),
            dma((3, pieces)),
            dma((3, pieces)),
        ],
        compiler_params=pltpu.CompilerParams(
            collective_id=2, has_side_effects=True, vmem_limit_bytes=VMEM_LIMIT
        ),
        name="scatter_and_smooth",
    )(terms, probes, kext)


def per_device(probes, kappa, footprint, block_source, block_receptor, block_count, obs_weight):
    n_src, n_rcv = lax.axis_size("src"), lax.axis_size("rcv")
    rows_first = probes.transpose(1, 0, 2)
    lat, loc, lon = rows_first.shape
    total = loc * n_rcv
    blocks = footprint.reshape(footprint.shape[2:])
    sources = block_source.reshape(-1)
    receptors = block_receptor.reshape(-1)
    count = block_count.reshape(1)
    field, kext = smooth_and_gather(n_src, n_rcv, rows_first, kappa)
    evolved = block_products(
        forward_kernel, "forward", (RB_LOC, total, BLK), (RB_LOC, total, BLK),
        sources, receptors, count, field, blocks,
    )
    weighted = reduce_and_weigh(n_src, evolved, obs_weight.reshape(RB_LOC, BLK))
    terms = block_products(
        adjoint_kernel, "adjoint", (lat, total, lon), (lat * lon // BLK, total, BLK),
        sources, receptors, count, weighted, blocks,
    )
    out = scatter_and_smooth(n_src, terms, rows_first, kext)
    return out.transpose(1, 0, 2)


def solution(mesh):
    placed = (
        P("rcv", "src", None),
        P("src", None),
        P("src", "rcv", None, None, None),
        P("src", "rcv", None),
        P("src", "rcv", None),
        P("src", "rcv"),
        P("rcv"),
    )
    return jax.shard_map(
        per_device, mesh=mesh, in_specs=placed, out_specs=P("rcv", "src", None), check_vma=False
    )
```

time: 1020 us -> 136 us (0.13); the launches traced: 1000 us -> 136 us
  waiting for transfers between devices: 729 us -> 0 us
  Pallas kernels: 0 us -> 130 us
  other arithmetic: 126 us -> 0 us
  matrix products: 53.5 us -> 0 us
  starting transfers between devices: 40.5 us -> 0 us
  local copies, waits for them, and re-layouts: 40.5 us -> 4.8 us
  between operations: 13.5 us -> 0.69 us
    psum x1 -> x0, waiting for transfers between devices: 565 us -> none  [per_device(): receptor_all = lax.psum(sim_rows, 'src')]
    pallas_call x0 -> x5, Pallas kernels: none -> 130 us  [the longest x1 42.3 us: reduce_and_weigh(): pl.pallas_call(functools.partial(reduce_kernel, planes, probes), out_shap...]
    scatter-add x12 -> x0, other arithmetic: 98.5 us -> none  [the longest x6 59.6 us: adjoint_group(): return running.at[:, source_ids].add(hessian_result * in_use[None, :, None])]
    reduce_scatter x1 -> x0, waiting for transfers between devices: 86.7 us -> none  [per_device(): lax.psum_scatter(adjoint_rows, 'rcv', scatter_dimension=0, tiled=True)]
    dot_general x12 -> x0, matrix products: 53.5 us -> none  [the longest x6 28.1 us: forward_group(): jnp.einsum('wlq,wqd->wld', block_portion, selected_entries, preferred_ele...]
    all_gather x1 -> x0, waiting for transfers between devices: 46.8 us -> none  [per_device(): gathered = lax.all_gather(local_field, 'rcv', axis=0, tiled=True)]
    ppermute x16 -> x0, starting transfers between devices: 40.2 us -> none  [the longest x8 29.9 us: extended(): before = lax.ppermute(last, axis, up)]
    ppermute x16 -> x0, waiting for transfers between devices: 30.2 us -> none  [the longest x8 30.1 us: extended(): after = lax.ppermute(leading, axis, down)]
  transfers between devices with their start and end apart: 19 -> 0, of which waited for: 11 -> 0; matrix products, arithmetic and copies ran while one was open for 0% -> 0% of each run, Pallas kernels for 0% -> 0%
where the time goes in v1:
time: 136 us
  Pallas kernels  130 us (96%)
  local copies, waits for them, and re-layouts  4.8 us (4%)
    pallas_call x1, Pallas kernels, reduce_and_weigh(): pl.pallas_call(functools.partial(reduce_kernel, planes, probes), out_shap...  42.3 us
    pallas_call x1, Pallas kernels, scatter_and_smooth(): pl.pallas_call(functools.partial(back_kernel, n_src), out_shape=jax.Shape...  42.1 us
    pallas_call x1, Pallas kernels, smooth_and_gather(): pl.pallas_call(functools.partial(smooth_kernel, n_src), out_shape=(jax.Sh...  33.9 us
    pallas_call x2, Pallas kernels, block_products(): pl.pallas_call(kernel, out_shape=jax.ShapeDtypeStruct(out_shape, BF16), i...  11.8 us
    transpose x1, local copies, waits for them, and re-layouts, per_device(): return out.transpose(1, 0, 2)  2.81 us

profile of v1, /device:TPU:1, one launch (start us, length us, event | category | flops | bytes accessed | tf_op | source)
XLA Modules:
  0.0 135.6 jit_solution(10992593605513044419)
XLA Ops:
  0.7 2.0 %copy.11 = bf16[64,16,256]{2,0,1:T(8,128)(2,1)} copy(bf16[64,16,256]{2,1,0:T(8,128)(2,1)} %param.7) | data formatting | bytes 1048576 | tf_op args[0]
  2.6 33.9 %smooth_and_gather.1 = (bf16[16,256,256]{2,1,0:T(8,128)(2,1)}, f32[32,256]{1,0:T(8,128)}) custom-call(bf16[16,64,256]{2,1,0:T(8,128)(2,1)} %bitcast.15, f32[16,256]{1,0:T(8,128)} %kappa_ref.1), custom_call_target="tpu_custom_call" | custom-call | tf_op jit(solution)/shard_map/smooth_and_gather/pallas_call | solution.py:145
  36.6 5.9 %forward.1 = bf16[16,256,128]{2,1,0:T(8,128)(2,1)} custom-call(s32[192]{0:T(256)} %bitcast.21, s32[192]{0:T(256)} %bitcast.23, s32[1]{0:T(128)} %bitcast.11.count_ref, bf16[16,256,256]{2,1,0:T(8,128)(2,1)} %get-tuple-element.7.field_ref, bf16[192,128,128]{2,1,0:T(8,128)(2,1)} %bitcast.13), custom_call_target="tpu_custom_call" | custom-call | tf_op jit(solution)/shard_map/forward/pallas_call | solution.py:248
  42.5 42.3 %reduce_and_weigh.1 = bf16[8,8,64,128]{3,2,1,0:T(8,128)(2,1)} custom-call(f32[16,128]{1,0:T(8,128)} %bitcast.20, bf16[8,8,64,128]{3,2,1,0:T(8,128)(2,1)} %bitcast.19), custom_call_target="tpu_custom_call" | custom-call | tf_op jit(solution)/shard_map/reduce_and_weigh/pallas_call | solution.py:335
  84.8 5.9 %adjoint.1.terms_ref = bf16[16,256,256]{2,1,0:T(8,128)(2,1)} custom-call(s32[192]{0:T(256)} %bitcast.22, s32[192]{0:T(256)} %bitcast.24, s32[1]{0:T(128)} %bitcast.12.count_ref, bf16[16,256,128]{2,1,0:T(8,128)(2,1)} %bitcast.18, bf16[192,128,128]{2,1,0:T(8,128)(2,1)} %bitcast.14), custom_call_target="tpu_custom_call" | custom-call | tf_op jit(solution)/shard_map/adjoint/pallas_call | solution.py:248
  90.7 42.1 %scatter_and_smooth.1 = f32[16,64,256]{2,1,0:T(8,128)} custom-call(bf16[16,256,256]{2,1,0:T(8,128)(2,1)} %adjoint.1.terms_ref, bf16[16,64,256]{2,1,0:T(8,128)(2,1)} %bitcast.16, f32[32,256]{1,0:T(8,128)} %get-tuple-element.8.kext_ref), custom_call_target="tpu_custom_call" | custom-call | tf_op jit(solution)/shard_map/scatter_and_smooth/pallas_call | solution.py:440
  132.8 2.8 %copy.9 = f32[64,16,256]{2,1,0:T(8,128)} copy(f32[64,16,256]{2,0,1:T(8,128)} %bitcast.17) | data formatting | bytes 2097152 | tf_op jit(solution)/shard_map/transpose | solution.py:486

commit v2 on v1

v2 whole, which is shorter than its diff:
```python
import functools

import jax
import jax.numpy as jnp
from jax import lax
from jax.experimental import pallas as pl
from jax.experimental.pallas import tpu as pltpu
from jax.sharding import PartitionSpec as P

BLK = 128
RB_LOC = 16
SMOOTH = 4
PLANE = 8
SLAB = 16
TOGETHER = 16
MESH = pl.DeviceIdType.MESH
VMEM = pltpu.VMEM
F32 = jnp.float32
BF16 = jnp.bfloat16
VMEM_LIMIT = 24 * 1024 * 1024


def announce(devices):
    barrier = pltpu.get_barrier_semaphore()
    for device in devices:
        pl.semaphore_signal(barrier, inc=1, device_id=device, device_id_type=MESH)


def await_all(devices):
    pl.semaphore_wait(pltpu.get_barrier_semaphore(), len(devices))


def remote(src, dst, send_sem, recv_sem, device):
    return pltpu.make_async_remote_copy(
        src_ref=src,
        dst_ref=dst,
        send_sem=send_sem,
        recv_sem=recv_sem,
        device_id=device,
        device_id_type=MESH,
    )


def neighbours(n_src):
    me = lax.axis_index("src")
    group = lax.axis_index("rcv")
    high, core = group // 2, group % 2
    before = (lax.rem(me + n_src - 1, n_src), group)
    after = (lax.rem(me + 1, n_src), group)
    twin = high * 2 + (1 - core)
    opposite = (1 - high) * 2 + core
    return me, group, before, after, twin, opposite


def beside(centre):
    lanes = centre.shape[-1]
    lane = lax.broadcasted_iota(jnp.int32, centre.shape, centre.ndim - 1)
    west = jnp.where(lane == 0, 0.0, pltpu.roll(centre, 1, centre.ndim - 1))
    east = jnp.where(lane == lanes - 1, 0.0, pltpu.roll(centre, lanes - 1, centre.ndim - 1))
    return west + east


def spread_kappa(n_src, me, kext_ref, kwide, rows):
    for row in rows:
        value = kext_ref[8 - SMOOTH + row : 8 - SMOOTH + row + 1, :]
        if row < SMOOTH:
            value = jnp.where(me == 0, 0.0, value)
        if row >= kwide.shape[0] - SMOOTH:
            value = jnp.where(me == n_src - 1, 0.0, value)
        kwide[row] = jnp.broadcast_to(value, kwide.shape[1:])


def smooth_kernel(
    n_src, probes_ref, kappa_ref, field_ref, kext_ref, flat, halo, edge, wide, kwide, edge_send, edge_recv, send, recv
):
    me, group, before, after, twin, opposite = neighbours(n_src)
    lat, lon = kappa_ref.shape
    loc = probes_ref.shape[0] // lat
    slabs = loc // SLAB
    partners = [before, after, (me, twin), (me, opposite)]
    announce(partners)

    top, bottom = range(SMOOTH), range(lat - SMOOTH, lat)
    for side in range(lon // BLK):
        flat[side] = probes_ref[:, side * BLK : (side + 1) * BLK].astype(F32)

    def of_row(row):
        return jnp.concatenate([flat[side, pl.ds(row, loc, stride=lat), :] for side in range(lon // BLK)], axis=1)

    for side, rows in enumerate((top, bottom)):
        for place, row in enumerate(rows):
            value = of_row(row)
            wide[SMOOTH + row] = value
            edge[side, place] = value.astype(BF16)
    await_all(partners)
    edges = [
        remote(edge.at[1], halo.at[0], edge_send.at[0], edge_recv.at[0], after),
        remote(edge.at[0], halo.at[1], edge_send.at[1], edge_recv.at[1], before),
        remote(kappa_ref.at[pl.ds(lat - 8, 8)], kext_ref.at[pl.ds(0, 8)], edge_send.at[2], edge_recv.at[2], after),
        remote(kappa_ref.at[pl.ds(0, 8)], kext_ref.at[pl.ds(lat + 8, 8)], edge_send.at[3], edge_recv.at[3], before),
    ]
    for copy in edges:
        copy.start()
    for row in range(SMOOTH, lat - SMOOTH):
        wide[SMOOTH + row] = of_row(row)
    kext_ref[8 : lat + 8, :] = kappa_ref[...]
    spread_kappa(n_src, me, kext_ref, kwide, range(SMOOTH, lat + SMOOTH))

    parts = ((SMOOTH, lat - SMOOTH), (0, SMOOTH), (lat - SMOOTH, lat))

    def place(owner, part, slab):
        first, last = parts[part]
        return field_ref.at[
            pl.ds(first, last - first), pl.ds(pl.multiple_of(owner * loc + slab * SLAB, SLAB), SLAB), :
        ]

    def to_twin(part, slab):
        where = place(group, part, slab)
        return remote(where, where, send.at[0, part, slab], recv.at[0, part, slab], (me, twin))

    def to_opposite(part, slab):
        where = place(group, part, slab)
        return remote(where, where, send.at[1, part, slab], recv.at[1, part, slab], (me, opposite))

    def relay(part, slab):
        where = place(opposite, part, slab)
        return remote(where, where, send.at[2, part, slab], recv.at[2, part, slab], (me, twin))

    def smooth_part(part, slab):
        first, last = parts[part]
        halves = []
        for half in range(SLAB // 8):
            some = pl.ds(pl.multiple_of(slab * SLAB + half * 8, 8), 8)
            value = wide[first : last + 2 * SMOOTH, some, :]
            for step in range(SMOOTH):
                centre = value[1:-1]
                lap = value[:-2] + value[2:] + beside(centre) - 4.0 * centre
                value = centre + kwide[first + step + 1 : last + 2 * SMOOTH - 1 - step] * lap
            halves.append(value)
        mine = pl.ds(pl.multiple_of(group * loc + slab * SLAB, SLAB), SLAB)
        field_ref[first:last, mine, :] = jnp.concatenate(halves, axis=1).astype(BF16)
        to_opposite(part, slab).start()
        to_twin(part, slab).start()

    def inner(slab, carry):
        smooth_part(0, slab)
        return carry

    def outer(slab, carry):
        smooth_part(1, slab)
        smooth_part(2, slab)
        return carry

    lax.fori_loop(0, slabs, inner, 0)
    for copy in edges:
        copy.wait()
    wide[0:SMOOTH] = jnp.where(me == 0, 0.0, halo[0].astype(F32))
    wide[lat + SMOOTH :] = jnp.where(me == n_src - 1, 0.0, halo[1].astype(F32))
    spread_kappa(n_src, me, kext_ref, kwide, [*range(SMOOTH), *range(lat + SMOOTH, lat + 2 * SMOOTH)])
    lax.fori_loop(0, slabs, outer, 0)

    def pass_on(parts_here):
        def one(slab, carry):
            for part in parts_here:
                to_opposite(part, slab).wait_recv()
                relay(part, slab).start()
            return carry

        lax.fori_loop(0, slabs, one, 0)

    pass_on((0,))
    pass_on((1, 2))

    def finish(slab, carry):
        for part in range(3):
            to_opposite(part, slab).wait_send()
            to_twin(part, slab).wait()
            relay(part, slab).wait()
        return carry

    lax.fori_loop(0, slabs, finish, 0)


def smooth_and_gather(n_src, n_rcv, probes, kappa):
    lat, lon = kappa.shape
    loc = probes.shape[0] // lat
    slabs = loc // SLAB
    dma = pltpu.SemaphoreType.DMA
    return pl.pallas_call(
        functools.partial(smooth_kernel, n_src),
        out_shape=(
            jax.ShapeDtypeStruct((lat, loc * n_rcv, lon), BF16),
            jax.ShapeDtypeStruct((lat + 16, lon), F32),
        ),
        in_specs=[pl.BlockSpec(memory_space=VMEM)] * 2,
        out_specs=(pl.BlockSpec(memory_space=VMEM),) * 2,
        scratch_shapes=[
            VMEM((lon // BLK, loc * lat, BLK), F32),
            VMEM((2, SMOOTH, loc, lon), BF16),
            VMEM((2, SMOOTH, loc, lon), BF16),
            VMEM((lat + 2 * SMOOTH, loc, lon), F32),
            VMEM((lat + 2 * SMOOTH, 8, lon), F32),
            dma((4,)),
            dma((4,)),
            dma((3, 3, slabs)),
            dma((3, 3, slabs)),
        ],
        compiler_params=pltpu.CompilerParams(
            collective_id=0, has_side_effects=True, vmem_limit_bytes=VMEM_LIMIT
        ),
        cost_estimate=pl.CostEstimate(flops=20_000_000_000, bytes_accessed=64_000_000, transcendentals=0),
        name="smooth_and_gather",
    )(probes, kappa)


def each_used_block(count, work):
    def some(index, carry):
        work([index * TOGETHER + step for step in range(TOGETHER)])
        return carry

    lax.fori_loop(0, (count + TOGETHER - 1) // TOGETHER, some, 0)


def forward_kernel(source_ref, receptor_ref, count_ref, field_ref, blocks_ref, out_ref, total):
    count = count_ref[0]

    def work(slots):
        products = []
        for slot in slots:
            source = source_ref[slot]
            half = pl.ds(pl.multiple_of(source % 2 * BLK, BLK), BLK)
            products.append(
                lax.dot_general(
                    field_ref[source // 2, :, half],
                    blocks_ref[slot],
                    (((1,), (1,)), ((), ())),
                    preferred_element_type=F32,
                )
            )
        for slot, product in zip(slots, products):
            total[jnp.where(slot < count, receptor_ref[slot], RB_LOC)] += product

    total[...] = jnp.zeros_like(total)
    each_used_block(count, work)
    out_ref[...] = total[0:RB_LOC].astype(BF16)


def adjoint_kernel(source_ref, receptor_ref, count_ref, weighted_ref, blocks_ref, out_ref, total):
    count, spare = count_ref[0], total.shape[0] - 1

    def work(slots):
        products = [
            jnp.dot(weighted_ref[receptor_ref[slot]], blocks_ref[slot], preferred_element_type=F32) for slot in slots
        ]
        for slot, product in zip(slots, products):
            total[jnp.where(slot < count, source_ref[slot], spare)] += product

    total[...] = jnp.zeros_like(total)
    each_used_block(count, work)
    for row in range(out_ref.shape[0]):
        for half in range(2):
            out_ref[row, :, half * BLK : (half + 1) * BLK] = total[2 * row + half].astype(BF16)


def block_products(kernel, name, out_shape, total_shape, sources, receptors, count, dense, blocks):
    smem = pl.BlockSpec(memory_space=pltpu.SMEM)
    return pl.pallas_call(
        kernel,
        out_shape=jax.ShapeDtypeStruct(out_shape, BF16),
        in_specs=[smem, smem, smem, pl.BlockSpec(memory_space=VMEM), pl.BlockSpec(memory_space=VMEM)],
        out_specs=pl.BlockSpec(memory_space=VMEM),
        scratch_shapes=[VMEM(total_shape, F32)],
        compiler_params=pltpu.CompilerParams(vmem_limit_bytes=VMEM_LIMIT),
        name=name,
    )(sources, receptors, count, dense, blocks)


def reduce_kernel(planes, probes, weight_ref, mine_ref, out_ref, first, part, second, line, mixed, last, *sems):
    me = lax.axis_index("src")
    group = lax.axis_index("rcv")
    plane, spot = me // PLANE, me % PLANE
    pairs = iter(sems)
    a_plane, a_line, c_line, c_plane, ga_line, ga_plane, gc_plane, gc_line = zip(pairs, pairs)
    rows = mine_ref.shape[2]
    cut = rows * 3 // 4
    upper, lower = pl.ds(0, cut), pl.ds(cut, rows - cut)
    half_planes = planes // 2
    in_planes = range(1, PLANE)
    in_lines = range(1, planes)

    def spot_of(distance):
        return lax.rem(spot + distance, PLANE)

    def plane_of(distance):
        return lax.rem(plane + distance, planes)

    def in_plane(distance):
        return (plane * PLANE + spot_of(distance), group)

    def in_line(distance):
        return (plane_of(distance) * PLANE + spot, group)

    def copy(pair, index, src, dst, device):
        return remote(src, dst, pair[0].at[index], pair[1].at[index], device)

    def some(half):
        return pl.ds(half * half_planes, half_planes)

    def scatter_a_plane(d, half):
        return copy(
            a_plane, (d - 1, half), mine_ref.at[spot_of(d), some(half), upper], first.at[d - 1, some(half)], in_plane(d)
        )

    def scatter_a_line(piece):
        d = lax.rem(piece + planes - plane, planes)
        return copy(a_line, (d - 1,), part.at[piece], second.at[d - 1], (piece * PLANE + spot, group))

    def scatter_c_line(d):
        return copy(c_line, (d - 1,), mine_ref.at[:, plane_of(d), lower], line.at[d - 1], in_line(d))

    def scatter_c_plane(d):
        return copy(c_plane, (d - 1,), mixed.at[spot_of(d)], last.at[d - 1], in_plane(d))

    def gather_a_line(d):
        where = out_ref.at[spot, plane, upper]
        return copy(ga_line, (d - 1,), where, where, in_line(d))

    def gather_a_plane(d, half):
        where = out_ref.at[spot, some(half), upper]
        return copy(ga_plane, (d - 1, half), where, where, in_plane(d))

    def gather_c_plane(d):
        where = out_ref.at[spot, plane, lower]
        return copy(gc_plane, (d - 1,), where, where, in_plane(d))

    def gather_c_line(d):
        where = out_ref.at[:, plane, lower]
        return copy(gc_line, (d - 1,), where, where, in_line(d))

    partners = [in_plane(d) for d in in_planes] + [in_line(d) for d in in_lines]
    announce(partners)
    await_all(partners)
    for d in in_planes:
        scatter_a_plane(d, 0).start()
    for d in in_lines:
        scatter_c_line(d).start()
    for d in in_planes:
        scatter_a_plane(d, 1).start()
    weight = weight_ref[pl.ds(spot * (RB_LOC // PLANE) + plane * rows // probes, 1), :]

    def finish_half(half):
        for d in in_planes:
            scatter_a_plane(d, half).wait_recv()
        for index in range(half_planes):
            piece = half * half_planes + index
            total = mine_ref[spot, piece, 0:cut].astype(F32)
            for other in range(PLANE - 1):
                total = total + first[other, piece].astype(F32)
            part[piece] = total.astype(BF16)

            @pl.when(piece != plane)
            def _():
                scatter_a_line(piece).start()

    finish_half(0)
    for d in in_lines:
        scatter_c_line(d).wait_recv()
    for d in [*in_planes, 0]:
        piece = spot_of(d)
        total = mine_ref[piece, plane, cut:rows].astype(F32)
        for other in range(planes - 1):
            total = total + line[other, piece].astype(F32)
        mixed[piece] = total.astype(BF16)
        if d:
            scatter_c_plane(d).start()
    finish_half(1)
    for d in in_planes:
        scatter_c_plane(d).wait_recv()
    total = mixed[spot].astype(F32)
    for other in range(PLANE - 1):
        total = total + last[other].astype(F32)
    out_ref[spot, plane, cut:rows] = (total * weight).astype(BF16)
    for d in in_planes:
        gather_c_plane(d).start()

    def landed(piece):
        return lax.rem(plane + planes - piece, planes) - 1

    for d in in_lines:
        copy(a_line, (d - 1,), part.at[plane], second.at[d - 1], in_line(d)).wait_recv()
    total = part[plane].astype(F32)
    for other in range(planes - 1):
        total = total + second[other].astype(F32)
    out_ref[spot, plane, 0:cut] = (total * weight).astype(BF16)
    for d in in_lines:
        gather_a_line(d).start()
    for d in in_planes:
        gather_c_plane(d).wait_recv()
    for d in in_lines:
        gather_c_line(d).start()
    near = plane // half_planes
    for half in (near, 1 - near):
        for index in range(half_planes):
            piece = half * half_planes + index

            @pl.when(piece != plane)
            def _():
                where = out_ref.at[spot, piece, upper]
                copy(ga_line, (landed(piece),), where, where, in_line(1)).wait_recv()

        for d in in_planes:
            gather_a_plane(d, half).start()
    for d in in_planes:
        for half in (0, 1):
            gather_a_plane(d, half).wait()
            scatter_a_plane(d, half).wait_send()
        scatter_c_plane(d).wait_send()
        gather_c_plane(d).wait_send()
    for d in in_lines:
        gather_c_line(d).wait()
        gather_a_line(d).wait_send()
        scatter_c_line(d).wait_send()
        copy(a_line, (d - 1,), part.at[plane], second.at[d - 1], in_line(d)).wait_send()


def reduce_and_weigh(n_src, evolved, weight):
    blocks, probes, receptors = evolved.shape
    planes = n_src // PLANE
    rows = blocks * probes // (PLANE * planes)
    cut = rows * 3 // 4
    dma = pltpu.SemaphoreType.DMA
    per_spot, per_plane, halves = (PLANE - 1,), (planes - 1,), (PLANE - 1, 2)
    counts = (halves, per_plane, per_plane, per_spot, per_plane, halves, per_spot, per_plane)
    out = pl.pallas_call(
        functools.partial(reduce_kernel, planes, probes),
        out_shape=jax.ShapeDtypeStruct((PLANE, planes, rows, receptors), BF16),
        in_specs=[pl.BlockSpec(memory_space=VMEM)] * 2,
        out_specs=pl.BlockSpec(memory_space=VMEM),
        scratch_shapes=[
            VMEM((PLANE - 1, planes, cut, receptors), BF16),
            VMEM((planes, cut, receptors), BF16),
            VMEM((planes - 1, cut, receptors), BF16),
            VMEM((planes - 1, PLANE, rows - cut, receptors), BF16),
            VMEM((PLANE, rows - cut, receptors), BF16),
            VMEM((PLANE - 1, rows - cut, receptors), BF16),
        ]
        + [dma(count) for count in counts for _ in range(2)],
        compiler_params=pltpu.CompilerParams(
            collective_id=1, has_side_effects=True, vmem_limit_bytes=VMEM_LIMIT
        ),
        name="reduce_and_weigh",
    )(weight, evolved.reshape(PLANE, planes, rows, receptors))
    return out.reshape(blocks, probes, receptors)


def back_kernel(
    n_src, terms_ref, probes_ref, kext_ref, out_ref, pair, relayed, joined, far, edge, halo, wide, kwide, flat,
    edge_send, edge_recv, send, recv,
):
    me, group, before, after, twin, opposite = neighbours(n_src)
    lat = kext_ref.shape[0] - 16
    loc, lon = probes_ref.shape[0] // lat, probes_ref.shape[1]
    diagonal = 3 - group
    order = (0, lat // SMOOTH - 1) + tuple(range(1, lat // SMOOTH - 1))
    partners = [before, after, (me, twin), (me, opposite)]
    announce(partners)
    await_all(partners)

    def term(owner, piece):
        return terms_ref.at[
            pl.ds(piece * SMOOTH, SMOOTH), pl.ds(pl.multiple_of(owner * loc, loc), loc), :
        ]

    def for_relay(k):
        return remote(term(diagonal, k), relayed.at[k], send.at[0, k], recv.at[0, k], (me, twin))

    def for_twin(k):
        return remote(term(twin, k), pair.at[k], send.at[1, k], recv.at[1, k], (me, twin))

    def across(k):
        return remote(joined.at[k], far.at[k], send.at[2, k], recv.at[2, k], (me, opposite))

    edges = [
        remote(edge.at[0], halo.at[1], edge_send.at[0], edge_recv.at[0], before),
        remote(edge.at[1], halo.at[0], edge_send.at[1], edge_recv.at[1], after),
    ]
    for k in order:
        for_relay(k).start()
    for k in order:
        for_twin(k).start()
    for k in order:
        for_relay(k).wait_recv()
        joined[k] = (term(opposite, k)[...].astype(F32) + relayed[k].astype(F32)).astype(BF16)
        across(k).start()
    spread_kappa(n_src, me, kext_ref, kwide, range(lat + 2 * SMOOTH))
    for k in order:
        for_twin(k).wait_recv()
        across(k).wait_recv()
        total = term(group, k)[...].astype(F32) + pair[k].astype(F32) + far[k].astype(F32)
        wide[SMOOTH + k * SMOOTH : 2 * SMOOTH + k * SMOOTH] = total
        if k == 0:
            edge[0] = total.astype(BF16)
            edges[0].start()
        if k == lat // SMOOTH - 1:
            edge[1] = total.astype(BF16)
            edges[1].start()
    for copy in edges:
        copy.wait()
    wide[0:SMOOTH] = halo[0].astype(F32)
    wide[lat + SMOOTH :] = halo[1].astype(F32)

    def one_slab(slab, carry):
        for half in range(SLAB // 8):
            some = pl.ds(pl.multiple_of(slab * SLAB + half * 8, 8), 8)
            value = wide[:, some, :]
            for step in range(SMOOTH):
                scaled = kwide[step : lat + 2 * SMOOTH - step] * value
                centre = scaled[1:-1]
                lap = scaled[:-2] + scaled[2:] + beside(centre) - 4.0 * centre
                value = value[1:-1] + lap
            for row in range(lat):
                for side in range(lon // BLK):
                    flat[side, pl.ds(half * 8 * lat + row, 8, stride=lat), :] = value[
                        row, :, side * BLK : (side + 1) * BLK
                    ]
        some = pl.ds(pl.multiple_of(slab * SLAB * lat, SLAB * lat), SLAB * lat)
        for side in range(lon // BLK):
            lanes = slice(side * BLK, (side + 1) * BLK)
            out_ref[some, lanes] = flat[side] + probes_ref[some, lanes].astype(F32)
        return carry

    lax.fori_loop(0, loc // SLAB, one_slab, 0)
    for k in order:
        for_relay(k).wait_send()
        for_twin(k).wait_send()
        across(k).wait_send()


def scatter_and_smooth(n_src, terms, probes, kext):
    lat = kext.shape[0] - 16
    loc, lon = probes.shape[0] // lat, probes.shape[1]
    pieces = lat // SMOOTH
    landing = VMEM((pieces, SMOOTH, loc, lon), BF16)
    dma = pltpu.SemaphoreType.DMA
    return pl.pallas_call(
        functools.partial(back_kernel, n_src),
        out_shape=jax.ShapeDtypeStruct(probes.shape, F32),
        in_specs=[pl.BlockSpec(memory_space=VMEM)] * 3,
        out_specs=pl.BlockSpec(memory_space=VMEM),
        scratch_shapes=[
            landing,
            landing,
            landing,
            landing,
            VMEM((2, SMOOTH, loc, lon), BF16),
            VMEM((2, SMOOTH, loc, lon), BF16),
            VMEM((lat + 2 * SMOOTH, loc, lon), F32),
            VMEM((lat + 2 * SMOOTH, 8, lon), F32),
            VMEM((lon // BLK, SLAB * lat, BLK), F32),
            dma((2,)),
            dma((2,)),
            dma((3, pieces)),
            dma((3, pieces)),
        ],
        compiler_params=pltpu.CompilerParams(
            collective_id=2, has_side_effects=True, vmem_limit_bytes=VMEM_LIMIT
        ),
        name="scatter_and_smooth",
    )(terms, probes, kext)


def per_device(probes, kappa, footprint, block_source, block_receptor, block_count, obs_weight):
    n_src, n_rcv = lax.axis_size("src"), lax.axis_size("rcv")
    loc, lat, lon = probes.shape
    flat = probes.reshape(loc * lat, lon)
    total = loc * n_rcv
    blocks = footprint.reshape(footprint.shape[2:])
    sources = block_source.reshape(-1)
    receptors = block_receptor.reshape(-1)
    count = block_count.reshape(1)
    field, kext = smooth_and_gather(n_src, n_rcv, flat, kappa)
    evolved = block_products(
        forward_kernel, "forward", (RB_LOC, total, BLK), (RB_LOC + 1, total, BLK),
        sources, receptors, count, field, blocks,
    )
    weighted = reduce_and_weigh(n_src, evolved, obs_weight.reshape(RB_LOC, BLK))
    terms = block_products(
        adjoint_kernel, "adjoint", (lat, total, lon), (lat * lon // BLK + 1, total, BLK),
        sources, receptors, count, weighted, blocks,
    )
    out = scatter_and_smooth(n_src, terms, flat, kext)
    return out.reshape(loc, lat, lon)


def solution(mesh):
    placed = (
        P("rcv", "src", None),
        P("src", None),
        P("src", "rcv", None, None, None),
        P("src", "rcv", None),
        P("src", "rcv", None),
        P("src", "rcv"),
        P("rcv"),
    )
    return jax.shard_map(
        per_device, mesh=mesh, in_specs=placed, out_specs=P("rcv", "src", None), check_vma=False
    )
```

time: 136 us -> 97.7 us (0.72)
  Pallas kernels: 130 us -> 92.3 us
  local copies, waits for them, and re-layouts: 4.8 us -> 3.12 us
    pallas_call x1, Pallas kernels: 42.1 us -> 26 us  [scatter_and_smooth(): pl.pallas_call(functools.partial(back_kernel, n_src), out_shape=jax.Shape...]
    pallas_call x1, Pallas kernels: 42.3 us -> 31.4 us  [reduce_and_weigh(): pl.pallas_call(functools.partial(reduce_kernel, planes, probes), out_shap...]
    pallas_call x1, Pallas kernels: 33.9 us -> 27.5 us  [smooth_and_gather(): pl.pallas_call(functools.partial(smooth_kernel, n_src), out_shape=(jax.Sh...]
    pallas_call x2, Pallas kernels: 11.8 us -> 7.39 us  [block_products(): pl.pallas_call(kernel, out_shape=jax.ShapeDtypeStruct(out_shape, BF16), i...]
    transpose x1 -> x0, local copies, waits for them, and re-layouts: 2.81 us -> none  [per_device(): return out.transpose(1, 0, 2)]
    unnamed x1 -> x17, local copies, waits for them, and re-layouts: 1.99 us -> 3.12 us
where the time goes in v2:
time: 97.7 us; the launch traced here: 96.2 us
  Pallas kernels  92.3 us (94%)
  local copies, waits for them, and re-layouts  3.12 us (3%)
    pallas_call x1, Pallas kernels, reduce_and_weigh(): pl.pallas_call(functools.partial(reduce_kernel, planes, probes), out_shap...  31.4 us
    pallas_call x1, Pallas kernels, smooth_and_gather(): pl.pallas_call(functools.partial(smooth_kernel, n_src), out_shape=(jax.Sh...  27.5 us
    pallas_call x1, Pallas kernels, scatter_and_smooth(): pl.pallas_call(functools.partial(back_kernel, n_src), out_shape=jax.Shape...  26 us
    pallas_call x2, Pallas kernels, block_products(): pl.pallas_call(kernel, out_shape=jax.ShapeDtypeStruct(out_shape, BF16), i...  7.39 us
    unnamed x17, local copies, waits for them, and re-layouts  3.12 us

profile of v2, /device:TPU:1, one launch (start us, length us, event | category | flops | bytes accessed | tf_op | source)
XLA Modules:
  0.0 96.2 jit_solution(583336885215080733)
XLA Ops:
  0.7 0.0 slice-start
  0.7 0.0 copy-start
  0.7 1.2 %copy-done = bf16[64,16,256]{2,1,0:T(8,128)(2,1)S(1)} copy-done((bf16[64,16,256]{2,1,0:T(8,128)(2,1)S(1)}, bf16[64,16,256]{2,1,0:T(8,128)(2,1)}, u32[]{:S(2)}) %copy-start) | copy-done | bytes 524312
  1.9 0.0 copy-start.5
  1.9 0.9 copy-done.5
  2.8 0.0 slice-start.1
  2.8 0.0 copy-start.3
  2.8 0.0 copy-start.4
  2.8 27.5 %smooth_and_gather.1 = (bf16[16,256,256]{2,1,0:T(8,128)(2,1)S(1)}, f32[32,256]{1,0:T(8,128)S(1)}) custom-call(bf16[1024,256]{1,0:T(8,128)(2,1)S(1)} %bitcast.18, f32[16,256]{1,0:T(8,128)S(1)} %copy-done.5), custom_call_target="tpu_custom_call" | custom-call | flops 20000000000 | bytes 64000000 | tf_op jit(solution)/shard_map/smooth_and_gather/pallas_call | solution.py:189
  30.3 0.0 slice-done
  30.3 0.0 slice-done.1
  30.3 0.0 copy-done.3
  30.3 0.0 copy-done.4
  30.3 0.0 copy-start.2
  30.3 3.6 %forward.1 = bf16[16,256,128]{2,1,0:T(8,128)(2,1)S(1)} custom-call(s32[192]{0:T(256)S(1)} %bitcast.21, s32[192]{0:T(256)S(1)} %bitcast.23, s32[1]{0:T(128)} %bitcast.9.count_ref, bf16[16,256,256]{2,1,0:T(8,128)(2,1)S(1)} %get-tuple-element.7.field_ref, bf16[192,128,128]{2,1,0:T(8,128)(2,1)S(1)} %bitcast.13), custom_call_target="tpu_custom_call" | custom-call | tf_op jit(solution)/shard_map/forward/pallas_call | solution.py:267
  33.9 0.0 copy-done.2
  33.9 31.4 %reduce_and_weigh.1 = bf16[8,8,64,128]{3,2,1,0:T(8,128)(2,1)S(1)} custom-call(f32[16,128]{1,0:T(8,128)S(1)} %bitcast.20, bf16[8,8,64,128]{3,2,1,0:T(8,128)(2,1)S(1)} %bitcast.17), custom_call_target="tpu_custom_call" | custom-call | tf_op jit(solution)/shard_map/reduce_and_weigh/pallas_call | solution.py:434
  65.4 0.0 copy-start.1
  65.4 3.8 %adjoint.1.terms_ref = bf16[16,256,256]{2,1,0:T(8,128)(2,1)S(1)} custom-call(s32[192]{0:T(256)S(1)} %bitcast.22, s32[192]{0:T(256)S(1)} %bitcast.24, s32[1]{0:T(128)} %bitcast.10.count_ref, bf16[16,256,128]{2,1,0:T(8,128)(2,1)S(1)} %bitcast.16, bf16[192,128,128]{2,1,0:T(8,128)(2,1)S(1)} %bitcast.14), custom_call_target="tpu_custom_call" | custom-call | tf_op jit(solution)/shard_map/adjoint/pallas_call | solution.py:267
  69.2 0.0 copy-done.1
  69.2 26.0 %scatter_and_smooth.1 = f32[1024,256]{1,0:T(8,128)S(1)} custom-call(bf16[16,256,256]{2,1,0:T(8,128)(2,1)S(1)} %adjoint.1.terms_ref, bf16[1024,256]{1,0:T(8,128)(2,1)S(1)} %bitcast.19, f32[32,256]{1,0:T(8,128)S(1)} %get-tuple-element.8.kext_ref), custom_call_target="tpu_custom_call" | custom-call | tf_op jit(solution)/shard_map/scatter_and_smooth/pallas_call | solution.py:545
  95.2 1.0 %copy.10 = f32[64,16,256]{2,1,0:T(8,128)} copy(f32[64,16,256]{2,1,0:T(8,128)S(1)} %bitcast.15) | data formatting | bytes 2097152
  (1 shorter events, 0.0 us)
Async XLA Ops:
  0.7 29.6 %slice-start = ((s8[6291456]{0:T(1024)(128)(4,1)}), s8[4194304]{0:T(1024)(128)(4,1)S(1)}, s32[]{:S(2)}) async-start(s8[6291456]{0:T(1024)(128)(4,1)} %bitcast.11), calls=%async_computation | async-start | bytes 8388608
  0.7 1.2 %copy-start = (bf16[64,16,256]{2,1,0:T(8,128)(2,1)S(1)}, bf16[64,16,256]{2,1,0:T(8,128)(2,1)}, u32[]{:S(2)}) copy-start(bf16[64,16,256]{2,1,0:T(8,128)(2,1)} %param.7) | copy-start | bytes 1572868
  1.9 0.9 copy-start.5
  2.8 27.5 %slice-start.1 = ((s8[6291456]{0:T(1024)(128)(4,1)}), s8[2097152]{0:T(1024)(128)(4,1)S(1)}, s32[]{:S(2)}) async-start(s8[6291456]{0:T(1024)(128)(4,1)} %bitcast.11), calls=%async_computation.1 | async-start | bytes 4194304
  2.8 27.5 %copy-start.3 = (s32[1,1,192]{2,1,0:T(1,128)S(1)}, s32[1,1,192]{2,1,0:T(1,128)}, u32[]{:S(2)}) copy-start(s32[1,1,192]{2,1,0:T(1,128)} %param.10) | copy-start | bytes 2308
  2.8 27.5 %copy-start.4 = (s32[1,1,192]{2,1,0:T(1,128)S(1)}, s32[1,1,192]{2,1,0:T(1,128)}, u32[]{:S(2)}) copy-start(s32[1,1,192]{2,1,0:T(1,128)} %param.11) | copy-start | bytes 2308
  30.3 3.6 %copy-start.2 = (f32[2048]{0:T(1024)S(1)}, f32[2048]{0:T(1024)}, u32[]{:S(2)}) copy-start(f32[2048]{0:T(1024)} %param.13) | copy-start | bytes 24580
  65.4 3.8 %copy-start.1 = (bf16[64,16,256]{2,1,0:T(8,128)(2,1)S(1)}, bf16[64,16,256]{2,1,0:T(8,128)(2,1)}, u32[]{:S(2)}) copy-start(bf16[64,16,256]{2,1,0:T(8,128)(2,1)} %param.7) | copy-start | bytes 1572868

commit v3 on v2

--- a/solution.py
+++ b/solution.py
@@ -11,8 +11,9 @@
 RB_LOC = 16
 SMOOTH = 4
 PLANE = 8
+REDUCE_GROUPS = 4
 SLAB = 16
-TOGETHER = 16
+TOGETHER = 32
 MESH = pl.DeviceIdType.MESH
 VMEM = pltpu.VMEM
 F32 = jnp.float32
@@ -52,26 +53,37 @@
     return me, group, before, after, twin, opposite
 
 
-def beside(centre):
-    lanes = centre.shape[-1]
-    lane = lax.broadcasted_iota(jnp.int32, centre.shape, centre.ndim - 1)
-    west = jnp.where(lane == 0, 0.0, pltpu.roll(centre, 1, centre.ndim - 1))
-    east = jnp.where(lane == lanes - 1, 0.0, pltpu.roll(centre, lanes - 1, centre.ndim - 1))
-    return west + east
-
-
-def spread_kappa(n_src, me, kext_ref, kwide, rows):
+def beside(west_half, east_half):
+    axis = west_half.ndim - 1
+    lane = lax.broadcasted_iota(jnp.int32, west_half.shape, axis)
+    first, last = lane == 0, lane == BLK - 1
+    up_w, up_e = pltpu.roll(west_half, 1, axis), pltpu.roll(east_half, 1, axis)
+    down_w, down_e = pltpu.roll(west_half, BLK - 1, axis), pltpu.roll(east_half, BLK - 1, axis)
+    return (
+        jnp.where(first, 0.0, up_w) + jnp.where(last, down_e, down_w),
+        jnp.where(first, up_w, up_e) + jnp.where(last, 0.0, down_e),
+    )
+
+
+def halves_of(ref, rows, *middle):
+    return [ref[(rows, *middle, slice(side * BLK, (side + 1) * BLK))] for side in range(2)]
+
+
+def spread_kappa(n_src, me, kext_ref, kwide, keep, rows):
     for row in rows:
         value = kext_ref[8 - SMOOTH + row : 8 - SMOOTH + row + 1, :]
         if row < SMOOTH:
             value = jnp.where(me == 0, 0.0, value)
         if row >= kwide.shape[0] - SMOOTH:
             value = jnp.where(me == n_src - 1, 0.0, value)
-        kwide[row] = jnp.broadcast_to(value, kwide.shape[1:])
+        wide = jnp.broadcast_to(value, kwide.shape[1:])
+        kwide[row] = wide
+        keep[row] = 1.0 - 4.0 * wide
 
 
 def smooth_kernel(
-    n_src, probes_ref, kappa_ref, field_ref, kext_ref, flat, halo, edge, wide, kwide, edge_send, edge_recv, send, recv
+    n_src, probes_ref, kappa_ref, field_ref, kext_ref, flat, halo, edge, wide, kwide, keep,
+    edge_send, edge_recv, send, recv,
 ):
     me, group, before, after, twin, opposite = neighbours(n_src)
     lat, lon = kappa_ref.shape
@@ -92,19 +104,16 @@
             value = of_row(row)
             wide[SMOOTH + row] = value
             edge[side, place] = value.astype(BF16)
-    await_all(partners)
+    for row in range(SMOOTH, lat - SMOOTH):
+        wide[SMOOTH + row] = of_row(row)
+    kext_ref[8 : lat + 8, :] = kappa_ref[...]
+    spread_kappa(n_src, me, kext_ref, kwide, keep, range(SMOOTH, lat + SMOOTH))
     edges = [
         remote(edge.at[1], halo.at[0], edge_send.at[0], edge_recv.at[0], after),
         remote(edge.at[0], halo.at[1], edge_send.at[1], edge_recv.at[1], before),
         remote(kappa_ref.at[pl.ds(lat - 8, 8)], kext_ref.at[pl.ds(0, 8)], edge_send.at[2], edge_recv.at[2], after),
         remote(kappa_ref.at[pl.ds(0, 8)], kext_ref.at[pl.ds(lat + 8, 8)], edge_send.at[3], edge_recv.at[3], before),
     ]
-    for copy in edges:
-        copy.start()
-    for row in range(SMOOTH, lat - SMOOTH):
-        wide[SMOOTH + row] = of_row(row)
-    kext_ref[8 : lat + 8, :] = kappa_ref[...]
-    spread_kappa(n_src, me, kext_ref, kwide, range(SMOOTH, lat + SMOOTH))
 
     parts = ((SMOOTH, lat - SMOOTH), (0, SMOOTH), (lat - SMOOTH, lat))
 
@@ -128,35 +137,53 @@
 
     def smooth_part(part, slab):
         first, last = parts[part]
-        halves = []
+        groups = []
         for half in range(SLAB // 8):
             some = pl.ds(pl.multiple_of(slab * SLAB + half * 8, 8), 8)
-            value = wide[first : last + 2 * SMOOTH, some, :]
+            value = halves_of(wide, slice(first, last + 2 * SMOOTH), some)
             for step in range(SMOOTH):
-                centre = value[1:-1]
-                lap = value[:-2] + value[2:] + beside(centre) - 4.0 * centre
-                value = centre + kwide[first + step + 1 : last + 2 * SMOOTH - 1 - step] * lap
-            halves.append(value)
+                rows = slice(first + step + 1, last + 2 * SMOOTH - 1 - step)
+                centre = [v[1:-1] for v in value]
+                around = beside(*centre)
+                value = [
+                    c * k + w * (v[:-2] + v[2:] + a)
+                    for c, k, w, v, a in zip(
+                        centre, halves_of(keep, rows, slice(None)), halves_of(kwide, rows, slice(None)), value, around
+                    )
+                ]
+            groups.append(value)
         mine = pl.ds(pl.multiple_of(group * loc + slab * SLAB, SLAB), SLAB)
-        field_ref[first:last, mine, :] = jnp.concatenate(halves, axis=1).astype(BF16)
+        for side in range(2):
+            field_ref[first:last, mine, side * BLK : (side + 1) * BLK] = jnp.concatenate(
+                [g[side] for g in groups], axis=1
+            ).astype(BF16)
+
+    def post(part, slab):
         to_opposite(part, slab).start()
         to_twin(part, slab).start()
 
     def inner(slab, carry):
         smooth_part(0, slab)
+        post(0, slab)
         return carry
 
     def outer(slab, carry):
-        smooth_part(1, slab)
-        smooth_part(2, slab)
+        for part in (1, 2):
+            smooth_part(part, slab)
+            post(part, slab)
         return carry
 
-    lax.fori_loop(0, slabs, inner, 0)
+    smooth_part(0, 0)
+    await_all(partners)
+    post(0, 0)
+    for copy in edges:
+        copy.start()
+    lax.fori_loop(1, slabs, inner, 0)
     for copy in edges:
         copy.wait()
     wide[0:SMOOTH] = jnp.where(me == 0, 0.0, halo[0].astype(F32))
     wide[lat + SMOOTH :] = jnp.where(me == n_src - 1, 0.0, halo[1].astype(F32))
-    spread_kappa(n_src, me, kext_ref, kwide, [*range(SMOOTH), *range(lat + SMOOTH, lat + 2 * SMOOTH)])
+    spread_kappa(n_src, me, kext_ref, kwide, keep, [*range(SMOOTH), *range(lat + SMOOTH, lat + 2 * SMOOTH)])
     lax.fori_loop(0, slabs, outer, 0)
 
     def pass_on(parts_here):
@@ -200,6 +227,7 @@
             VMEM((2, SMOOTH, loc, lon), BF16),
             VMEM((lat + 2 * SMOOTH, loc, lon), F32),
             VMEM((lat + 2 * SMOOTH, 8, lon), F32),
+            VMEM((lat + 2 * SMOOTH, 8, lon), F32),
             dma((4,)),
             dma((4,)),
             dma((3, 3, slabs)),
@@ -284,7 +312,8 @@
     rows = mine_ref.shape[2]
     cut = rows * 3 // 4
     upper, lower = pl.ds(0, cut), pl.ds(cut, rows - cut)
-    half_planes = planes // 2
+    groups = min(REDUCE_GROUPS, planes)
+    size = planes // groups
     in_planes = range(1, PLANE)
     in_lines = range(1, planes)
 
@@ -303,12 +332,12 @@
     def copy(pair, index, src, dst, device):
         return remote(src, dst, pair[0].at[index], pair[1].at[index], device)
 
-    def some(half):
-        return pl.ds(half * half_planes, half_planes)
-
-    def scatter_a_plane(d, half):
+    def some(g):
+        return pl.ds(g * size, size)
+
+    def scatter_a_plane(d, g):
         return copy(
-            a_plane, (d - 1, half), mine_ref.at[spot_of(d), some(half), upper], first.at[d - 1, some(half)], in_plane(d)
+            a_plane, (d - 1, g), mine_ref.at[spot_of(d), some(g), upper], first.at[d - 1, some(g)], in_plane(d)
         )
 
     def scatter_a_line(piece):
@@ -325,9 +354,9 @@
         where = out_ref.at[spot, plane, upper]
         return copy(ga_line, (d - 1,), where, where, in_line(d))
 
-    def gather_a_plane(d, half):
-        where = out_ref.at[spot, some(half), upper]
-        return copy(ga_plane, (d - 1, half), where, where, in_plane(d))
+    def gather_a_plane(d, g):
+        where = out_ref.at[spot, some(g), upper]
+        return copy(ga_plane, (d - 1, g), where, where, in_plane(d))
 
     def gather_c_plane(d):
         where = out_ref.at[spot, plane, lower]
@@ -337,22 +366,19 @@
         where = out_ref.at[:, plane, lower]
         return copy(gc_line, (d - 1,), where, where, in_line(d))
 
-    partners = [in_plane(d) for d in in_planes] + [in_line(d) for d in in_lines]
-    announce(partners)
-    await_all(partners)
-    for d in in_planes:
-        scatter_a_plane(d, 0).start()
-    for d in in_lines:
-        scatter_c_line(d).start()
-    for d in in_planes:
-        scatter_a_plane(d, 1).start()
     weight = weight_ref[pl.ds(spot * (RB_LOC // PLANE) + plane * rows // probes, 1), :]
 
-    def finish_half(half):
+    def begin_group(g):
         for d in in_planes:
-            scatter_a_plane(d, half).wait_recv()
-        for index in range(half_planes):
-            piece = half * half_planes + index
+            scatter_a_plane(d, g).start()
+
+    def plane_sums(g):
+        for d in in_planes:
+            scatter_a_plane(d, g).wait_recv()
+        if g + 2 < groups:
+            begin_group(g + 2)
+        for index in range(size):
+            piece = g * size + index
             total = mine_ref[spot, piece, 0:cut].astype(F32)
             for other in range(PLANE - 1):
                 total = total + first[other, piece].astype(F32)
@@ -362,58 +388,78 @@
             def _():
                 scatter_a_line(piece).start()
 
-    finish_half(0)
-    for d in in_lines:
-        scatter_c_line(d).wait_recv()
-    for d in [*in_planes, 0]:
-        piece = spot_of(d)
-        total = mine_ref[piece, plane, cut:rows].astype(F32)
-        for other in range(planes - 1):
-            total = total + line[other, piece].astype(F32)
-        mixed[piece] = total.astype(BF16)
-        if d:
-            scatter_c_plane(d).start()
-    finish_half(1)
-    for d in in_planes:
-        scatter_c_plane(d).wait_recv()
-    total = mixed[spot].astype(F32)
-    for other in range(PLANE - 1):
-        total = total + last[other].astype(F32)
-    out_ref[spot, plane, cut:rows] = (total * weight).astype(BF16)
-    for d in in_planes:
-        gather_c_plane(d).start()
-
-    def landed(piece):
-        return lax.rem(plane + planes - piece, planes) - 1
-
-    for d in in_lines:
-        copy(a_line, (d - 1,), part.at[plane], second.at[d - 1], in_line(d)).wait_recv()
-    total = part[plane].astype(F32)
-    for other in range(planes - 1):
-        total = total + second[other].astype(F32)
-    out_ref[spot, plane, 0:cut] = (total * weight).astype(BF16)
-    for d in in_lines:
-        gather_a_line(d).start()
-    for d in in_planes:
-        gather_c_plane(d).wait_recv()
-    for d in in_lines:
-        gather_c_line(d).start()
-    near = plane // half_planes
-    for half in (near, 1 - near):
-        for index in range(half_planes):
-            piece = half * half_planes + index
+    def own_rows(g):
+        @pl.when(plane // size == g)
+        def _():
+            for d in in_lines:
+                copy(a_line, (d - 1,), part.at[plane], second.at[d - 1], in_line(d)).wait_recv()
+            total = part[plane].astype(F32)
+            for other in range(planes - 1):
+                total = total + second[other].astype(F32)
+            out_ref[spot, plane, 0:cut] = (total * weight).astype(BF16)
+            for d in in_lines:
+                gather_a_line(d).start()
+
+    def spread_group(g):
+        for index in range(size):
+            piece = g * size + index
 
             @pl.when(piece != plane)
             def _():
                 where = out_ref.at[spot, piece, upper]
-                copy(ga_line, (landed(piece),), where, where, in_line(1)).wait_recv()
+                sender = lax.rem(plane + planes - piece, planes) - 1
+                copy(ga_line, (sender,), where, where, in_line(1)).wait_recv()
 
         for d in in_planes:
-            gather_a_plane(d, half).start()
+            gather_a_plane(d, g).start()
+
+    def line_sums():
+        for d in in_lines:
+            scatter_c_line(d).wait_recv()
+        for d in [*in_planes, 0]:
+            piece = spot_of(d)
+            total = mine_ref[piece, plane, cut:rows].astype(F32)
+            for other in range(planes - 1):
+                total = total + line[other, piece].astype(F32)
+            mixed[piece] = total.astype(BF16)
+            if d:
+                scatter_c_plane(d).start()
+
+    def own_lower_rows():
+        for d in in_planes:
+            scatter_c_plane(d).wait_recv()
+        total = mixed[spot].astype(F32)
+        for other in range(PLANE - 1):
+            total = total + last[other].astype(F32)
+        out_ref[spot, plane, cut:rows] = (total * weight).astype(BF16)
+        for d in in_planes:
+            gather_c_plane(d).start()
+
+    def spread_lower_rows():
+        for d in in_planes:
+            gather_c_plane(d).wait_recv()
+        for d in in_lines:
+            gather_c_line(d).start()
+
+    partners = [in_plane(d) for d in in_planes] + [in_line(d) for d in in_lines]
+    announce(partners)
+    await_all(partners)
+    begin_group(0)
+    for d in in_lines:
+        scatter_c_line(d).start()
+    if groups > 1:
+        begin_group(1)
+    steps = [(2.6, line_sums), (6.3, own_lower_rows), (10.0, spread_lower_rows)]
+    for g in range(groups):
+        steps.append((2.5 * g, functools.partial(plane_sums, g)))
+        steps.append((2.5 * g + 3.5, functools.partial(own_rows, g)))
+        steps.append((2.5 * g + 7.0, functools.partial(spread_group, g)))
+    for _, step in sorted(steps, key=lambda pair: pair[0]):
+        step()
     for d in in_planes:
-        for half in (0, 1):
-            gather_a_plane(d, half).wait()
-            scatter_a_plane(d, half).wait_send()
+        for g in range(groups):
+            gather_a_plane(d, g).wait()
+            scatter_a_plane(d, g).wait_send()
         scatter_c_plane(d).wait_send()
         gather_c_plane(d).wait_send()
     for d in in_lines:
@@ -429,8 +475,8 @@
     rows = blocks * probes // (PLANE * planes)
     cut = rows * 3 // 4
     dma = pltpu.SemaphoreType.DMA
-    per_spot, per_plane, halves = (PLANE - 1,), (planes - 1,), (PLANE - 1, 2)
-    counts = (halves, per_plane, per_plane, per_spot, per_plane, halves, per_spot, per_plane)
+    per_spot, per_plane, parts = (PLANE - 1,), (planes - 1,), (PLANE - 1, min(REDUCE_GROUPS, planes))
+    counts = (parts, per_plane, per_plane, per_spot, per_plane, parts, per_spot, per_plane)
     out = pl.pallas_call(
         functools.partial(reduce_kernel, planes, probes),
         out_shape=jax.ShapeDtypeStruct((PLANE, planes, rows, receptors), BF16),
@@ -454,93 +500,112 @@
 
 
 def back_kernel(
-    n_src, terms_ref, probes_ref, kext_ref, out_ref, pair, relayed, joined, far, edge, halo, wide, kwide, flat,
+    n_src, terms_ref, probes_ref, kext_ref, out_ref, pair, relayed, joined, far, edge, halo, wide, kwide, keep, flat,
     edge_send, edge_recv, send, recv,
 ):
     me, group, before, after, twin, opposite = neighbours(n_src)
     lat = kext_ref.shape[0] - 16
     loc, lon = probes_ref.shape[0] // lat, probes_ref.shape[1]
+    slabs = loc // SLAB
     diagonal = 3 - group
-    order = (0, lat // SMOOTH - 1) + tuple(range(1, lat // SMOOTH - 1))
     partners = [before, after, (me, twin), (me, opposite)]
     announce(partners)
     await_all(partners)
 
-    def term(owner, piece):
-        return terms_ref.at[
-            pl.ds(piece * SMOOTH, SMOOTH), pl.ds(pl.multiple_of(owner * loc, loc), loc), :
-        ]
+    def view(ref, k, offset=0):
+        if isinstance(k, int) and k < 2:
+            return ref.at[pl.ds(k * (lat - SMOOTH), SMOOTH), pl.ds(pl.multiple_of(offset, loc), loc), :]
+        start = pl.multiple_of(offset + (k - 2) * SLAB, SLAB)
+        return ref.at[pl.ds(SMOOTH, lat - 2 * SMOOTH), pl.ds(start, SLAB), :]
+
+    def term(owner, k):
+        return view(terms_ref, k, owner * loc)
 
     def for_relay(k):
-        return remote(term(diagonal, k), relayed.at[k], send.at[0, k], recv.at[0, k], (me, twin))
+        return remote(term(diagonal, k), view(relayed, k), send.at[0, k], recv.at[0, k], (me, twin))
 
     def for_twin(k):
-        return remote(term(twin, k), pair.at[k], send.at[1, k], recv.at[1, k], (me, twin))
+        return remote(term(twin, k), view(pair, k), send.at[1, k], recv.at[1, k], (me, twin))
 
     def across(k):
-        return remote(joined.at[k], far.at[k], send.at[2, k], recv.at[2, k], (me, opposite))
+        return remote(view(joined, k), view(far, k), send.at[2, k], recv.at[2, k], (me, opposite))
+
+    def each(work):
+        work(0)
+        work(1)
+        lax.fori_loop(2, slabs + 2, lambda k, carry: (work(k), carry)[1], 0)
+
+    def join(k):
+        for_relay(k).wait_recv()
+        view(joined, k)[...] = (term(opposite, k)[...].astype(F32) + view(relayed, k)[...].astype(F32)).astype(BF16)
+        across(k).start()
+
+    def total(k):
+        for_twin(k).wait_recv()
+        across(k).wait_recv()
+        return term(group, k)[...].astype(F32) + view(pair, k)[...].astype(F32) + view(far, k)[...].astype(F32)
 
     edges = [
         remote(edge.at[0], halo.at[1], edge_send.at[0], edge_recv.at[0], before),
         remote(edge.at[1], halo.at[0], edge_send.at[1], edge_recv.at[1], after),
     ]
-    for k in order:
-        for_relay(k).start()
-    for k in order:
-        for_twin(k).start()
-    for k in order:
-        for_relay(k).wait_recv()
-        joined[k] = (term(opposite, k)[...].astype(F32) + relayed[k].astype(F32)).astype(BF16)
-        across(k).start()
-    spread_kappa(n_src, me, kext_ref, kwide, range(lat + 2 * SMOOTH))
-    for k in order:
-        for_twin(k).wait_recv()
-        across(k).wait_recv()
-        total = term(group, k)[...].astype(F32) + pair[k].astype(F32) + far[k].astype(F32)
-        wide[SMOOTH + k * SMOOTH : 2 * SMOOTH + k * SMOOTH] = total
-        if k == 0:
-            edge[0] = total.astype(BF16)
-            edges[0].start()
-        if k == lat // SMOOTH - 1:
-            edge[1] = total.astype(BF16)
-            edges[1].start()
-    for copy in edges:
-        copy.wait()
-    wide[0:SMOOTH] = halo[0].astype(F32)
-    wide[lat + SMOOTH :] = halo[1].astype(F32)
+    each(lambda k: for_relay(k).start())
+    each(lambda k: for_twin(k).start())
+    each(join)
+    spread_kappa(n_src, me, kext_ref, kwide, keep, range(lat + 2 * SMOOTH))
+    for k, row in ((0, SMOOTH), (1, lat)):
+        rows = total(k)
+        wide[row : row + SMOOTH] = rows
+        edge[k] = rows.astype(BF16)
+        edges[k].start()
 
     def one_slab(slab, carry):
+        probes_here = pl.ds(pl.multiple_of(slab * SLAB, SLAB), SLAB)
+        wide[2 * SMOOTH : lat, probes_here, :] = total(slab + 2)
+
+        @pl.when(slab == 0)
+        def _():
+            for copy in edges:
+                copy.wait()
+            wide[0:SMOOTH] = halo[0].astype(F32)
+            wide[lat + SMOOTH :] = halo[1].astype(F32)
+
         for half in range(SLAB // 8):
             some = pl.ds(pl.multiple_of(slab * SLAB + half * 8, 8), 8)
-            value = wide[:, some, :]
+            value = halves_of(wide, slice(None), some)
             for step in range(SMOOTH):
-                scaled = kwide[step : lat + 2 * SMOOTH - step] * value
-                centre = scaled[1:-1]
-                lap = scaled[:-2] + scaled[2:] + beside(centre) - 4.0 * centre
-                value = value[1:-1] + lap
-            for row in range(lat):
-                for side in range(lon // BLK):
-                    flat[side, pl.ds(half * 8 * lat + row, 8, stride=lat), :] = value[
-                        row, :, side * BLK : (side + 1) * BLK
-                    ]
+                rows = slice(step, lat + 2 * SMOOTH - step)
+                scaled = [w * v for w, v in zip(halves_of(kwide, rows, slice(None)), value)]
+                around = beside(*[v[1:-1] for v in scaled])
+                inner = slice(step + 1, lat + 2 * SMOOTH - 1 - step)
+                value = [
+                    v[1:-1] * k + (g[:-2] + g[2:] + a)
+                    for v, k, g, a in zip(value, halves_of(keep, inner, slice(None)), scaled, around)
+                ]
+            for side in range(2):
+                for row in range(lat):
+                    flat[side, pl.ds(half * 8 * lat + row, 8, stride=lat), :] = value[side][row]
         some = pl.ds(pl.multiple_of(slab * SLAB * lat, SLAB * lat), SLAB * lat)
-        for side in range(lon // BLK):
+        for side in range(2):
             lanes = slice(side * BLK, (side + 1) * BLK)
             out_ref[some, lanes] = flat[side] + probes_ref[some, lanes].astype(F32)
         return carry
 
-    lax.fori_loop(0, loc // SLAB, one_slab, 0)
-    for k in order:
+    lax.fori_loop(0, slabs, one_slab, 0)
+
+    def finish(k):
         for_relay(k).wait_send()
         for_twin(k).wait_send()
         across(k).wait_send()
 
+    each(finish)
+
 
 def scatter_and_smooth(n_src, terms, probes, kext):
     lat = kext.shape[0] - 16
     loc, lon = probes.shape[0] // lat, probes.shape[1]
-    pieces = lat // SMOOTH
-    landing = VMEM((pieces, SMOOTH, loc, lon), BF16)
+    pieces = loc // SLAB + 2
+    landing = VMEM((lat, loc, lon), BF16)
     dma = pltpu.SemaphoreType.DMA
     return pl.pallas_call(
         functools.partial(back_kernel, n_src),
@@ -555,6 +620,7 @@
             VMEM((2, SMOOTH, loc, lon), BF16),
             VMEM((2, SMOOTH, loc, lon), BF16),
             VMEM((lat + 2 * SMOOTH, loc, lon), F32),
+            VMEM((lat + 2 * SMOOTH, 8, lon), F32),
             VMEM((lat + 2 * SMOOTH, 8, lon), F32),
             VMEM((lon // BLK, SLAB * lat, BLK), F32),
             dma((2,)),

time: 97.7 us -> 102 us (1.044); the launches traced: 96.2 us -> 102 us
  Pallas kernels: 92.3 us -> 97.7 us
    pallas_call x1, Pallas kernels: 31.4 us -> 38.3 us  [reduce_and_weigh(): pl.pallas_call(functools.partial(reduce_kernel, planes, probes), out_shap...]
    pallas_call x2, Pallas kernels: 7.39 us -> 3.46 us  [block_products(): pl.pallas_call(kernel, out_shape=jax.ShapeDtypeStruct(out_shape, BF16), i...]
    pallas_call x1, Pallas kernels: 26 us -> 29.4 us  [scatter_and_smooth(): pl.pallas_call(functools.partial(back_kernel, n_src), out_shape=jax.Shape...]
where the time goes in v3:
time: 102 us
  Pallas kernels  97.7 us (96%)
  local copies, waits for them, and re-layouts  3.12 us (3%)
    pallas_call x1, Pallas kernels, reduce_and_weigh(): pl.pallas_call(functools.partial(reduce_kernel, planes, probes), out_shap...  38.3 us
    pallas_call x1, Pallas kernels, scatter_and_smooth(): pl.pallas_call(functools.partial(back_kernel, n_src), out_shape=jax.Shape...  29.4 us
    pallas_call x1, Pallas kernels, smooth_and_gather(): pl.pallas_call(functools.partial(smooth_kernel, n_src), out_shape=(jax.Sh...  26.6 us
    pallas_call x2, Pallas kernels, block_products(): pl.pallas_call(kernel, out_shape=jax.ShapeDtypeStruct(out_shape, BF16), i...  3.46 us
    unnamed x17, local copies, waits for them, and re-layouts  3.12 us

profile of v3, /device:TPU:1, one launch (start us, length us, event | category | flops | bytes accessed | tf_op | source)
XLA Modules:
  0.0 101.6 jit_solution(4678568676723659569)
XLA Ops:
  0.7 0.0 slice-start
  0.7 0.0 copy-start
  0.7 1.2 %copy-done = bf16[64,16,256]{2,1,0:T(8,128)(2,1)S(1)} copy-done((bf16[64,16,256]{2,1,0:T(8,128)(2,1)S(1)}, bf16[64,16,256]{2,1,0:T(8,128)(2,1)}, u32[]{:S(2)}) %copy-start) | copy-done | bytes 524312
  1.9 0.0 copy-start.5
  1.9 0.9 copy-done.5
  2.8 0.0 slice-start.1
  2.8 0.0 copy-start.3
  2.8 0.0 copy-start.4
  2.8 26.6 %smooth_and_gather.1 = (bf16[16,256,256]{2,1,0:T(8,128)(2,1)S(1)}, f32[32,256]{1,0:T(8,128)S(1)}) custom-call(bf16[1024,256]{1,0:T(8,128)(2,1)S(1)} %bitcast.18, f32[16,256]{1,0:T(8,128)S(1)} %copy-done.5), custom_call_target="tpu_custom_call" | custom-call | flops 20000000000 | bytes 64000000 | tf_op jit(solution)/shard_map/smooth_and_gather/pallas_call | solution.py:216
  29.4 0.0 slice-done
  29.4 0.0 slice-done.1
  29.4 0.0 copy-done.3
  29.4 0.0 copy-done.4
  29.5 0.0 copy-start.2
  29.5 1.6 %forward.1 = bf16[16,256,128]{2,1,0:T(8,128)(2,1)S(1)} custom-call(s32[192]{0:T(256)S(1)} %bitcast.21, s32[192]{0:T(256)S(1)} %bitcast.23, s32[1]{0:T(128)} %bitcast.9.count_ref, bf16[16,256,256]{2,1,0:T(8,128)(2,1)S(1)} %get-tuple-element.7.field_ref, bf16[192,128,128]{2,1,0:T(8,128)(2,1)S(1)} %bitcast.13), custom_call_target="tpu_custom_call" | custom-call | tf_op jit(solution)/shard_map/forward/pallas_call | solution.py:295
  31.1 0.0 copy-done.2
  31.1 38.3 %reduce_and_weigh.1 = bf16[8,8,64,128]{3,2,1,0:T(8,128)(2,1)S(1)} custom-call(f32[16,128]{1,0:T(8,128)S(1)} %bitcast.20, bf16[8,8,64,128]{3,2,1,0:T(8,128)(2,1)S(1)} %bitcast.17), custom_call_target="tpu_custom_call" | custom-call | tf_op jit(solution)/shard_map/reduce_and_weigh/pallas_call | solution.py:480
  69.4 0.0 copy-start.1
  69.4 1.9 %adjoint.1.terms_ref = bf16[16,256,256]{2,1,0:T(8,128)(2,1)S(1)} custom-call(s32[192]{0:T(256)S(1)} %bitcast.22, s32[192]{0:T(256)S(1)} %bitcast.24, s32[1]{0:T(128)} %bitcast.10.count_ref, bf16[16,256,128]{2,1,0:T(8,128)(2,1)S(1)} %bitcast.16, bf16[192,128,128]{2,1,0:T(8,128)(2,1)S(1)} %bitcast.14), custom_call_target="tpu_custom_call" | custom-call | tf_op jit(solution)/shard_map/adjoint/pallas_call | solution.py:295
  71.3 0.0 copy-done.1
  71.3 29.4 %scatter_and_smooth.1 = f32[1024,256]{1,0:T(8,128)S(1)} custom-call(bf16[16,256,256]{2,1,0:T(8,128)(2,1)S(1)} %adjoint.1.terms_ref, bf16[1024,256]{1,0:T(8,128)(2,1)S(1)} %bitcast.19, f32[32,256]{1,0:T(8,128)S(1)} %get-tuple-element.8.kext_ref), custom_call_target="tpu_custom_call" | custom-call | tf_op jit(solution)/shard_map/scatter_and_smooth/pallas_call | solution.py:610
  100.7 1.0 copy.10
  (1 shorter events, 0.0 us)
Async XLA Ops:
  0.7 28.8 %slice-start = ((s8[6291456]{0:T(1024)(128)(4,1)}), s8[4194304]{0:T(1024)(128)(4,1)S(1)}, s32[]{:S(2)}) async-start(s8[6291456]{0:T(1024)(128)(4,1)} %bitcast.11), calls=%async_computation | async-start | bytes 8388608
  0.7 1.2 %copy-start = (bf16[64,16,256]{2,1,0:T(8,128)(2,1)S(1)}, bf16[64,16,256]{2,1,0:T(8,128)(2,1)}, u32[]{:S(2)}) copy-start(bf16[64,16,256]{2,1,0:T(8,128)(2,1)} %param.7) | copy-start | bytes 1572868
  1.9 0.9 copy-start.5
  2.8 26.6 %slice-start.1 = ((s8[6291456]{0:T(1024)(128)(4,1)}), s8[2097152]{0:T(1024)(128)(4,1)S(1)}, s32[]{:S(2)}) async-start(s8[6291456]{0:T(1024)(128)(4,1)} %bitcast.11), calls=%async_computation.1 | async-start | bytes 4194304
  2.8 26.6 %copy-start.3 = (s32[1,1,192]{2,1,0:T(1,128)S(1)}, s32[1,1,192]{2,1,0:T(1,128)}, u32[]{:S(2)}) copy-start(s32[1,1,192]{2,1,0:T(1,128)} %param.10) | copy-start | bytes 2308
  2.8 26.6 %copy-start.4 = (s32[1,1,192]{2,1,0:T(1,128)S(1)}, s32[1,1,192]{2,1,0:T(1,128)}, u32[]{:S(2)}) copy-start(s32[1,1,192]{2,1,0:T(1,128)} %param.11) | copy-start | bytes 2308
  29.5 1.6 %copy-start.2 = (f32[2048]{0:T(1024)S(1)}, f32[2048]{0:T(1024)}, u32[]{:S(2)}) copy-start(f32[2048]{0:T(1024)} %param.13) | copy-start | bytes 24580
  69.4 1.9 %copy-start.1 = (bf16[64,16,256]{2,1,0:T(8,128)(2,1)S(1)}, bf16[64,16,256]{2,1,0:T(8,128)(2,1)}, u32[]{:S(2)}) copy-start(bf16[64,16,256]{2,1,0:T(8,128)(2,1)} %param.7) | copy-start | bytes 1572868

commit v4 on v3

--- a/solution.py
+++ b/solution.py
@@ -11,7 +11,6 @@
 RB_LOC = 16
 SMOOTH = 4
 PLANE = 8
-REDUCE_GROUPS = 4
 SLAB = 16
 TOGETHER = 32
 MESH = pl.DeviceIdType.MESH
@@ -81,8 +80,46 @@
         keep[row] = 1.0 - 4.0 * wide
 
 
+def make_plan(source_ref, receptor_ref, count_ref, plan_ref):
+    slots, lanes = source_ref.shape[1], plan_ref.shape[1]
+    row_of = lax.broadcasted_iota(jnp.int32, (slots, slots), 0)
+    lane_of = lax.broadcasted_iota(jnp.int32, (slots, slots), 1)
+    place = lax.broadcasted_iota(jnp.int32, (slots, lanes), 1)
+    slot = lax.broadcasted_iota(jnp.int32, (1, slots), 1)
+    used = slot < count_ref[...]
+
+    def place_of(receptor):
+        return receptor // 2 * 4 + receptor % 2
+
+    def column(row):
+        return jnp.sum(jnp.where(row_of == lane_of, row, 0.0), axis=1, keepdims=True)
+
+    first_lane = lax.broadcasted_iota(jnp.int32, (1, lanes), 1) == 0
+    for base, key_ref, other in ((0, receptor_ref, source_ref[...]), (8, source_ref, place_of(receptor_ref[...]))):
+        key = jnp.where(used, key_ref[...] * 256 + slot, 64 * 256 + slot).astype(F32)
+        tall = column(key)
+        rank = jnp.sum(jnp.where(key < tall, 1.0, 0.0), axis=1, keepdims=True)
+        here = rank.astype(jnp.int32) == place
+
+        def ordered(values):
+            return jnp.sum(jnp.where(here, values, 0.0), axis=0, keepdims=True).astype(jnp.int32)
+
+        keys = ordered(tall)
+        block = keys // 256
+        ends = jnp.sum(
+            jnp.where(tall < ((place + 1) * 256).astype(F32), 1.0, 0.0), axis=0, keepdims=True
+        ).astype(jnp.int32)
+        start = jnp.where(first_lane, 0, pltpu.roll(ends, 1, 1))
+        same = (block == pltpu.roll(block, 1, 1)) & jnp.logical_not(first_lane)
+        plan_ref[base : base + 1, :] = keys - block * 256
+        plan_ref[base + 1 : base + 2, :] = ordered(column(other.astype(F32)))
+        plan_ref[base + 2 : base + 3, :] = same.astype(jnp.int32)
+        plan_ref[base + 3 : base + 4, :] = jnp.maximum(ends - 1, 0)
+        plan_ref[base + 4 : base + 5, :] = (ends > start).astype(jnp.int32)
+
+
 def smooth_kernel(
-    n_src, probes_ref, kappa_ref, field_ref, kext_ref, flat, halo, edge, wide, kwide, keep,
+    n_src, probes_ref, kappa_ref, source_ref, receptor_ref, count_ref, field_ref, kext_ref, plan_ref, flat, halo, edge, wide, kwide, keep,
     edge_send, edge_recv, send, recv,
 ):
     me, group, before, after, twin, opposite = neighbours(n_src)
@@ -120,7 +157,7 @@
     def place(owner, part, slab):
         first, last = parts[part]
         return field_ref.at[
-            pl.ds(first, last - first), pl.ds(pl.multiple_of(owner * loc + slab * SLAB, SLAB), SLAB), :
+            pl.ds(2 * first, 2 * (last - first)), pl.ds(pl.multiple_of(owner * loc + slab * SLAB, SLAB), SLAB), :
         ]
 
     def to_twin(part, slab):
@@ -154,9 +191,9 @@
             groups.append(value)
         mine = pl.ds(pl.multiple_of(group * loc + slab * SLAB, SLAB), SLAB)
         for side in range(2):
-            field_ref[first:last, mine, side * BLK : (side + 1) * BLK] = jnp.concatenate(
-                [g[side] for g in groups], axis=1
-            ).astype(BF16)
+            smoothed = jnp.concatenate([g[side] for g in groups], axis=1).astype(BF16)
+            for row in range(first, last):
+                field_ref[2 * row + side, mine, :] = smoothed[row - first]
 
     def post(part, slab):
         to_opposite(part, slab).start()
@@ -185,6 +222,7 @@
     wide[lat + SMOOTH :] = jnp.where(me == n_src - 1, 0.0, halo[1].astype(F32))
     spread_kappa(n_src, me, kext_ref, kwide, keep, [*range(SMOOTH), *range(lat + SMOOTH, lat + 2 * SMOOTH)])
     lax.fori_loop(0, slabs, outer, 0)
+    make_plan(source_ref, receptor_ref, count_ref, plan_ref)
 
     def pass_on(parts_here):
         def one(slab, carry):
@@ -208,7 +246,7 @@
     lax.fori_loop(0, slabs, finish, 0)
 
 
-def smooth_and_gather(n_src, n_rcv, probes, kappa):
+def smooth_and_gather(n_src, n_rcv, probes, kappa, sources, receptors, count):
     lat, lon = kappa.shape
     loc = probes.shape[0] // lat
     slabs = loc // SLAB
@@ -216,11 +254,12 @@
     return pl.pallas_call(
         functools.partial(smooth_kernel, n_src),
         out_shape=(
-            jax.ShapeDtypeStruct((lat, loc * n_rcv, lon), BF16),
+            jax.ShapeDtypeStruct((lat * lon // BLK, loc * n_rcv, BLK), BF16),
             jax.ShapeDtypeStruct((lat + 16, lon), F32),
+            jax.ShapeDtypeStruct((16, 256), jnp.int32),
         ),
-        in_specs=[pl.BlockSpec(memory_space=VMEM)] * 2,
-        out_specs=(pl.BlockSpec(memory_space=VMEM),) * 2,
+        in_specs=[pl.BlockSpec(memory_space=VMEM)] * 5,
+        out_specs=(pl.BlockSpec(memory_space=VMEM),) * 3,
         scratch_shapes=[
             VMEM((lon // BLK, loc * lat, BLK), F32),
             VMEM((2, SMOOTH, loc, lon), BF16),
@@ -238,72 +277,33 @@
         ),
         cost_estimate=pl.CostEstimate(flops=20_000_000_000, bytes_accessed=64_000_000, transcendentals=0),
         name="smooth_and_gather",
-    )(probes, kappa)
-
-
-def each_used_block(count, work):
-    def some(index, carry):
-        work([index * TOGETHER + step for step in range(TOGETHER)])
-        return carry
-
-    lax.fori_loop(0, (count + TOGETHER - 1) // TOGETHER, some, 0)
-
-
-def forward_kernel(source_ref, receptor_ref, count_ref, field_ref, blocks_ref, out_ref, total):
-    count = count_ref[0]
-
-    def work(slots):
-        products = []
-        for slot in slots:
-            source = source_ref[slot]
-            half = pl.ds(pl.multiple_of(source % 2 * BLK, BLK), BLK)
-            products.append(
-                lax.dot_general(
-                    field_ref[source // 2, :, half],
-                    blocks_ref[slot],
-                    (((1,), (1,)), ((), ())),
-                    preferred_element_type=F32,
-                )
-            )
-        for slot, product in zip(slots, products):
-            total[jnp.where(slot < count, receptor_ref[slot], RB_LOC)] += product
-
-    total[...] = jnp.zeros_like(total)
-    each_used_block(count, work)
-    out_ref[...] = total[0:RB_LOC].astype(BF16)
-
-
-def adjoint_kernel(source_ref, receptor_ref, count_ref, weighted_ref, blocks_ref, out_ref, total):
-    count, spare = count_ref[0], total.shape[0] - 1
-
-    def work(slots):
-        products = [
-            jnp.dot(weighted_ref[receptor_ref[slot]], blocks_ref[slot], preferred_element_type=F32) for slot in slots
-        ]
-        for slot, product in zip(slots, products):
-            total[jnp.where(slot < count, source_ref[slot], spare)] += product
-
-    total[...] = jnp.zeros_like(total)
-    each_used_block(count, work)
-    for row in range(out_ref.shape[0]):
-        for half in range(2):
-            out_ref[row, :, half * BLK : (half + 1) * BLK] = total[2 * row + half].astype(BF16)
-
-
-def block_products(kernel, name, out_shape, total_shape, sources, receptors, count, dense, blocks):
-    smem = pl.BlockSpec(memory_space=pltpu.SMEM)
-    return pl.pallas_call(
-        kernel,
-        out_shape=jax.ShapeDtypeStruct(out_shape, BF16),
-        in_specs=[smem, smem, smem, pl.BlockSpec(memory_space=VMEM), pl.BlockSpec(memory_space=VMEM)],
-        out_specs=pl.BlockSpec(memory_space=VMEM),
-        scratch_shapes=[VMEM(total_shape, F32)],
-        compiler_params=pltpu.CompilerParams(vmem_limit_bytes=VMEM_LIMIT),
-        name=name,
-    )(sources, receptors, count, dense, blocks)
-
-
-def reduce_kernel(planes, probes, weight_ref, mine_ref, out_ref, first, part, second, line, mixed, last, *sems):
+    )(probes, kappa, sources, receptors, count)
+
+
+def running_sums(plan_ref, base, slots, product, products, sums):
+    together = products.shape[0]
+
+    def several(turn, total):
+        for step in range(together):
+            k = turn * together + step
+            products[step] = product(plan_ref[base, k], plan_ref[base + 1, k])
+        for step in range(together):
+            k = turn * together + step
+            total = products[step] + total * plan_ref[base + 2, k].astype(F32)
+            sums[k] = total.astype(BF16)
+        return total
+
+    lax.fori_loop(0, slots // together, several, jnp.zeros(sums.shape[1:], F32))
+
+
+def block_sum(plan_ref, base, block, sums):
+    value = sums[plan_ref[base + 3, block]]
+    return (value.astype(F32) * plan_ref[base + 4, block].astype(F32)).astype(BF16)
+
+
+def reduce_kernel(
+    planes, plan_ref, field_ref, blocks_ref, weight_ref, out_ref, products, sums, mine_ref, first, part, second, line, mixed, last, *sems
+):
     me = lax.axis_index("src")
     group = lax.axis_index("rcv")
     plane, spot = me // PLANE, me % PLANE
@@ -312,7 +312,8 @@
     rows = mine_ref.shape[2]
     cut = rows * 3 // 4
     upper, lower = pl.ds(0, cut), pl.ds(cut, rows - cut)
-    groups = min(REDUCE_GROUPS, planes)
+    half_probes = field_ref.shape[1] // 2
+    groups = 2
     size = planes // groups
     in_planes = range(1, PLANE)
     in_lines = range(1, planes)
@@ -366,7 +367,36 @@
         where = out_ref.at[:, plane, lower]
         return copy(gc_line, (d - 1,), where, where, in_line(d))
 
-    weight = weight_ref[pl.ds(spot * (RB_LOC // PLANE) + plane * rows // probes, 1), :]
+    per_block = max(1, half_probes // rows)
+    weight = jnp.concatenate(
+        [
+            jnp.broadcast_to(
+                weight_ref[pl.ds(spot * (RB_LOC // PLANE) + plane % size // per_block + extra, 1), :],
+                (min(rows, half_probes), BLK),
+            )
+            for extra in range(max(1, rows // half_probes))
+        ],
+        axis=0,
+    )
+
+    def forward(half):
+        def product(slot, source):
+            return lax.dot_general(
+                field_ref[source, half * half_probes : (half + 1) * half_probes, :],
+                blocks_ref[slot],
+                (((1,), (1,)), ((), ())),
+                preferred_element_type=F32,
+            )
+
+        running_sums(plan_ref, 0, blocks_ref.shape[0], product, products, sums)
+        step = min(rows, half_probes)
+        for block in range(RB_LOC):
+            value = block_sum(plan_ref, 0, block, sums)
+            for inner in range(half_probes // step):
+                at = block % 2 * half_probes + inner * step
+                mine_ref[block // 2, half * size + at // rows, at % rows : at % rows + step] = value[
+                    inner * step : (inner + 1) * step
+                ]
 
     def begin_group(g):
         for d in in_planes:
@@ -375,8 +405,6 @@
     def plane_sums(g):
         for d in in_planes:
             scatter_a_plane(d, g).wait_recv()
-        if g + 2 < groups:
-            begin_group(g + 2)
         for index in range(size):
             piece = g * size + index
             total = mine_ref[spot, piece, 0:cut].astype(F32)
@@ -396,7 +424,7 @@
             total = part[plane].astype(F32)
             for other in range(planes - 1):
                 total = total + second[other].astype(F32)
-            out_ref[spot, plane, 0:cut] = (total * weight).astype(BF16)
+            out_ref[spot, plane, 0:cut] = (total * weight[0:cut]).astype(BF16)
             for d in in_lines:
                 gather_a_line(d).start()
 
@@ -431,7 +459,7 @@
         total = mixed[spot].astype(F32)
         for other in range(PLANE - 1):
             total = total + last[other].astype(F32)
-        out_ref[spot, plane, cut:rows] = (total * weight).astype(BF16)
+        out_ref[spot, plane, cut:rows] = (total * weight[cut:rows]).astype(BF16)
         for d in in_planes:
             gather_c_plane(d).start()
 
@@ -443,19 +471,22 @@
 
     partners = [in_plane(d) for d in in_planes] + [in_line(d) for d in in_lines]
     announce(partners)
+    forward(0)
     await_all(partners)
     begin_group(0)
+    forward(1)
     for d in in_lines:
         scatter_c_line(d).start()
-    if groups > 1:
-        begin_group(1)
-    steps = [(2.6, line_sums), (6.3, own_lower_rows), (10.0, spread_lower_rows)]
-    for g in range(groups):
-        steps.append((2.5 * g, functools.partial(plane_sums, g)))
-        steps.append((2.5 * g + 3.5, functools.partial(own_rows, g)))
-        steps.append((2.5 * g + 7.0, functools.partial(spread_group, g)))
-    for _, step in sorted(steps, key=lambda pair: pair[0]):
-        step()
+    begin_group(1)
+    plane_sums(0)
+    line_sums()
+    plane_sums(1)
+    own_lower_rows()
+    own_rows(0)
+    own_rows(1)
+    spread_group(0)
+    spread_lower_rows()
+    spread_group(1)
     for d in in_planes:
         for g in range(groups):
             gather_a_plane(d, g).wait()
@@ -469,48 +500,50 @@
         copy(a_line, (d - 1,), part.at[plane], second.at[d - 1], in_line(d)).wait_send()
 
 
-def reduce_and_weigh(n_src, evolved, weight):
-    blocks, probes, receptors = evolved.shape
+def reduce_and_weigh(n_src, plan, field, blocks, weight):
+    probes = field.shape[1]
+    slots = blocks.shape[0]
     planes = n_src // PLANE
-    rows = blocks * probes // (PLANE * planes)
+    rows = RB_LOC * probes // (PLANE * planes)
     cut = rows * 3 // 4
     dma = pltpu.SemaphoreType.DMA
-    per_spot, per_plane, parts = (PLANE - 1,), (planes - 1,), (PLANE - 1, min(REDUCE_GROUPS, planes))
+    per_spot, per_plane, parts = (PLANE - 1,), (planes - 1,), (PLANE - 1, 2)
     counts = (parts, per_plane, per_plane, per_spot, per_plane, parts, per_spot, per_plane)
-    out = pl.pallas_call(
-        functools.partial(reduce_kernel, planes, probes),
-        out_shape=jax.ShapeDtypeStruct((PLANE, planes, rows, receptors), BF16),
-        in_specs=[pl.BlockSpec(memory_space=VMEM)] * 2,
+    return pl.pallas_call(
+        functools.partial(reduce_kernel, planes),
+        out_shape=jax.ShapeDtypeStruct((PLANE, planes, rows, BLK), BF16),
+        in_specs=[pl.BlockSpec(memory_space=pltpu.SMEM)] + [pl.BlockSpec(memory_space=VMEM)] * 3,
         out_specs=pl.BlockSpec(memory_space=VMEM),
         scratch_shapes=[
-            VMEM((PLANE - 1, planes, cut, receptors), BF16),
-            VMEM((planes, cut, receptors), BF16),
-            VMEM((planes - 1, cut, receptors), BF16),
-            VMEM((planes - 1, PLANE, rows - cut, receptors), BF16),
-            VMEM((PLANE, rows - cut, receptors), BF16),
-            VMEM((PLANE - 1, rows - cut, receptors), BF16),
+            VMEM((min(TOGETHER, slots), probes // 2, BLK), F32),
+            VMEM((slots, probes // 2, BLK), BF16),
+            VMEM((PLANE, planes, rows, BLK), BF16),
+            VMEM((PLANE - 1, planes, cut, BLK), BF16),
+            VMEM((planes, cut, BLK), BF16),
+            VMEM((planes - 1, cut, BLK), BF16),
+            VMEM((planes - 1, PLANE, rows - cut, BLK), BF16),
+            VMEM((PLANE, rows - cut, BLK), BF16),
+            VMEM((PLANE - 1, rows - cut, BLK), BF16),
         ]
         + [dma(count) for count in counts for _ in range(2)],
         compiler_params=pltpu.CompilerParams(
             collective_id=1, has_side_effects=True, vmem_limit_bytes=VMEM_LIMIT
         ),
         name="reduce_and_weigh",
-    )(weight, evolved.reshape(PLANE, planes, rows, receptors))
-    return out.reshape(blocks, probes, receptors)
+    )(plan, field, blocks, weight)
 
 
 def back_kernel(
-    n_src, terms_ref, probes_ref, kext_ref, out_ref, pair, relayed, joined, far, edge, halo, wide, kwide, keep, flat,
+    n_src, plan_ref, weighted_ref, blocks_ref, probes_ref, kext_ref, out_ref, products, sums, terms_far, terms_near, pair, relayed, joined, far, edge, halo, wide, kwide, keep, flat,
     edge_send, edge_recv, send, recv,
 ):
     me, group, before, after, twin, opposite = neighbours(n_src)
     lat = kext_ref.shape[0] - 16
     loc, lon = probes_ref.shape[0] // lat, probes_ref.shape[1]
     slabs = loc // SLAB
-    diagonal = 3 - group
+    high, core = group // 2, group % 2
     partners = [before, after, (me, twin), (me, opposite)]
     announce(partners)
-    await_all(partners)
 
     def view(ref, k, offset=0):
         if isinstance(k, int) and k < 2:
@@ -518,14 +551,24 @@
         start = pl.multiple_of(offset + (k - 2) * SLAB, SLAB)
         return ref.at[pl.ds(SMOOTH, lat - 2 * SMOOTH), pl.ds(start, SLAB), :]
 
-    def term(owner, k):
-        return view(terms_ref, k, owner * loc)
+    def term(terms, core_of, k):
+        return view(terms, k, core_of * loc)
+
+    def adjoint(half, terms):
+        def product(slot, place):
+            block = weighted_ref[place + half * 2]
+            return jnp.dot(block, blocks_ref[slot], preferred_element_type=F32)
+
+        running_sums(plan_ref, 8, blocks_ref.shape[0], product, products, sums)
+        for row in range(lat):
+            for side in range(2):
+                terms[row, :, side * BLK : (side + 1) * BLK] = block_sum(plan_ref, 8, 2 * row + side, sums)
 
     def for_relay(k):
-        return remote(term(diagonal, k), view(relayed, k), send.at[0, k], recv.at[0, k], (me, twin))
+        return remote(term(terms_far, 1 - core, k), view(relayed, k), send.at[0, k], recv.at[0, k], (me, twin))
 
     def for_twin(k):
-        return remote(term(twin, k), view(pair, k), send.at[1, k], recv.at[1, k], (me, twin))
+        return remote(term(terms_near, 1 - core, k), view(pair, k), send.at[1, k], recv.at[1, k], (me, twin))
 
     def across(k):
         return remote(view(joined, k), view(far, k), send.at[2, k], recv.at[2, k], (me, opposite))
@@ -537,22 +580,27 @@
 
     def join(k):
         for_relay(k).wait_recv()
-        view(joined, k)[...] = (term(opposite, k)[...].astype(F32) + view(relayed, k)[...].astype(F32)).astype(BF16)
+        view(joined, k)[...] = (
+            term(terms_far, core, k)[...].astype(F32) + view(relayed, k)[...].astype(F32)
+        ).astype(BF16)
         across(k).start()
 
     def total(k):
         for_twin(k).wait_recv()
         across(k).wait_recv()
-        return term(group, k)[...].astype(F32) + view(pair, k)[...].astype(F32) + view(far, k)[...].astype(F32)
+        return term(terms_near, core, k)[...].astype(F32) + view(pair, k)[...].astype(F32) + view(far, k)[...].astype(F32)
 
     edges = [
         remote(edge.at[0], halo.at[1], edge_send.at[0], edge_recv.at[0], before),
         remote(edge.at[1], halo.at[0], edge_send.at[1], edge_recv.at[1], after),
     ]
+    adjoint(1 - high, terms_far)
+    await_all(partners)
     each(lambda k: for_relay(k).start())
+    spread_kappa(n_src, me, kext_ref, kwide, keep, range(lat + 2 * SMOOTH))
+    each(join)
+    adjoint(high, terms_near)
     each(lambda k: for_twin(k).start())
-    each(join)
-    spread_kappa(n_src, me, kext_ref, kwide, keep, range(lat + 2 * SMOOTH))
     for k, row in ((0, SMOOTH), (1, lat)):
         rows = total(k)
         wide[row : row + SMOOTH] = rows
@@ -601,7 +649,7 @@
     each(finish)
 
 
-def scatter_and_smooth(n_src, terms, probes, kext):
+def scatter_and_smooth(n_src, plan, weighted, blocks, probes, kext):
     lat = kext.shape[0] - 16
     loc, lon = probes.shape[0] // lat, probes.shape[1]
     pieces = loc // SLAB + 2
@@ -610,9 +658,13 @@
     return pl.pallas_call(
         functools.partial(back_kernel, n_src),
         out_shape=jax.ShapeDtypeStruct(probes.shape, F32),
-        in_specs=[pl.BlockSpec(memory_space=VMEM)] * 3,
+        in_specs=[pl.BlockSpec(memory_space=pltpu.SMEM)] + [pl.BlockSpec(memory_space=VMEM)] * 4,
         out_specs=pl.BlockSpec(memory_space=VMEM),
         scratch_shapes=[
+            VMEM((min(TOGETHER, blocks.shape[0]), 2 * loc, BLK), F32),
+            VMEM((blocks.shape[0], 2 * loc, BLK), BF16),
+            VMEM((lat, 2 * loc, lon), BF16),
+            VMEM((lat, 2 * loc, lon), BF16),
             landing,
             landing,
             landing,
@@ -632,29 +684,21 @@
             collective_id=2, has_side_effects=True, vmem_limit_bytes=VMEM_LIMIT
         ),
         name="scatter_and_smooth",
-    )(terms, probes, kext)
+    )(plan, weighted, blocks, probes, kext)
 
 
 def per_device(probes, kappa, footprint, block_source, block_receptor, block_count, obs_weight):
     n_src, n_rcv = lax.axis_size("src"), lax.axis_size("rcv")
     loc, lat, lon = probes.shape
     flat = probes.reshape(loc * lat, lon)
-    total = loc * n_rcv
     blocks = footprint.reshape(footprint.shape[2:])
-    sources = block_source.reshape(-1)
-    receptors = block_receptor.reshape(-1)
-    count = block_count.reshape(1)
-    field, kext = smooth_and_gather(n_src, n_rcv, flat, kappa)
-    evolved = block_products(
-        forward_kernel, "forward", (RB_LOC, total, BLK), (RB_LOC + 1, total, BLK),
-        sources, receptors, count, field, blocks,
+    slots = blocks.shape[0]
+    field, kext, plan = smooth_and_gather(
+        n_src, n_rcv, flat, kappa, block_source.reshape(1, slots), block_receptor.reshape(1, slots), block_count.reshape(1, 1)
     )
-    weighted = reduce_and_weigh(n_src, evolved, obs_weight.reshape(RB_LOC, BLK))
-    terms = block_products(
-        adjoint_kernel, "adjoint", (lat, total, lon), (lat * lon // BLK + 1, total, BLK),
-        sources, receptors, count, weighted, blocks,
-    )
-    out = scatter_and_smooth(n_src, terms, flat, kext)
+    weighted = reduce_and_weigh(n_src, plan, field, blocks, obs_weight.reshape(RB_LOC, BLK))
+    weighted = weighted.reshape(2 * RB_LOC, loc * n_rcv // 2, BLK)
+    out = scatter_and_smooth(n_src, plan, weighted, blocks, flat, kext)
     return out.reshape(loc, lat, lon)
 
 

time: 102 us -> 97.4 us (0.955)
  Pallas kernels: 97.7 us -> 92.4 us
    pallas_call x3 -> x1, Pallas kernels: 41.8 us -> 38 us  [reduce_and_weigh(): pl.pallas_call(functools.partial(reduce_kernel, planes), out_shape=jax.Sh...]
    pallas_call x1, Pallas kernels: 29.4 us -> 27.8 us  [scatter_and_smooth(): pl.pallas_call(functools.partial(back_kernel, n_src), out_shape=jax.Shape...]
    unnamed x17 -> x13, local copies, waits for them, and re-layouts: 3.12 us -> 4.09 us
where the time goes in v4:
time: 97.4 us; the launch traced here: 97.2 us
  Pallas kernels  92.4 us (95%)
  local copies, waits for them, and re-layouts  4.09 us (4%)
    pallas_call x1, Pallas kernels, reduce_and_weigh(): pl.pallas_call(functools.partial(reduce_kernel, planes), out_shape=jax.Sh...  38 us
    pallas_call x1, Pallas kernels, scatter_and_smooth(): pl.pallas_call(functools.partial(back_kernel, n_src), out_shape=jax.Shape...  27.8 us
    pallas_call x1, Pallas kernels, smooth_and_gather(): pl.pallas_call(functools.partial(smooth_kernel, n_src), out_shape=(jax.Sh...  26.6 us
    unnamed x13, local copies, waits for them, and re-layouts  4.09 us

profile of v4, /device:TPU:1, one launch (start us, length us, event | category | flops | bytes accessed | tf_op | source)
XLA Modules:
  0.0 97.2 jit_solution(4821602937843783017)
XLA Ops:
  0.7 0.0 copy-start.1
  0.7 1.0 %copy-done.1 = bf16[64,16,256]{2,1,0:T(8,128)(2,1)S(1)} copy-done((bf16[64,16,256]{2,1,0:T(8,128)(2,1)S(1)}, bf16[64,16,256]{2,1,0:T(8,128)(2,1)}, u32[]{:S(2)}) %copy-start.1) | copy-done | bytes 524312
  1.7 0.0 copy-start.3
  1.7 0.7 copy-done.3
  2.4 0.0 copy-start.4
  2.4 0.7 copy-done.4
  3.1 0.0 copy-start.5
  3.1 0.7 copy-done.5
  3.8 0.0 copy-start
  3.8 0.0 copy-start.2
  3.8 26.6 %smooth_and_gather.1 = (bf16[32,256,128]{2,1,0:T(8,128)(2,1)S(1)}, f32[32,256]{1,0:T(8,128)S(1)}, s32[16,256]{1,0:T(8,128)S(1)}) custom-call(bf16[1024,256]{1,0:T(8,128)(2,1)S(1)} %bitcast.11, f32[16,256]{1,0:T(8,128)S(1)} %copy-done.3, s32[1,192]{1,0:T(1,128)S(1)} %bitcast.14, s32[1,192]{1,0:T(1,128)S(1)} %bitcast.15, s32[1,1]{1,0:T(1,128)S(6)} %copy.9.count_ref), custom_call_target="tpu_custom_call" | custom-call | flops 20000000000 | bytes 64000000 | tf_op jit(solution)/shard_map/smooth_and_gather/pallas_call | solution.py:254
  30.4 0.0 copy-done
  30.4 0.0 copy-done.2
  30.4 38.0 %reduce_and_weigh.1 = bf16[8,8,64,128]{3,2,1,0:T(8,128)(2,1)S(1)} custom-call(s32[16,256]{1,0:T(8,128)S(1)} %get-tuple-element.8.plan_ref, bf16[32,256,128]{2,1,0:T(8,128)(2,1)S(1)} %get-tuple-element.9.field_ref, bf16[192,128,128]{2,1,0:T(8,128)(2,1)S(1)} %bitcast.7, f32[16,128]{1,0:T(8,128)S(1)} %bitcast.13), custom_call_target="tpu_custom_call" | custom-call | tf_op jit(solution)/shard_map/reduce_and_weigh/pallas_call | solution.py:512
  68.4 27.8 %scatter_and_smooth.1 = f32[1024,256]{1,0:T(8,128)S(1)} custom-call(s32[16,256]{1,0:T(8,128)S(1)} %get-tuple-element.8.plan_ref, bf16[32,128,128]{2,1,0:T(8,128)(2,1)S(1)} %bitcast.10, bf16[192,128,128]{2,1,0:T(8,128)(2,1)S(1)} %bitcast.8, bf16[1024,256]{1,0:T(8,128)(2,1)S(1)} %bitcast.12, f32[32,256]{1,0:T(8,128)S(1)} %get-tuple-element.10.kext_ref), custom_call_target="tpu_custom_call" | custom-call | tf_op jit(solution)/shard_map/scatter_and_smooth/pallas_call | solution.py:658
  96.2 1.0 %copy.10 = f32[64,16,256]{2,1,0:T(8,128)} copy(f32[64,16,256]{2,1,0:T(8,128)S(1)} %bitcast.9) | data formatting | bytes 2097152
Async XLA Ops:
  0.7 1.0 %copy-start.1 = (bf16[64,16,256]{2,1,0:T(8,128)(2,1)S(1)}, bf16[64,16,256]{2,1,0:T(8,128)(2,1)}, u32[]{:S(2)}) copy-start(bf16[64,16,256]{2,1,0:T(8,128)(2,1)} %param.7) | copy-start | bytes 1572868
  1.7 0.7 copy-start.3
  2.4 0.7 copy-start.4
  3.1 0.7 copy-start.5
  3.8 26.6 %copy-start = (bf16[1,1,192,128,128]{4,3,2,1,0:T(8,128)(2,1)S(1)}, bf16[1,1,192,128,128]{4,3,2,1,0:T(8,128)(2,1)}, u32[]{:S(2)}) copy-start(bf16[1,1,192,128,128]{4,3,2,1,0:T(8,128)(2,1)} %param.9) | copy-start | bytes 18874372
  3.8 26.6 %copy-start.2 = (f32[2048]{0:T(1024)S(1)}, f32[2048]{0:T(1024)}, u32[]{:S(2)}) copy-start(f32[2048]{0:T(1024)} %param.13) | copy-start | bytes 24580

commit v5 on v4

--- a/solution.py
+++ b/solution.py
@@ -12,12 +12,13 @@
 SMOOTH = 4
 PLANE = 8
 SLAB = 16
+SLOT_BASE = 64
 TOGETHER = 32
 MESH = pl.DeviceIdType.MESH
 VMEM = pltpu.VMEM
 F32 = jnp.float32
 BF16 = jnp.bfloat16
-VMEM_LIMIT = 24 * 1024 * 1024
+VMEM_LIMIT = 32 * 1024 * 1024
 
 
 def announce(devices):
@@ -80,13 +81,14 @@
         keep[row] = 1.0 - 4.0 * wide
 
 
-def make_plan(source_ref, receptor_ref, count_ref, plan_ref):
-    slots, lanes = source_ref.shape[1], plan_ref.shape[1]
+def make_plan(packed, plan_ref):
+    slots, lanes = packed.shape[1], plan_ref.shape[1]
+    sources, receptors = packed % SLOT_BASE, packed // SLOT_BASE % SLOT_BASE
     row_of = lax.broadcasted_iota(jnp.int32, (slots, slots), 0)
     lane_of = lax.broadcasted_iota(jnp.int32, (slots, slots), 1)
     place = lax.broadcasted_iota(jnp.int32, (slots, lanes), 1)
     slot = lax.broadcasted_iota(jnp.int32, (1, slots), 1)
-    used = slot < count_ref[...]
+    used = packed < SLOT_BASE * SLOT_BASE
 
     def place_of(receptor):
         return receptor // 2 * 4 + receptor % 2
@@ -95,8 +97,8 @@
         return jnp.sum(jnp.where(row_of == lane_of, row, 0.0), axis=1, keepdims=True)
 
     first_lane = lax.broadcasted_iota(jnp.int32, (1, lanes), 1) == 0
-    for base, key_ref, other in ((0, receptor_ref, source_ref[...]), (8, source_ref, place_of(receptor_ref[...]))):
-        key = jnp.where(used, key_ref[...] * 256 + slot, 64 * 256 + slot).astype(F32)
+    for base, owner, other in ((0, receptors, sources), (8, sources, place_of(receptors))):
+        key = jnp.where(used, owner * 256 + slot, 64 * 256 + slot).astype(F32)
         tall = column(key)
         rank = jnp.sum(jnp.where(key < tall, 1.0, 0.0), axis=1, keepdims=True)
         here = rank.astype(jnp.int32) == place
@@ -119,7 +121,7 @@
 
 
 def smooth_kernel(
-    n_src, probes_ref, kappa_ref, source_ref, receptor_ref, count_ref, field_ref, kext_ref, plan_ref, flat, halo, edge, wide, kwide, keep,
+    n_src, probes_ref, kappa_ref, slots_ref, field_ref, kext_ref, plan_ref, flat, halo, edge, wide, kwide, keep,
     edge_send, edge_recv, send, recv,
 ):
     me, group, before, after, twin, opposite = neighbours(n_src)
@@ -222,7 +224,7 @@
     wide[lat + SMOOTH :] = jnp.where(me == n_src - 1, 0.0, halo[1].astype(F32))
     spread_kappa(n_src, me, kext_ref, kwide, keep, [*range(SMOOTH), *range(lat + SMOOTH, lat + 2 * SMOOTH)])
     lax.fori_loop(0, slabs, outer, 0)
-    make_plan(source_ref, receptor_ref, count_ref, plan_ref)
+    make_plan(slots_ref[...], plan_ref)
 
     def pass_on(parts_here):
         def one(slab, carry):
@@ -246,7 +248,7 @@
     lax.fori_loop(0, slabs, finish, 0)
 
 
-def smooth_and_gather(n_src, n_rcv, probes, kappa, sources, receptors, count):
+def smooth_and_gather(n_src, n_rcv, probes, kappa, packed):
     lat, lon = kappa.shape
     loc = probes.shape[0] // lat
     slabs = loc // SLAB
@@ -258,7 +260,7 @@
             jax.ShapeDtypeStruct((lat + 16, lon), F32),
             jax.ShapeDtypeStruct((16, 256), jnp.int32),
         ),
-        in_specs=[pl.BlockSpec(memory_space=VMEM)] * 5,
+        in_specs=[pl.BlockSpec(memory_space=VMEM)] * 3,
         out_specs=(pl.BlockSpec(memory_space=VMEM),) * 3,
         scratch_shapes=[
             VMEM((lon // BLK, loc * lat, BLK), F32),
@@ -277,7 +279,7 @@
         ),
         cost_estimate=pl.CostEstimate(flops=20_000_000_000, bytes_accessed=64_000_000, transcendentals=0),
         name="smooth_and_gather",
-    )(probes, kappa, sources, receptors, count)
+    )(probes, kappa, packed)
 
 
 def running_sums(plan_ref, base, slots, product, products, sums):
@@ -379,21 +381,19 @@
         axis=0,
     )
 
-    def forward(half):
-        def product(slot, source):
-            return lax.dot_general(
-                field_ref[source, half * half_probes : (half + 1) * half_probes, :],
-                blocks_ref[slot],
-                (((1,), (1,)), ((), ())),
-                preferred_element_type=F32,
-            )
-
+    def product(slot, source):
+        return lax.dot_general(
+            field_ref[source], blocks_ref[slot], (((1,), (1,)), ((), ())), preferred_element_type=F32
+        )
+
+    def forward():
         running_sums(plan_ref, 0, blocks_ref.shape[0], product, products, sums)
         step = min(rows, half_probes)
         for block in range(RB_LOC):
             value = block_sum(plan_ref, 0, block, sums)
-            for inner in range(half_probes // step):
-                at = block % 2 * half_probes + inner * step
+            for inner in range(2 * half_probes // step):
+                half, at = divmod(inner * step, half_probes)
+                at += block % 2 * half_probes
                 mine_ref[block // 2, half * size + at // rows, at % rows : at % rows + step] = value[
                     inner * step : (inner + 1) * step
                 ]
@@ -471,10 +471,9 @@
 
     partners = [in_plane(d) for d in in_planes] + [in_line(d) for d in in_lines]
     announce(partners)
-    forward(0)
+    forward()
     await_all(partners)
     begin_group(0)
-    forward(1)
     for d in in_lines:
         scatter_c_line(d).start()
     begin_group(1)
@@ -515,8 +514,8 @@
         in_specs=[pl.BlockSpec(memory_space=pltpu.SMEM)] + [pl.BlockSpec(memory_space=VMEM)] * 3,
         out_specs=pl.BlockSpec(memory_space=VMEM),
         scratch_shapes=[
-            VMEM((min(TOGETHER, slots), probes // 2, BLK), F32),
-            VMEM((slots, probes // 2, BLK), BF16),
+            VMEM((min(TOGETHER, slots), probes, BLK), F32),
+            VMEM((slots, probes, BLK), BF16),
             VMEM((PLANE, planes, rows, BLK), BF16),
             VMEM((PLANE - 1, planes, cut, BLK), BF16),
             VMEM((planes, cut, BLK), BF16),
@@ -693,9 +692,10 @@
     flat = probes.reshape(loc * lat, lon)
     blocks = footprint.reshape(footprint.shape[2:])
     slots = blocks.shape[0]
-    field, kext, plan = smooth_and_gather(
-        n_src, n_rcv, flat, kappa, block_source.reshape(1, slots), block_receptor.reshape(1, slots), block_count.reshape(1, 1)
-    )
+    sources, receptors = block_source.reshape(1, slots), block_receptor.reshape(1, slots)
+    unused = lax.broadcasted_iota(jnp.int32, (1, slots), 1) >= block_count.reshape(1, 1)
+    packed = sources + SLOT_BASE * (receptors + SLOT_BASE * unused.astype(jnp.int32))
+    field, kext, plan = smooth_and_gather(n_src, n_rcv, flat, kappa, packed)
     weighted = reduce_and_weigh(n_src, plan, field, blocks, obs_weight.reshape(RB_LOC, BLK))
     weighted = weighted.reshape(2 * RB_LOC, loc * n_rcv // 2, BLK)
     out = scatter_and_smooth(n_src, plan, weighted, blocks, flat, kext)

time: 97.4 us -> 90.5 us (0.929)
  Pallas kernels: 92.4 us -> 86.1 us
  local copies, waits for them, and re-layouts: 4.09 us -> 2.74 us
    pallas_call x1, Pallas kernels: 38 us -> 32.9 us  [reduce_and_weigh(): pl.pallas_call(functools.partial(reduce_kernel, planes), out_shape=jax.Sh...]
    unnamed x13 -> x9, local copies, waits for them, and re-layouts: 4.09 us -> 2.74 us
    pallas_call x1, Pallas kernels: 27.8 us -> 26.6 us  [scatter_and_smooth(): pl.pallas_call(functools.partial(back_kernel, n_src), out_shape=jax.Shape...]
where the time goes in v5:
time: 90.5 us; the launch traced here: 90.3 us
  Pallas kernels  86.1 us (95%)
  local copies, waits for them, and re-layouts  2.74 us (3%)
    pallas_call x1, Pallas kernels, reduce_and_weigh(): pl.pallas_call(functools.partial(reduce_kernel, planes), out_shape=jax.Sh...  32.9 us
    pallas_call x1, Pallas kernels, scatter_and_smooth(): pl.pallas_call(functools.partial(back_kernel, n_src), out_shape=jax.Shape...  26.6 us
    pallas_call x1, Pallas kernels, smooth_and_gather(): pl.pallas_call(functools.partial(smooth_kernel, n_src), out_shape=(jax.Sh...  26.6 us
    unnamed x9, local copies, waits for them, and re-layouts  2.74 us

profile of v5, /device:TPU:1, one launch (start us, length us, event | category | flops | bytes accessed | tf_op | source)
XLA Modules:
  0.0 90.3 jit_solution(15936076602883522913)
XLA Ops:
  0.7 0.7 bitcast_add_fusion.slots_ref
  1.4 0.0 copy-start.1
  1.4 1.0 %copy-done.1 = bf16[64,16,256]{2,1,0:T(8,128)(2,1)S(1)} copy-done((bf16[64,16,256]{2,1,0:T(8,128)(2,1)S(1)}, bf16[64,16,256]{2,1,0:T(8,128)(2,1)}, u32[]{:S(2)}) %copy-start.1) | copy-done | bytes 524312
  2.4 0.0 copy-start.3
  2.4 0.7 copy-done.3
  3.1 0.0 copy-start
  3.1 0.0 copy-start.2
  3.1 26.6 %smooth_and_gather.1 = (bf16[32,256,128]{2,1,0:T(8,128)(2,1)S(1)}, f32[32,256]{1,0:T(8,128)S(1)}, s32[16,256]{1,0:T(8,128)S(1)}) custom-call(bf16[1024,256]{1,0:T(8,128)(2,1)S(1)} %bitcast.17, f32[16,256]{1,0:T(8,128)S(1)} %copy-done.3, s32[1,192]{1,0:T(1,128)S(1)} %bitcast_add_fusion.slots_ref), custom_call_target="tpu_custom_call" | custom-call | flops 20000000000 | bytes 64000000 | tf_op jit(solution)/shard_map/smooth_and_gather/pallas_call | solution.py:256
  29.7 0.0 copy-done
  29.7 0.0 copy-done.2
  29.7 32.9 %reduce_and_weigh.1 = bf16[8,8,64,128]{3,2,1,0:T(8,128)(2,1)S(1)} custom-call(s32[16,256]{1,0:T(8,128)S(1)} %get-tuple-element.8.plan_ref, bf16[32,256,128]{2,1,0:T(8,128)(2,1)S(1)} %get-tuple-element.9.field_ref, bf16[192,128,128]{2,1,0:T(8,128)(2,1)S(1)} %bitcast.13, f32[16,128]{1,0:T(8,128)S(1)} %bitcast.19), custom_call_target="tpu_custom_call" | custom-call | tf_op jit(solution)/shard_map/reduce_and_weigh/pallas_call | solution.py:511
  62.7 26.6 %scatter_and_smooth.1 = f32[1024,256]{1,0:T(8,128)S(1)} custom-call(s32[16,256]{1,0:T(8,128)S(1)} %get-tuple-element.8.plan_ref, bf16[32,128,128]{2,1,0:T(8,128)(2,1)S(1)} %bitcast.16, bf16[192,128,128]{2,1,0:T(8,128)(2,1)S(1)} %bitcast.14, bf16[1024,256]{1,0:T(8,128)(2,1)S(1)} %bitcast.18, f32[32,256]{1,0:T(8,128)S(1)} %get-tuple-element.10.kext_ref), custom_call_target="tpu_custom_call" | custom-call | tf_op jit(solution)/shard_map/scatter_and_smooth/pallas_call | solution.py:657
  89.3 1.0 %copy.10 = f32[64,16,256]{2,1,0:T(8,128)} copy(f32[64,16,256]{2,1,0:T(8,128)S(1)} %bitcast.15) | data formatting | bytes 2097152
Async XLA Ops:
  1.4 1.0 %copy-start.1 = (bf16[64,16,256]{2,1,0:T(8,128)(2,1)S(1)}, bf16[64,16,256]{2,1,0:T(8,128)(2,1)}, u32[]{:S(2)}) copy-start(bf16[64,16,256]{2,1,0:T(8,128)(2,1)} %param.7) | copy-start | bytes 1572868
  2.4 0.7 copy-start.3
  3.1 26.6 %copy-start = (bf16[1,1,192,128,128]{4,3,2,1,0:T(8,128)(2,1)S(1)}, bf16[1,1,192,128,128]{4,3,2,1,0:T(8,128)(2,1)}, u32[]{:S(2)}) copy-start(bf16[1,1,192,128,128]{4,3,2,1,0:T(8,128)(2,1)} %param.9) | copy-start | bytes 18874372
  3.1 26.6 %copy-start.2 = (f32[2048]{0:T(1024)S(1)}, f32[2048]{0:T(1024)}, u32[]{:S(2)}) copy-start(f32[2048]{0:T(1024)} %param.13) | copy-start | bytes 24580

commit v6 on v5

--- a/solution.py
+++ b/solution.py
@@ -18,7 +18,7 @@
 VMEM = pltpu.VMEM
 F32 = jnp.float32
 BF16 = jnp.bfloat16
-VMEM_LIMIT = 32 * 1024 * 1024
+VMEM_LIMIT = 44 * 1024 * 1024
 
 
 def announce(devices):
@@ -81,7 +81,7 @@
         keep[row] = 1.0 - 4.0 * wide
 
 
-def make_plan(packed, plan_ref):
+def make_plan(lower_pieces, packed, plan_ref):
     slots, lanes = packed.shape[1], plan_ref.shape[1]
     sources, receptors = packed % SLOT_BASE, packed // SLOT_BASE % SLOT_BASE
     row_of = lax.broadcasted_iota(jnp.int32, (slots, slots), 0)
@@ -90,14 +90,11 @@
     slot = lax.broadcasted_iota(jnp.int32, (1, slots), 1)
     used = packed < SLOT_BASE * SLOT_BASE
 
-    def place_of(receptor):
-        return receptor // 2 * 4 + receptor % 2
-
     def column(row):
         return jnp.sum(jnp.where(row_of == lane_of, row, 0.0), axis=1, keepdims=True)
 
     first_lane = lax.broadcasted_iota(jnp.int32, (1, lanes), 1) == 0
-    for base, owner, other in ((0, receptors, sources), (8, sources, place_of(receptors))):
+    for base, owner, other in ((0, receptors, sources), (8, sources, receptors)):
         key = jnp.where(used, owner * 256 + slot, 64 * 256 + slot).astype(F32)
         tall = column(key)
         rank = jnp.sum(jnp.where(key < tall, 1.0, 0.0), axis=1, keepdims=True)
@@ -117,6 +114,9 @@
         plan_ref[base + 1 : base + 2, :] = ordered(column(other.astype(F32)))
         plan_ref[base + 2 : base + 3, :] = same.astype(jnp.int32)
         plan_ref[base + 3 : base + 4, :] = jnp.maximum(ends - 1, 0)
+        if base:
+            lower = other % 2 * (lower_pieces * PLANE) + other // 2
+            plan_ref[base + 5 : base + 6, :] = ordered(column(lower.astype(F32)))
         plan_ref[base + 4 : base + 5, :] = (ends > start).astype(jnp.int32)
 
 
@@ -156,6 +156,9 @@
 
     parts = ((SMOOTH, lat - SMOOTH), (0, SMOOTH), (lat - SMOOTH, lat))
 
+    core = group % 2
+    own, far = 2 + core, core
+
     def place(owner, part, slab):
         first, last = parts[part]
         return field_ref.at[
@@ -163,15 +166,15 @@
         ]
 
     def to_twin(part, slab):
-        where = place(group, part, slab)
+        where = place(own, part, slab)
         return remote(where, where, send.at[0, part, slab], recv.at[0, part, slab], (me, twin))
 
     def to_opposite(part, slab):
-        where = place(group, part, slab)
-        return remote(where, where, send.at[1, part, slab], recv.at[1, part, slab], (me, opposite))
+        there = place(far, part, slab)
+        return remote(place(own, part, slab), there, send.at[1, part, slab], recv.at[1, part, slab], (me, opposite))
 
     def relay(part, slab):
-        where = place(opposite, part, slab)
+        where = place(far, part, slab)
         return remote(where, where, send.at[2, part, slab], recv.at[2, part, slab], (me, twin))
 
     def smooth_part(part, slab):
@@ -191,7 +194,7 @@
                     )
                 ]
             groups.append(value)
-        mine = pl.ds(pl.multiple_of(group * loc + slab * SLAB, SLAB), SLAB)
+        mine = pl.ds(pl.multiple_of(own * loc + slab * SLAB, SLAB), SLAB)
         for side in range(2):
             smoothed = jnp.concatenate([g[side] for g in groups], axis=1).astype(BF16)
             for row in range(first, last):
@@ -224,7 +227,7 @@
     wide[lat + SMOOTH :] = jnp.where(me == n_src - 1, 0.0, halo[1].astype(F32))
     spread_kappa(n_src, me, kext_ref, kwide, keep, [*range(SMOOTH), *range(lat + SMOOTH, lat + 2 * SMOOTH)])
     lax.fori_loop(0, slabs, outer, 0)
-    make_plan(slots_ref[...], plan_ref)
+    make_plan(n_src // PLANE // 4, slots_ref[...], plan_ref)
 
     def pass_on(parts_here):
         def one(slab, carry):
@@ -288,7 +291,7 @@
     def several(turn, total):
         for step in range(together):
             k = turn * together + step
-            products[step] = product(plan_ref[base, k], plan_ref[base + 1, k])
+            products[step] = product(k)
         for step in range(together):
             k = turn * together + step
             total = products[step] + total * plan_ref[base + 2, k].astype(F32)
@@ -303,9 +306,7 @@
     return (value.astype(F32) * plan_ref[base + 4, block].astype(F32)).astype(BF16)
 
 
-def reduce_kernel(
-    planes, plan_ref, field_ref, blocks_ref, weight_ref, out_ref, products, sums, mine_ref, first, part, second, line, mixed, last, *sems
-):
+def reduction(planes, plan_ref, field_ref, blocks_ref, weight_ref, products, sums, mine_ref, first, part, second, line, mixed, last, upper, lower, *sems):
     me = lax.axis_index("src")
     group = lax.axis_index("rcv")
     plane, spot = me // PLANE, me % PLANE
@@ -313,7 +314,7 @@
     a_plane, a_line, c_line, c_plane, ga_line, ga_plane, gc_plane, gc_line = zip(pairs, pairs)
     rows = mine_ref.shape[2]
     cut = rows * 3 // 4
-    upper, lower = pl.ds(0, cut), pl.ds(cut, rows - cut)
+    upper_rows, lower_rows = pl.ds(0, cut), pl.ds(cut, rows - cut)
     half_probes = field_ref.shape[1] // 2
     groups = 2
     size = planes // groups
@@ -340,7 +341,7 @@
 
     def scatter_a_plane(d, g):
         return copy(
-            a_plane, (d - 1, g), mine_ref.at[spot_of(d), some(g), upper], first.at[d - 1, some(g)], in_plane(d)
+            a_plane, (d - 1, g), mine_ref.at[spot_of(d), some(g), upper_rows], first.at[d - 1, some(g)], in_plane(d)
         )
 
     def scatter_a_line(piece):
@@ -348,55 +349,56 @@
         return copy(a_line, (d - 1,), part.at[piece], second.at[d - 1], (piece * PLANE + spot, group))
 
     def scatter_c_line(d):
-        return copy(c_line, (d - 1,), mine_ref.at[:, plane_of(d), lower], line.at[d - 1], in_line(d))
+        return copy(c_line, (d - 1,), mine_ref.at[:, plane_of(d), lower_rows], line.at[d - 1], in_line(d))
 
     def scatter_c_plane(d):
         return copy(c_plane, (d - 1,), mixed.at[spot_of(d)], last.at[d - 1], in_plane(d))
 
-    def gather_a_line(d):
-        where = out_ref.at[spot, plane, upper]
+    own_index = plane % size
+
+    def gather_a_line(d, g):
+        where = upper[g].at[spot * size + own_index]
         return copy(ga_line, (d - 1,), where, where, in_line(d))
 
     def gather_a_plane(d, g):
-        where = out_ref.at[spot, some(g), upper]
+        where = upper[g].at[pl.ds(spot * size, size)]
         return copy(ga_plane, (d - 1, g), where, where, in_plane(d))
 
-    def gather_c_plane(d):
-        where = out_ref.at[spot, plane, lower]
+    def gather_c_plane(d, g):
+        where = lower[g].at[own_index * PLANE + spot]
         return copy(gc_plane, (d - 1,), where, where, in_plane(d))
 
-    def gather_c_line(d):
-        where = out_ref.at[:, plane, lower]
+    def gather_c_line(d, g):
+        where = lower[g].at[pl.ds(own_index * PLANE, PLANE)]
         return copy(gc_line, (d - 1,), where, where, in_line(d))
 
-    per_block = max(1, half_probes // rows)
-    weight = jnp.concatenate(
-        [
-            jnp.broadcast_to(
-                weight_ref[pl.ds(spot * (RB_LOC // PLANE) + plane % size // per_block + extra, 1), :],
-                (min(rows, half_probes), BLK),
-            )
-            for extra in range(max(1, rows // half_probes))
-        ],
-        axis=0,
-    )
-
-    def product(slot, source):
+    def sender(piece):
+        return lax.rem(plane + planes - piece, planes)
+
+    def on_own_group(work):
+        for g in range(groups):
+            pl.when(plane // size == g)(functools.partial(work, g))
+
+    def others_of(g, work):
+        for index in range(size):
+            piece = g * size + index
+            pl.when(piece != plane)(functools.partial(work, piece))
+
+    weight = weight_ref[pl.ds(spot * (RB_LOC // PLANE) + own_index // (half_probes // rows), 1), :]
+
+    def product(k):
         return lax.dot_general(
-            field_ref[source], blocks_ref[slot], (((1,), (1,)), ((), ())), preferred_element_type=F32
+            field_ref[plan_ref[1, k]], blocks_ref[plan_ref[0, k]], (((1,), (1,)), ((), ())), preferred_element_type=F32
         )
 
     def forward():
         running_sums(plan_ref, 0, blocks_ref.shape[0], product, products, sums)
-        step = min(rows, half_probes)
         for block in range(RB_LOC):
             value = block_sum(plan_ref, 0, block, sums)
-            for inner in range(2 * half_probes // step):
-                half, at = divmod(inner * step, half_probes)
-                at += block % 2 * half_probes
-                mine_ref[block // 2, half * size + at // rows, at % rows : at % rows + step] = value[
-                    inner * step : (inner + 1) * step
-                ]
+            for start in range(0, 2 * half_probes, rows):
+                half, at = divmod(start, half_probes)
+                piece = half * size + (block % 2 * half_probes + at) // rows
+                mine_ref[block // 2, piece] = value[start : start + rows]
 
     def begin_group(g):
         for d in in_planes:
@@ -417,27 +419,21 @@
                 scatter_a_line(piece).start()
 
     def own_rows(g):
-        @pl.when(plane // size == g)
-        def _():
-            for d in in_lines:
-                copy(a_line, (d - 1,), part.at[plane], second.at[d - 1], in_line(d)).wait_recv()
-            total = part[plane].astype(F32)
-            for other in range(planes - 1):
-                total = total + second[other].astype(F32)
-            out_ref[spot, plane, 0:cut] = (total * weight[0:cut]).astype(BF16)
-            for d in in_lines:
-                gather_a_line(d).start()
+        for d in in_lines:
+            copy(a_line, (d - 1,), part.at[plane], second.at[d - 1], in_line(d)).wait_recv()
+        total = part[plane].astype(F32)
+        for other in range(planes - 1):
+            total = total + second[other].astype(F32)
+        upper[g][spot * size + own_index] = (total * weight).astype(BF16)
+        for d in in_lines:
+            gather_a_line(d, g).start()
 
     def spread_group(g):
-        for index in range(size):
-            piece = g * size + index
-
-            @pl.when(piece != plane)
-            def _():
-                where = out_ref.at[spot, piece, upper]
-                sender = lax.rem(plane + planes - piece, planes) - 1
-                copy(ga_line, (sender,), where, where, in_line(1)).wait_recv()
-
+        def landed(piece):
+            where = upper[g].at[spot * size + piece % size]
+            copy(ga_line, (sender(piece) - 1,), where, where, in_line(1)).wait_recv()
+
+        others_of(g, landed)
         for d in in_planes:
             gather_a_plane(d, g).start()
 
@@ -453,96 +449,84 @@
             if d:
                 scatter_c_plane(d).start()
 
-    def own_lower_rows():
+    def own_lower_rows(g):
         for d in in_planes:
             scatter_c_plane(d).wait_recv()
         total = mixed[spot].astype(F32)
         for other in range(PLANE - 1):
             total = total + last[other].astype(F32)
-        out_ref[spot, plane, cut:rows] = (total * weight[cut:rows]).astype(BF16)
+        lower[g][own_index * PLANE + spot] = (total * weight).astype(BF16)
         for d in in_planes:
-            gather_c_plane(d).start()
-
-    def spread_lower_rows():
+            gather_c_plane(d, g).start()
+
+    def spread_lower_rows(g):
         for d in in_planes:
-            gather_c_plane(d).wait_recv()
+            gather_c_plane(d, g).wait_recv()
         for d in in_lines:
-            gather_c_line(d).start()
+            gather_c_line(d, g).start()
+
+    def run():
+        begin_group(0)
+        for d in in_lines:
+            scatter_c_line(d).start()
+        begin_group(1)
+        plane_sums(0)
+        line_sums()
+        plane_sums(1)
+        on_own_group(own_lower_rows)
+        on_own_group(own_rows)
+        spread_group(0)
+        on_own_group(spread_lower_rows)
+        spread_group(1)
+
+    def ready(g):
+        for d in in_planes:
+            gather_a_plane(d, g).wait_recv()
+
+        def landed(piece):
+            where = lower[g].at[pl.ds(piece % size * PLANE, PLANE)]
+            copy(gc_line, (sender(piece) - 1,), where, where, in_line(1)).wait_recv()
+
+        others_of(g, landed)
+
+    def finish():
+        for d in in_planes:
+            for g in range(groups):
+                gather_a_plane(d, g).wait_send()
+                scatter_a_plane(d, g).wait_send()
+            scatter_c_plane(d).wait_send()
+            gather_c_plane(d, 0).wait_send()
+        for d in in_lines:
+            gather_c_line(d, 0).wait_send()
+            gather_a_line(d, 0).wait_send()
+            scatter_c_line(d).wait_send()
+            copy(a_line, (d - 1,), part.at[plane], second.at[d - 1], in_line(d)).wait_send()
 
     partners = [in_plane(d) for d in in_planes] + [in_line(d) for d in in_lines]
-    announce(partners)
-    forward()
-    await_all(partners)
-    begin_group(0)
-    for d in in_lines:
-        scatter_c_line(d).start()
-    begin_group(1)
-    plane_sums(0)
-    line_sums()
-    plane_sums(1)
-    own_lower_rows()
-    own_rows(0)
-    own_rows(1)
-    spread_group(0)
-    spread_lower_rows()
-    spread_group(1)
-    for d in in_planes:
-        for g in range(groups):
-            gather_a_plane(d, g).wait()
-            scatter_a_plane(d, g).wait_send()
-        scatter_c_plane(d).wait_send()
-        gather_c_plane(d).wait_send()
-    for d in in_lines:
-        gather_c_line(d).wait()
-        gather_a_line(d).wait_send()
-        scatter_c_line(d).wait_send()
-        copy(a_line, (d - 1,), part.at[plane], second.at[d - 1], in_line(d)).wait_send()
-
-
-def reduce_and_weigh(n_src, plan, field, blocks, weight):
-    probes = field.shape[1]
-    slots = blocks.shape[0]
-    planes = n_src // PLANE
-    rows = RB_LOC * probes // (PLANE * planes)
-    cut = rows * 3 // 4
-    dma = pltpu.SemaphoreType.DMA
-    per_spot, per_plane, parts = (PLANE - 1,), (planes - 1,), (PLANE - 1, 2)
-    counts = (parts, per_plane, per_plane, per_spot, per_plane, parts, per_spot, per_plane)
-    return pl.pallas_call(
-        functools.partial(reduce_kernel, planes),
-        out_shape=jax.ShapeDtypeStruct((PLANE, planes, rows, BLK), BF16),
-        in_specs=[pl.BlockSpec(memory_space=pltpu.SMEM)] + [pl.BlockSpec(memory_space=VMEM)] * 3,
-        out_specs=pl.BlockSpec(memory_space=VMEM),
-        scratch_shapes=[
-            VMEM((min(TOGETHER, slots), probes, BLK), F32),
-            VMEM((slots, probes, BLK), BF16),
-            VMEM((PLANE, planes, rows, BLK), BF16),
-            VMEM((PLANE - 1, planes, cut, BLK), BF16),
-            VMEM((planes, cut, BLK), BF16),
-            VMEM((planes - 1, cut, BLK), BF16),
-            VMEM((planes - 1, PLANE, rows - cut, BLK), BF16),
-            VMEM((PLANE, rows - cut, BLK), BF16),
-            VMEM((PLANE - 1, rows - cut, BLK), BF16),
-        ]
-        + [dma(count) for count in counts for _ in range(2)],
-        compiler_params=pltpu.CompilerParams(
-            collective_id=1, has_side_effects=True, vmem_limit_bytes=VMEM_LIMIT
-        ),
-        name="reduce_and_weigh",
-    )(plan, field, blocks, weight)
-
-
-def back_kernel(
-    n_src, plan_ref, weighted_ref, blocks_ref, probes_ref, kext_ref, out_ref, products, sums, terms_far, terms_near, pair, relayed, joined, far, edge, halo, wide, kwide, keep, flat,
-    edge_send, edge_recv, send, recv,
-):
+    return partners, forward, run, ready, finish
+
+
+def hessian_kernel(n_src, plan_ref, field_ref, blocks_ref, weight_ref, probes_ref, kext_ref, out_ref, *scratch):
+    (
+        products, sums, back_products, back_sums, mine, first, part, second, line, mixed, last,
+        upper_far, upper_near, lower_far, lower_near, terms_far, terms_near, pair, relayed, joined, far,
+        edge, halo, wide, kwide, keep, flat, edge_send, edge_recv, send, recv, *sems,
+    ) = scratch
+    upper, lower = (upper_far, upper_near), (lower_far, lower_near)
+    reduce_partners, forward, run, ready, finish_reduction = reduction(
+        n_src // PLANE, plan_ref, field_ref, blocks_ref, weight_ref, products, sums, mine, first, part, second, line, mixed,
+        last, upper, lower, *sems,
+    )
     me, group, before, after, twin, opposite = neighbours(n_src)
     lat = kext_ref.shape[0] - 16
     loc, lon = probes_ref.shape[0] // lat, probes_ref.shape[1]
     slabs = loc // SLAB
-    high, core = group // 2, group % 2
-    partners = [before, after, (me, twin), (me, opposite)]
+    core = group % 2
+    partners = [before, after, (me, twin), (me, opposite), *reduce_partners]
     announce(partners)
+    forward()
+    await_all(partners)
+    run()
 
     def view(ref, k, offset=0):
         if isinstance(k, int) and k < 2:
@@ -554,14 +538,19 @@
         return view(terms, k, core_of * loc)
 
     def adjoint(half, terms):
-        def product(slot, place):
-            block = weighted_ref[place + half * 2]
-            return jnp.dot(block, blocks_ref[slot], preferred_element_type=F32)
-
-        running_sums(plan_ref, 8, blocks_ref.shape[0], product, products, sums)
+        pieces = upper_far.shape[0] // RB_LOC
+
+        def product(k):
+            receptor, low = plan_ref[9, k], plan_ref[13, k]
+            rows = []
+            for piece in range(pieces):
+                rows += [upper[half][receptor * pieces + piece], lower[half][low + piece * PLANE]]
+            return jnp.dot(jnp.concatenate(rows, axis=0), blocks_ref[plan_ref[8, k]], preferred_element_type=F32)
+
+        running_sums(plan_ref, 8, blocks_ref.shape[0], product, back_products, back_sums)
         for row in range(lat):
             for side in range(2):
-                terms[row, :, side * BLK : (side + 1) * BLK] = block_sum(plan_ref, 8, 2 * row + side, sums)
+                terms[row, :, side * BLK : (side + 1) * BLK] = block_sum(plan_ref, 8, 2 * row + side, back_sums)
 
     def for_relay(k):
         return remote(term(terms_far, 1 - core, k), view(relayed, k), send.at[0, k], recv.at[0, k], (me, twin))
@@ -593,12 +582,13 @@
         remote(edge.at[0], halo.at[1], edge_send.at[0], edge_recv.at[0], before),
         remote(edge.at[1], halo.at[0], edge_send.at[1], edge_recv.at[1], after),
     ]
-    adjoint(1 - high, terms_far)
-    await_all(partners)
+    ready(0)
+    adjoint(0, terms_far)
     each(lambda k: for_relay(k).start())
     spread_kappa(n_src, me, kext_ref, kwide, keep, range(lat + 2 * SMOOTH))
     each(join)
-    adjoint(high, terms_near)
+    ready(1)
+    adjoint(1, terms_near)
     each(lambda k: for_twin(k).start())
     for k, row in ((0, SMOOTH), (1, lat)):
         rows = total(k)
@@ -646,30 +636,49 @@
         across(k).wait_send()
 
     each(finish)
-
-
-def scatter_and_smooth(n_src, plan, weighted, blocks, probes, kext):
+    finish_reduction()
+
+
+def hessian_part(n_src, plan, field, blocks, weight, probes, kext):
     lat = kext.shape[0] - 16
     loc, lon = probes.shape[0] // lat, probes.shape[1]
+    total, slots = field.shape[1], blocks.shape[0]
+    half = total // 2
+    planes = n_src // PLANE
+    rows = RB_LOC * total // (PLANE * planes)
+    cut = rows * 3 // 4
+    rest = rows - cut
     pieces = loc // SLAB + 2
-    landing = VMEM((lat, loc, lon), BF16)
+    together = min(TOGETHER, slots)
     dma = pltpu.SemaphoreType.DMA
+    per_spot, per_plane, parts = (PLANE - 1,), (planes - 1,), (PLANE - 1, 2)
+    counts = (parts, per_plane, per_plane, per_spot, per_plane, parts, per_spot, per_plane)
+    held = [
+        (slots, total, BLK),
+        (PLANE, planes, rows, BLK),
+        (PLANE - 1, planes, cut, BLK),
+        (planes, cut, BLK),
+        (planes - 1, cut, BLK),
+        (planes - 1, PLANE, rest, BLK),
+        (PLANE, rest, BLK),
+        (PLANE - 1, rest, BLK),
+        *[(PLANE * planes // 2, cut, BLK)] * 2,
+        *[(PLANE * planes // 2, rest, BLK)] * 2,
+        *[(lat, half, lon)] * 2,
+        *[(lat, loc, lon)] * 4,
+        *[(2, SMOOTH, loc, lon)] * 2,
+    ]
     return pl.pallas_call(
-        functools.partial(back_kernel, n_src),
+        functools.partial(hessian_kernel, n_src),
         out_shape=jax.ShapeDtypeStruct(probes.shape, F32),
-        in_specs=[pl.BlockSpec(memory_space=pltpu.SMEM)] + [pl.BlockSpec(memory_space=VMEM)] * 4,
+        in_specs=[pl.BlockSpec(memory_space=pltpu.SMEM)] + [pl.BlockSpec(memory_space=VMEM)] * 5,
         out_specs=pl.BlockSpec(memory_space=VMEM),
         scratch_shapes=[
-            VMEM((min(TOGETHER, blocks.shape[0]), 2 * loc, BLK), F32),
-            VMEM((blocks.shape[0], 2 * loc, BLK), BF16),
-            VMEM((lat, 2 * loc, lon), BF16),
-            VMEM((lat, 2 * loc, lon), BF16),
-            landing,
-            landing,
-            landing,
-            landing,
-            VMEM((2, SMOOTH, loc, lon), BF16),
-            VMEM((2, SMOOTH, loc, lon), BF16),
+            VMEM((together, total, BLK), F32),
+            VMEM(held[0], BF16),
+            VMEM((together, half, BLK), F32),
+            VMEM((slots, half, BLK), BF16),
+            *[VMEM(shape, BF16) for shape in held[1:]],
             VMEM((lat + 2 * SMOOTH, loc, lon), F32),
             VMEM((lat + 2 * SMOOTH, 8, lon), F32),
             VMEM((lat + 2 * SMOOTH, 8, lon), F32),
@@ -678,12 +687,13 @@
             dma((2,)),
             dma((3, pieces)),
             dma((3, pieces)),
-        ],
+        ]
+        + [dma(count) for count in counts for _ in range(2)],
         compiler_params=pltpu.CompilerParams(
-            collective_id=2, has_side_effects=True, vmem_limit_bytes=VMEM_LIMIT
+            collective_id=1, has_side_effects=True, vmem_limit_bytes=VMEM_LIMIT
         ),
-        name="scatter_and_smooth",
-    )(plan, weighted, blocks, probes, kext)
+        name="hessian_part",
+    )(plan, field, blocks, weight, probes, kext)
 
 
 def per_device(probes, kappa, footprint, block_source, block_receptor, block_count, obs_weight):
@@ -696,9 +706,7 @@
     unused = lax.broadcasted_iota(jnp.int32, (1, slots), 1) >= block_count.reshape(1, 1)
     packed = sources + SLOT_BASE * (receptors + SLOT_BASE * unused.astype(jnp.int32))
     field, kext, plan = smooth_and_gather(n_src, n_rcv, flat, kappa, packed)
-    weighted = reduce_and_weigh(n_src, plan, field, blocks, obs_weight.reshape(RB_LOC, BLK))
-    weighted = weighted.reshape(2 * RB_LOC, loc * n_rcv // 2, BLK)
-    out = scatter_and_smooth(n_src, plan, weighted, blocks, flat, kext)
+    out = hessian_part(n_src, plan, field, blocks, obs_weight.reshape(RB_LOC, BLK), flat, kext)
     return out.reshape(loc, lat, lon)
 
 

time: 90.5 us -> 87.5 us (0.967)
  Pallas kernels: 86.1 us -> 83.2 us
    pallas_call x2 -> x1, Pallas kernels: 59.5 us -> 56.6 us  [hessian_part(): pl.pallas_call(functools.partial(hessian_kernel, n_src), out_shape=jax.Sh...]
where the time goes in v6:
time: 87.5 us; the launch traced here: 87.3 us
  Pallas kernels  83.2 us (95%)
  local copies, waits for them, and re-layouts  2.74 us (3%)
    pallas_call x1, Pallas kernels, hessian_part(): pl.pallas_call(functools.partial(hessian_kernel, n_src), out_shape=jax.Sh...  56.6 us
    pallas_call x1, Pallas kernels, smooth_and_gather(): pl.pallas_call(functools.partial(smooth_kernel, n_src), out_shape=(jax.Sh...  26.6 us
    unnamed x9, local copies, waits for them, and re-layouts  2.74 us

profile of v6, /device:TPU:1, one launch (start us, length us, event | category | flops | bytes accessed | tf_op | source)
XLA Modules:
  0.0 87.3 jit_solution(10452612955924763255)
XLA Ops:
  0.7 0.7 bitcast_add_fusion.slots_ref
  1.4 0.0 copy-start.1
  1.4 1.0 %copy-done.1 = bf16[64,16,256]{2,1,0:T(8,128)(2,1)S(1)} copy-done((bf16[64,16,256]{2,1,0:T(8,128)(2,1)S(1)}, bf16[64,16,256]{2,1,0:T(8,128)(2,1)}, u32[]{:S(2)}) %copy-start.1) | copy-done | bytes 524312
  2.4 0.0 copy-start.3
  2.4 0.7 copy-done.3
  3.1 0.0 copy-start
  3.1 0.0 copy-start.2
  3.1 26.6 %smooth_and_gather.1 = (bf16[32,256,128]{2,1,0:T(8,128)(2,1)S(1)}, f32[32,256]{1,0:T(8,128)S(1)}, s32[16,256]{1,0:T(8,128)S(1)}) custom-call(bf16[1024,256]{1,0:T(8,128)(2,1)S(1)} %bitcast.14, f32[16,256]{1,0:T(8,128)S(1)} %copy-done.3, s32[1,192]{1,0:T(1,128)S(1)} %bitcast_add_fusion.slots_ref), custom_call_target="tpu_custom_call" | custom-call | flops 20000000000 | bytes 64000000 | tf_op jit(solution)/shard_map/smooth_and_gather/pallas_call | solution.py:259
  29.7 0.0 copy-done
  29.7 0.0 copy-done.2
  29.7 56.6 %hessian_part.1 = f32[1024,256]{1,0:T(8,128)S(1)} custom-call(s32[16,256]{1,0:T(8,128)S(1)} %get-tuple-element.8.plan_ref, bf16[32,256,128]{2,1,0:T(8,128)(2,1)S(1)} %get-tuple-element.9.field_ref, bf16[192,128,128]{2,1,0:T(8,128)(2,1)S(1)} %bitcast.12, f32[16,128]{1,0:T(8,128)S(1)} %bitcast.16, bf16[1024,256]{1,0:T(8,128)(2,1)S(1)} %bitcast.15, ...), custom_call_target="tpu_custom_call" | custom-call | tf_op jit(solution)/shard_map/hessian_part/pallas_call | solution.py:671
  86.4 1.0 %copy.10 = f32[64,16,256]{2,1,0:T(8,128)} copy(f32[64,16,256]{2,1,0:T(8,128)S(1)} %bitcast.13) | data formatting | bytes 2097152
Async XLA Ops:
  1.4 1.0 %copy-start.1 = (bf16[64,16,256]{2,1,0:T(8,128)(2,1)S(1)}, bf16[64,16,256]{2,1,0:T(8,128)(2,1)}, u32[]{:S(2)}) copy-start(bf16[64,16,256]{2,1,0:T(8,128)(2,1)} %param.7) | copy-start | bytes 1572868
  2.4 0.7 copy-start.3
  3.1 26.6 %copy-start = (bf16[1,1,192,128,128]{4,3,2,1,0:T(8,128)(2,1)S(1)}, bf16[1,1,192,128,128]{4,3,2,1,0:T(8,128)(2,1)}, u32[]{:S(2)}) copy-start(bf16[1,1,192,128,128]{4,3,2,1,0:T(8,128)(2,1)} %param.9) | copy-start | bytes 18874372
  3.1 26.6 %copy-start.2 = (f32[2048]{0:T(1024)S(1)}, f32[2048]{0:T(1024)}, u32[]{:S(2)}) copy-start(f32[2048]{0:T(1024)} %param.13) | copy-start | bytes 24580

commit v7 on v6

--- a/solution.py
+++ b/solution.py
@@ -13,12 +13,12 @@
 PLANE = 8
 SLAB = 16
 SLOT_BASE = 64
-TOGETHER = 32
+TOGETHER = 64
 MESH = pl.DeviceIdType.MESH
 VMEM = pltpu.VMEM
 F32 = jnp.float32
 BF16 = jnp.bfloat16
-VMEM_LIMIT = 44 * 1024 * 1024
+VMEM_LIMIT = 40 * 1024 * 1024
 
 
 def announce(devices):
@@ -131,20 +131,19 @@
     partners = [before, after, (me, twin), (me, opposite)]
     announce(partners)
 
-    top, bottom = range(SMOOTH), range(lat - SMOOTH, lat)
-    for side in range(lon // BLK):
-        flat[side] = probes_ref[:, side * BLK : (side + 1) * BLK].astype(F32)
-
-    def of_row(row):
-        return jnp.concatenate([flat[side, pl.ds(row, loc, stride=lat), :] for side in range(lon // BLK)], axis=1)
-
-    for side, rows in enumerate((top, bottom)):
-        for place, row in enumerate(rows):
-            value = of_row(row)
-            wide[SMOOTH + row] = value
-            edge[side, place] = value.astype(BF16)
-    for row in range(SMOOTH, lat - SMOOTH):
-        wide[SMOOTH + row] = of_row(row)
+    def prepare(slab):
+        here = pl.ds(pl.multiple_of(slab * SLAB * lat, SLAB * lat), SLAB * lat)
+        some = pl.ds(pl.multiple_of(slab * SLAB, SLAB), SLAB)
+        for side in range(2):
+            flat[side] = probes_ref[here, side * BLK : (side + 1) * BLK].astype(F32)
+        for row in range(lat):
+            value = jnp.concatenate([flat[side, pl.ds(row, SLAB, stride=lat), :] for side in range(2)], axis=1)
+            wide[SMOOTH + row, some, :] = value
+            if row < SMOOTH:
+                edge[0, row, some, :] = value.astype(BF16)
+            if row >= lat - SMOOTH:
+                edge[1, row - lat + SMOOTH, some, :] = value.astype(BF16)
+
     kext_ref[8 : lat + 8, :] = kappa_ref[...]
     spread_kappa(n_src, me, kext_ref, kwide, keep, range(SMOOTH, lat + SMOOTH))
     edges = [
@@ -215,9 +214,11 @@
             post(part, slab)
         return carry
 
+    prepare(0)
     smooth_part(0, 0)
     await_all(partners)
     post(0, 0)
+    lax.fori_loop(1, slabs, lambda slab, carry: (prepare(slab), carry)[1], 0)
     for copy in edges:
         copy.start()
     lax.fori_loop(1, slabs, inner, 0)
@@ -266,7 +267,7 @@
         in_specs=[pl.BlockSpec(memory_space=VMEM)] * 3,
         out_specs=(pl.BlockSpec(memory_space=VMEM),) * 3,
         scratch_shapes=[
-            VMEM((lon // BLK, loc * lat, BLK), F32),
+            VMEM((lon // BLK, SLAB * lat, BLK), F32),
             VMEM((2, SMOOTH, loc, lon), BF16),
             VMEM((2, SMOOTH, loc, lon), BF16),
             VMEM((lat + 2 * SMOOTH, loc, lon), F32),
@@ -508,11 +509,13 @@
 
 def hessian_kernel(n_src, plan_ref, field_ref, blocks_ref, weight_ref, probes_ref, kext_ref, out_ref, *scratch):
     (
-        products, sums, back_products, back_sums, mine, first, part, second, line, mixed, last,
+        products, sums, mine, first, part, second, line, mixed, last,
         upper_far, upper_near, lower_far, lower_near, terms_far, terms_near, pair, relayed, joined, far,
         edge, halo, wide, kwide, keep, flat, edge_send, edge_recv, send, recv, *sems,
     ) = scratch
     upper, lower = (upper_far, upper_near), (lower_far, lower_near)
+    half_probes = pl.ds(0, field_ref.shape[1] // 2)
+    back_products, back_sums = products.at[:, half_probes], sums.at[:, half_probes]
     reduce_partners, forward, run, ready, finish_reduction = reduction(
         n_src // PLANE, plan_ref, field_ref, blocks_ref, weight_ref, products, sums, mine, first, part, second, line, mixed,
         last, upper, lower, *sems,
@@ -676,8 +679,6 @@
         scratch_shapes=[
             VMEM((together, total, BLK), F32),
             VMEM(held[0], BF16),
-            VMEM((together, half, BLK), F32),
-            VMEM((slots, half, BLK), BF16),
             *[VMEM(shape, BF16) for shape in held[1:]],
             VMEM((lat + 2 * SMOOTH, loc, lon), F32),
             VMEM((lat + 2 * SMOOTH, 8, lon), F32),

time: 87.5 us -> 86.8 us (level)
    pallas_call x1, Pallas kernels: 56.6 us -> 55.5 us  [hessian_part(): pl.pallas_call(functools.partial(hessian_kernel, n_src), out_shape=jax.Sh...]
where the time goes in v7:
time: 86.8 us; the launch traced here: 86.6 us
  Pallas kernels  82.4 us (95%)
  local copies, waits for them, and re-layouts  2.74 us (3%)
    pallas_call x1, Pallas kernels, hessian_part(): pl.pallas_call(functools.partial(hessian_kernel, n_src), out_shape=jax.Sh...  55.5 us
    pallas_call x1, Pallas kernels, smooth_and_gather(): pl.pallas_call(functools.partial(smooth_kernel, n_src), out_shape=(jax.Sh...  26.9 us
    unnamed x9, local copies, waits for them, and re-layouts  2.74 us

profile of v7, /device:TPU:1, one launch (start us, length us, event | category | flops | bytes accessed | tf_op | source)
XLA Modules:
  0.0 86.6 jit_solution(12162601917893412167)
XLA Ops:
  0.7 0.7 bitcast_add_fusion.slots_ref
  1.4 0.0 copy-start.1
  1.4 1.0 %copy-done.1 = bf16[64,16,256]{2,1,0:T(8,128)(2,1)S(1)} copy-done((bf16[64,16,256]{2,1,0:T(8,128)(2,1)S(1)}, bf16[64,16,256]{2,1,0:T(8,128)(2,1)}, u32[]{:S(2)}) %copy-start.1) | copy-done | bytes 524312
  2.4 0.0 copy-start.3
  2.4 0.7 copy-done.3
  3.1 0.0 copy-start
  3.1 0.0 copy-start.2
  3.1 26.9 %smooth_and_gather.1 = (bf16[32,256,128]{2,1,0:T(8,128)(2,1)S(1)}, f32[32,256]{1,0:T(8,128)S(1)}, s32[16,256]{1,0:T(8,128)S(1)}) custom-call(bf16[1024,256]{1,0:T(8,128)(2,1)S(1)} %bitcast.14, f32[16,256]{1,0:T(8,128)S(1)} %copy-done.3, s32[1,192]{1,0:T(1,128)S(1)} %bitcast_add_fusion.slots_ref), custom_call_target="tpu_custom_call" | custom-call | flops 20000000000 | bytes 64000000 | tf_op jit(solution)/shard_map/smooth_and_gather/pallas_call | solution.py:260
  30.1 0.0 copy-done
  30.1 0.0 copy-done.2
  30.1 55.5 %hessian_part.1 = f32[1024,256]{1,0:T(8,128)S(1)} custom-call(s32[16,256]{1,0:T(8,128)S(1)} %get-tuple-element.8.plan_ref, bf16[32,256,128]{2,1,0:T(8,128)(2,1)S(1)} %get-tuple-element.9.field_ref, bf16[192,128,128]{2,1,0:T(8,128)(2,1)S(1)} %bitcast.12, f32[16,128]{1,0:T(8,128)S(1)} %bitcast.16, bf16[1024,256]{1,0:T(8,128)(2,1)S(1)} %bitcast.15, ...), custom_call_target="tpu_custom_call" | custom-call | tf_op jit(solution)/shard_map/hessian_part/pallas_call | solution.py:674
  85.6 1.0 %copy.10 = f32[64,16,256]{2,1,0:T(8,128)} copy(f32[64,16,256]{2,1,0:T(8,128)S(1)} %bitcast.13) | data formatting | bytes 2097152
Async XLA Ops:
  1.4 1.0 %copy-start.1 = (bf16[64,16,256]{2,1,0:T(8,128)(2,1)S(1)}, bf16[64,16,256]{2,1,0:T(8,128)(2,1)}, u32[]{:S(2)}) copy-start(bf16[64,16,256]{2,1,0:T(8,128)(2,1)} %param.7) | copy-start | bytes 1572868
  2.4 0.7 copy-start.3
  3.1 26.9 %copy-start = (bf16[1,1,192,128,128]{4,3,2,1,0:T(8,128)(2,1)S(1)}, bf16[1,1,192,128,128]{4,3,2,1,0:T(8,128)(2,1)}, u32[]{:S(2)}) copy-start(bf16[1,1,192,128,128]{4,3,2,1,0:T(8,128)(2,1)} %param.9) | copy-start | bytes 18874372
  3.1 27.0 %copy-start.2 = (f32[2048]{0:T(1024)S(1)}, f32[2048]{0:T(1024)}, u32[]{:S(2)}) copy-start(f32[2048]{0:T(1024)} %param.13) | copy-start | bytes 24580

commit v8 on v6

--- a/solution.py
+++ b/solution.py
@@ -13,12 +13,12 @@
 PLANE = 8
 SLAB = 16
 SLOT_BASE = 64
-TOGETHER = 32
+TOGETHER = 64
 MESH = pl.DeviceIdType.MESH
 VMEM = pltpu.VMEM
 F32 = jnp.float32
 BF16 = jnp.bfloat16
-VMEM_LIMIT = 44 * 1024 * 1024
+VMEM_LIMIT = 40 * 1024 * 1024
 
 
 def announce(devices):
@@ -375,8 +375,8 @@
     def sender(piece):
         return lax.rem(plane + planes - piece, planes)
 
-    def on_own_group(work):
-        for g in range(groups):
+    def on_own_group(work, which=(0, 1)):
+        for g in which:
             pl.when(plane // size == g)(functools.partial(work, g))
 
     def others_of(g, work):
@@ -473,11 +473,13 @@
         plane_sums(0)
         line_sums()
         plane_sums(1)
+        on_own_group(own_rows, (0,))
         on_own_group(own_lower_rows)
-        on_own_group(own_rows)
+        on_own_group(own_rows, (1,))
         spread_group(0)
-        on_own_group(spread_lower_rows)
+        on_own_group(spread_lower_rows, (0,))
         spread_group(1)
+        on_own_group(spread_lower_rows, (1,))
 
     def ready(g):
         for d in in_planes:
@@ -508,11 +510,13 @@
 
 def hessian_kernel(n_src, plan_ref, field_ref, blocks_ref, weight_ref, probes_ref, kext_ref, out_ref, *scratch):
     (
-        products, sums, back_products, back_sums, mine, first, part, second, line, mixed, last,
+        products, sums, mine, first, part, second, line, mixed, last,
         upper_far, upper_near, lower_far, lower_near, terms_far, terms_near, pair, relayed, joined, far,
         edge, halo, wide, kwide, keep, flat, edge_send, edge_recv, send, recv, *sems,
     ) = scratch
     upper, lower = (upper_far, upper_near), (lower_far, lower_near)
+    half_probes = pl.ds(0, field_ref.shape[1] // 2)
+    back_products, back_sums = products.at[:, half_probes], sums.at[:, half_probes]
     reduce_partners, forward, run, ready, finish_reduction = reduction(
         n_src // PLANE, plan_ref, field_ref, blocks_ref, weight_ref, products, sums, mine, first, part, second, line, mixed,
         last, upper, lower, *sems,
@@ -676,8 +680,6 @@
         scratch_shapes=[
             VMEM((together, total, BLK), F32),
             VMEM(held[0], BF16),
-            VMEM((together, half, BLK), F32),
-            VMEM((slots, half, BLK), BF16),
             *[VMEM(shape, BF16) for shape in held[1:]],
             VMEM((lat + 2 * SMOOTH, loc, lon), F32),
             VMEM((lat + 2 * SMOOTH, 8, lon), F32),

time: 87.5 us -> 86.3 us (0.986)
  Pallas kernels: 83.2 us -> 82 us
    pallas_call x1, Pallas kernels: 56.6 us -> 55.4 us  [hessian_part(): pl.pallas_call(functools.partial(hessian_kernel, n_src), out_shape=jax.Sh...]
where the time goes in v8:
time: 86.3 us; the launch traced here: 86.1 us
  Pallas kernels  82 us (95%)
  local copies, waits for them, and re-layouts  2.74 us (3%)
    pallas_call x1, Pallas kernels, hessian_part(): pl.pallas_call(functools.partial(hessian_kernel, n_src), out_shape=jax.Sh...  55.4 us
    pallas_call x1, Pallas kernels, smooth_and_gather(): pl.pallas_call(functools.partial(smooth_kernel, n_src), out_shape=(jax.Sh...  26.6 us
    unnamed x9, local copies, waits for them, and re-layouts  2.74 us

profile of v8, /device:TPU:1, one launch (start us, length us, event | category | flops | bytes accessed | tf_op | source)
XLA Modules:
  0.0 86.1 jit_solution(5572155250984333099)
XLA Ops:
  0.7 0.7 bitcast_add_fusion.slots_ref
  1.4 0.0 copy-start.1
  1.4 1.0 %copy-done.1 = bf16[64,16,256]{2,1,0:T(8,128)(2,1)S(1)} copy-done((bf16[64,16,256]{2,1,0:T(8,128)(2,1)S(1)}, bf16[64,16,256]{2,1,0:T(8,128)(2,1)}, u32[]{:S(2)}) %copy-start.1) | copy-done | bytes 524312
  2.4 0.0 copy-start.3
  2.4 0.7 copy-done.3
  3.1 0.0 copy-start
  3.1 0.0 copy-start.2
  3.1 26.6 %smooth_and_gather.1 = (bf16[32,256,128]{2,1,0:T(8,128)(2,1)S(1)}, f32[32,256]{1,0:T(8,128)S(1)}, s32[16,256]{1,0:T(8,128)S(1)}) custom-call(bf16[1024,256]{1,0:T(8,128)(2,1)S(1)} %bitcast.14, f32[16,256]{1,0:T(8,128)S(1)} %copy-done.3, s32[1,192]{1,0:T(1,128)S(1)} %bitcast_add_fusion.slots_ref), custom_call_target="tpu_custom_call" | custom-call | flops 20000000000 | bytes 64000000 | tf_op jit(solution)/shard_map/smooth_and_gather/pallas_call | solution.py:259
  29.7 0.0 copy-done
  29.7 0.0 copy-done.2
  29.7 55.4 %hessian_part.1 = f32[1024,256]{1,0:T(8,128)S(1)} custom-call(s32[16,256]{1,0:T(8,128)S(1)} %get-tuple-element.8.plan_ref, bf16[32,256,128]{2,1,0:T(8,128)(2,1)S(1)} %get-tuple-element.9.field_ref, bf16[192,128,128]{2,1,0:T(8,128)(2,1)S(1)} %bitcast.12, f32[16,128]{1,0:T(8,128)S(1)} %bitcast.16, bf16[1024,256]{1,0:T(8,128)(2,1)S(1)} %bitcast.15, ...), custom_call_target="tpu_custom_call" | custom-call | tf_op jit(solution)/shard_map/hessian_part/pallas_call | solution.py:675
  85.1 1.0 %copy.10 = f32[64,16,256]{2,1,0:T(8,128)} copy(f32[64,16,256]{2,1,0:T(8,128)S(1)} %bitcast.13) | data formatting | bytes 2097152
Async XLA Ops:
  1.4 1.0 %copy-start.1 = (bf16[64,16,256]{2,1,0:T(8,128)(2,1)S(1)}, bf16[64,16,256]{2,1,0:T(8,128)(2,1)}, u32[]{:S(2)}) copy-start(bf16[64,16,256]{2,1,0:T(8,128)(2,1)} %param.7) | copy-start | bytes 1572868
  2.4 0.7 copy-start.3
  3.1 26.6 %copy-start = (bf16[1,1,192,128,128]{4,3,2,1,0:T(8,128)(2,1)S(1)}, bf16[1,1,192,128,128]{4,3,2,1,0:T(8,128)(2,1)}, u32[]{:S(2)}) copy-start(bf16[1,1,192,128,128]{4,3,2,1,0:T(8,128)(2,1)} %param.9) | copy-start | bytes 18874372
  3.1 26.6 %copy-start.2 = (f32[2048]{0:T(1024)S(1)}, f32[2048]{0:T(1024)}, u32[]{:S(2)}) copy-start(f32[2048]{0:T(1024)} %param.13) | copy-start | bytes 24580

commit v9 on v8

--- a/solution.py
+++ b/solution.py
@@ -360,9 +360,9 @@
         where = upper[g].at[spot * size + own_index]
         return copy(ga_line, (d - 1,), where, where, in_line(d))
 
-    def gather_a_plane(d, g):
-        where = upper[g].at[pl.ds(spot * size, size)]
-        return copy(ga_plane, (d - 1, g), where, where, in_plane(d))
+    def gather_a_plane(d, g, index):
+        where = upper[g].at[spot * size + index]
+        return copy(ga_plane, (d - 1, g * size + index), where, where, in_plane(d))
 
     def gather_c_plane(d, g):
         where = lower[g].at[own_index * PLANE + spot]
@@ -429,13 +429,17 @@
             gather_a_line(d, g).start()
 
     def spread_group(g):
-        def landed(piece):
-            where = upper[g].at[spot * size + piece % size]
-            copy(ga_line, (sender(piece) - 1,), where, where, in_line(1)).wait_recv()
-
-        others_of(g, landed)
-        for d in in_planes:
-            gather_a_plane(d, g).start()
+        for turn in range(size):
+            index = lax.rem(own_index + turn, size)
+            piece = g * size + index
+
+            @pl.when(piece != plane)
+            def _():
+                where = upper[g].at[spot * size + index]
+                copy(ga_line, (sender(piece) - 1,), where, where, in_line(1)).wait_recv()
+
+            for d in in_planes:
+                gather_a_plane(d, g, index).start()
 
     def line_sums():
         for d in in_lines:
@@ -483,7 +487,8 @@
 
     def ready(g):
         for d in in_planes:
-            gather_a_plane(d, g).wait_recv()
+            for index in range(size):
+                gather_a_plane(d, g, index).wait_recv()
 
         def landed(piece):
             where = lower[g].at[pl.ds(piece % size * PLANE, PLANE)]
@@ -494,8 +499,9 @@
     def finish():
         for d in in_planes:
             for g in range(groups):
-                gather_a_plane(d, g).wait_send()
                 scatter_a_plane(d, g).wait_send()
+                for index in range(size):
+                    gather_a_plane(d, g, index).wait_send()
             scatter_c_plane(d).wait_send()
             gather_c_plane(d, 0).wait_send()
         for d in in_lines:
@@ -656,7 +662,8 @@
     together = min(TOGETHER, slots)
     dma = pltpu.SemaphoreType.DMA
     per_spot, per_plane, parts = (PLANE - 1,), (planes - 1,), (PLANE - 1, 2)
-    counts = (parts, per_plane, per_plane, per_spot, per_plane, parts, per_spot, per_plane)
+    each = (PLANE - 1, planes)
+    counts = (parts, per_plane, per_plane, per_spot, per_plane, each, per_spot, per_plane)
     held = [
         (slots, total, BLK),
         (PLANE, planes, rows, BLK),

time: 86.3 us -> 86.2 us (level)
  no operation moved by 1% of the time
where the time goes in v9:
time: 86.2 us; the launch traced here: 86 us
  Pallas kernels  81.9 us (95%)
  local copies, waits for them, and re-layouts  2.74 us (3%)
    pallas_call x1, Pallas kernels, hessian_part(): pl.pallas_call(functools.partial(hessian_kernel, n_src), out_shape=jax.Sh...  55.3 us
    pallas_call x1, Pallas kernels, smooth_and_gather(): pl.pallas_call(functools.partial(smooth_kernel, n_src), out_shape=(jax.Sh...  26.6 us
    unnamed x9, local copies, waits for them, and re-layouts  2.74 us

profile of v9, /device:TPU:1, one launch (start us, length us, event | category | flops | bytes accessed | tf_op | source)
XLA Modules:
  0.0 86.0 jit_solution(7780656382778353286)
XLA Ops:
  0.7 0.7 bitcast_add_fusion.slots_ref
  1.4 0.0 copy-start.1
  1.4 1.0 %copy-done.1 = bf16[64,16,256]{2,1,0:T(8,128)(2,1)S(1)} copy-done((bf16[64,16,256]{2,1,0:T(8,128)(2,1)S(1)}, bf16[64,16,256]{2,1,0:T(8,128)(2,1)}, u32[]{:S(2)}) %copy-start.1) | copy-done | bytes 524312
  2.4 0.0 copy-start.3
  2.4 0.7 copy-done.3
  3.1 0.0 copy-start
  3.1 0.0 copy-start.2
  3.1 26.6 %smooth_and_gather.1 = (bf16[32,256,128]{2,1,0:T(8,128)(2,1)S(1)}, f32[32,256]{1,0:T(8,128)S(1)}, s32[16,256]{1,0:T(8,128)S(1)}) custom-call(bf16[1024,256]{1,0:T(8,128)(2,1)S(1)} %bitcast.14, f32[16,256]{1,0:T(8,128)S(1)} %copy-done.3, s32[1,192]{1,0:T(1,128)S(1)} %bitcast_add_fusion.slots_ref), custom_call_target="tpu_custom_call" | custom-call | flops 20000000000 | bytes 64000000 | tf_op jit(solution)/shard_map/smooth_and_gather/pallas_call | solution.py:259
  29.7 0.0 copy-done
  29.7 0.0 copy-done.2
  29.7 55.3 %hessian_part.1 = f32[1024,256]{1,0:T(8,128)S(1)} custom-call(s32[16,256]{1,0:T(8,128)S(1)} %get-tuple-element.8.plan_ref, bf16[32,256,128]{2,1,0:T(8,128)(2,1)S(1)} %get-tuple-element.9.field_ref, bf16[192,128,128]{2,1,0:T(8,128)(2,1)S(1)} %bitcast.12, f32[16,128]{1,0:T(8,128)S(1)} %bitcast.16, bf16[1024,256]{1,0:T(8,128)(2,1)S(1)} %bitcast.15, ...), custom_call_target="tpu_custom_call" | custom-call | tf_op jit(solution)/shard_map/hessian_part/pallas_call | solution.py:682
  85.0 1.0 %copy.10 = f32[64,16,256]{2,1,0:T(8,128)} copy(f32[64,16,256]{2,1,0:T(8,128)S(1)} %bitcast.13) | data formatting | bytes 2097152
Async XLA Ops:
  1.4 1.0 %copy-start.1 = (bf16[64,16,256]{2,1,0:T(8,128)(2,1)S(1)}, bf16[64,16,256]{2,1,0:T(8,128)(2,1)}, u32[]{:S(2)}) copy-start(bf16[64,16,256]{2,1,0:T(8,128)(2,1)} %param.7) | copy-start | bytes 1572868
  2.4 0.7 copy-start.3
  3.1 26.6 %copy-start = (bf16[1,1,192,128,128]{4,3,2,1,0:T(8,128)(2,1)S(1)}, bf16[1,1,192,128,128]{4,3,2,1,0:T(8,128)(2,1)}, u32[]{:S(2)}) copy-start(bf16[1,1,192,128,128]{4,3,2,1,0:T(8,128)(2,1)} %param.9) | copy-start | bytes 18874372
  3.1 26.6 %copy-start.2 = (f32[2048]{0:T(1024)S(1)}, f32[2048]{0:T(1024)}, u32[]{:S(2)}) copy-start(f32[2048]{0:T(1024)} %param.13) | copy-start | bytes 24580

commit v10 on v8

--- a/solution.py
+++ b/solution.py
@@ -14,6 +14,7 @@
 SLAB = 16
 SLOT_BASE = 64
 TOGETHER = 64
+SHIFTS = ((0, 0), (1, 2), (1, 1), (1, 3), (0, 2), (1, 0), (0, 1), (0, 3))
 MESH = pl.DeviceIdType.MESH
 VMEM = pltpu.VMEM
 F32 = jnp.float32
@@ -322,7 +323,8 @@
     in_lines = range(1, planes)
 
     def spot_of(distance):
-        return lax.rem(spot + distance, PLANE)
+        across, along = SHIFTS[distance]
+        return lax.rem(spot // 4 + across, 2) * 4 + lax.rem(spot % 4 + along, 4)
 
     def plane_of(distance):
         return lax.rem(plane + distance, planes)

time: 86.3 us -> 85.2 us (0.987)
  Pallas kernels: 82 us -> 80.8 us
    pallas_call x1, Pallas kernels: 55.4 us -> 54.2 us  [hessian_part(): pl.pallas_call(functools.partial(hessian_kernel, n_src), out_shape=jax.Sh...]
where the time goes in v10:
time: 85.2 us; the launch traced here: 85 us
  Pallas kernels  80.8 us (95%)
  local copies, waits for them, and re-layouts  2.74 us (3%)
    pallas_call x1, Pallas kernels, hessian_part(): pl.pallas_call(functools.partial(hessian_kernel, n_src), out_shape=jax.Sh...  54.2 us
    pallas_call x1, Pallas kernels, smooth_and_gather(): pl.pallas_call(functools.partial(smooth_kernel, n_src), out_shape=(jax.Sh...  26.6 us
    unnamed x9, local copies, waits for them, and re-layouts  2.74 us

profile of v10, /device:TPU:1, one launch (start us, length us, event | category | flops | bytes accessed | tf_op | source)
XLA Modules:
  0.0 85.0 jit_solution(13708096015269841164)
XLA Ops:
  0.7 0.7 bitcast_add_fusion.slots_ref
  1.4 0.0 copy-start.1
  1.4 1.0 %copy-done.1 = bf16[64,16,256]{2,1,0:T(8,128)(2,1)S(1)} copy-done((bf16[64,16,256]{2,1,0:T(8,128)(2,1)S(1)}, bf16[64,16,256]{2,1,0:T(8,128)(2,1)}, u32[]{:S(2)}) %copy-start.1) | copy-done | bytes 524312
  2.4 0.0 copy-start.3
  2.4 0.7 copy-done.3
  3.1 0.0 copy-start
  3.1 0.0 copy-start.2
  3.1 26.6 %smooth_and_gather.1 = (bf16[32,256,128]{2,1,0:T(8,128)(2,1)S(1)}, f32[32,256]{1,0:T(8,128)S(1)}, s32[16,256]{1,0:T(8,128)S(1)}) custom-call(bf16[1024,256]{1,0:T(8,128)(2,1)S(1)} %bitcast.14, f32[16,256]{1,0:T(8,128)S(1)} %copy-done.3, s32[1,192]{1,0:T(1,128)S(1)} %bitcast_add_fusion.slots_ref), custom_call_target="tpu_custom_call" | custom-call | flops 20000000000 | bytes 64000000 | tf_op jit(solution)/shard_map/smooth_and_gather/pallas_call | solution.py:260
  29.7 0.0 copy-done
  29.7 0.0 copy-done.2
  29.7 54.2 %hessian_part.1 = f32[1024,256]{1,0:T(8,128)S(1)} custom-call(s32[16,256]{1,0:T(8,128)S(1)} %get-tuple-element.8.plan_ref, bf16[32,256,128]{2,1,0:T(8,128)(2,1)S(1)} %get-tuple-element.9.field_ref, bf16[192,128,128]{2,1,0:T(8,128)(2,1)S(1)} %bitcast.12, f32[16,128]{1,0:T(8,128)S(1)} %bitcast.16, bf16[1024,256]{1,0:T(8,128)(2,1)S(1)} %bitcast.15, ...), custom_call_target="tpu_custom_call" | custom-call | tf_op jit(solution)/shard_map/hessian_part/pallas_call | solution.py:677
  84.0 1.0 %copy.10 = f32[64,16,256]{2,1,0:T(8,128)} copy(f32[64,16,256]{2,1,0:T(8,128)S(1)} %bitcast.13) | data formatting | bytes 2097152
Async XLA Ops:
  1.4 1.0 %copy-start.1 = (bf16[64,16,256]{2,1,0:T(8,128)(2,1)S(1)}, bf16[64,16,256]{2,1,0:T(8,128)(2,1)}, u32[]{:S(2)}) copy-start(bf16[64,16,256]{2,1,0:T(8,128)(2,1)} %param.7) | copy-start | bytes 1572868
  2.4 0.7 copy-start.3
  3.1 26.6 %copy-start = (bf16[1,1,192,128,128]{4,3,2,1,0:T(8,128)(2,1)S(1)}, bf16[1,1,192,128,128]{4,3,2,1,0:T(8,128)(2,1)}, u32[]{:S(2)}) copy-start(bf16[1,1,192,128,128]{4,3,2,1,0:T(8,128)(2,1)} %param.9) | copy-start | bytes 18874372
  3.1 26.6 %copy-start.2 = (f32[2048]{0:T(1024)S(1)}, f32[2048]{0:T(1024)}, u32[]{:S(2)}) copy-start(f32[2048]{0:T(1024)} %param.13) | copy-start | bytes 24580
